TPU v7x, 32 devices: a whole 2x2x4 slice. The times are simulated.
32 devices in a mesh: lon: 16 (over z, x, core), lat: 2 (over y).
Axes of the slice: x: 2, y: 2, z: 4, core: 2. Of those that a mesh axis runs over, the one named last changes fastest.
Arguments:
- heat_anomaly: float32 [16, 64, 2048], P(None, 'lat', 'lon'), may hold values from -11 to 11
- saltiness_anomaly: float32 [16, 64, 2048], P(None, 'lat', 'lon'), may hold values from -3 to 3
- zonal_stability_ratio: float32 [16, 64, 2048], P(None, 'lat', 'lon'), may hold values from -0.4 to 0.4
- meridional_stability_ratio: float32 [16, 64, 2048], P(None, 'lat', 'lon'), may hold values from -0.4 to 0.4
- ocean_layer_count: int32 [64, 2048], P('lat', 'lon'), may hold values from 0 to 16
Outputs:
- temperature_next: float32 [16, 64, 2048], P(None, 'lat', 'lon')
- salinity_next: float32 [16, 64, 2048], P(None, 'lat', 'lon')
All inputs are finite; a program needn't handle non-finite values.
Results may differ from a plain program's by a relative error of at most 0.0003.
Values sent between devices are 32-bit elements; how exact they have to be, the bound alone decides.
No kernel may reach another device: no remote copies, remote signals or barrier semaphores. Data moves between devices by JAX's collectives and lax.ppermute only.
A program may use at most 64 MiB of HBM per device.

v0:
```python
import jax
import jax.numpy as jnp
from jax import lax
from jax.sharding import PartitionSpec as P

heat_swelling_alpha = 0.1655
coef_beta = 0.76554
cabbeling_parameter = 0.05952
lambda_salt = 0.00054914
thermobaric_parameter = 0.0001497
press_salt = 1.109e-05
cross_coupling_contribution = 0.0024341
total_depth = 5000.0
kappa_iso = 0.1
slope_max = 1.0
strat_min = 0.1


def extended(array, sides, width, wrap):
    for axis, dim in sides:
        devices, length = (lax.axis_size(axis), array.shape[dim])
        up = [(i, (i + 1) % devices) for i in range(devices if wrap else devices - 1)]
        down = [(j, i) for i, j in up]
        last = lax.slice_in_dim(array, length - width, length, axis=dim)
        first = lax.slice_in_dim(array, 0, width, axis=dim)
        before = lax.ppermute(last, axis, up)
        after = lax.ppermute(first, axis, down)
        array = jnp.concatenate([before, array, after], axis=dim)
    return array


def passed_along(array, axis, by):
    devices = lax.axis_size(axis)
    return lax.ppermute(array, axis, [(i, (i + by) % devices) for i in range(devices)])


def passed_along_2(array, axis, by):
    devices = lax.axis_size(axis)
    pairs = [(i, i + by) for i in range(devices) if 0 <= i + by < devices]
    return lax.ppermute(array, axis, pairs)


def minmod(former, second):
    return jnp.where(
        former * second > 0.0, jnp.sign(former) * jnp.minimum(jnp.abs(former), jnp.abs(second)), 0.0
    )


def seawater_heaviness(heat_anomaly, saltiness_anomaly, seafloor_distances):
    return (
        -heat_swelling_alpha
        * (
            1.0
            + 0.5 * cabbeling_parameter * heat_anomaly
            + thermobaric_parameter * seafloor_distances
        )
        * heat_anomaly
        + coef_beta
        * (1.0 - 0.5 * lambda_salt * saltiness_anomaly - press_salt * seafloor_distances)
        * saltiness_anomaly
        - cross_coupling_contribution * heat_anomaly * saltiness_anomaly
    )


def vertical_diff(field):
    along = field.ndim - 3
    layer_stack_sum = field.shape[along]
    top_part = lax.slice_in_dim(field, 1, 2, axis=along) - lax.slice_in_dim(field, 0, 1, axis=along)
    middle = 0.5 * (
        lax.slice_in_dim(field, 2, layer_stack_sum, axis=along)
        - lax.slice_in_dim(field, 0, layer_stack_sum - 2, axis=along)
    )
    bottom = lax.slice_in_dim(
        field, layer_stack_sum - 1, layer_stack_sum, axis=along
    ) - lax.slice_in_dim(field, layer_stack_sum - 2, layer_stack_sum - 1, axis=along)
    return jnp.concatenate([top_part, middle, bottom], axis=along)


def face_flux(tracers, tracer_vert, rho_field, rho_vert, ocean_presence_flags, face_speed, along):

    def window(array, lower, upper):
        axis_pos = array.ndim + along
        return lax.slice_in_dim(array, lower, array.shape[axis_pos] - upper, axis=axis_pos)

    wet_face = window(ocean_presence_flags, 0, 1) * window(ocean_presence_flags, 1, 0)
    masked_step = wet_face * (window(tracers, 1, 0) - window(tracers, 0, 1))
    step_back = window(masked_step, 0, 2)
    step_here = window(masked_step, 1, 1)
    step_ahead = window(masked_step, 2, 0)
    cell_left = window(tracers, 1, 2)
    cell_right = window(tracers, 2, 1)
    face_wet = window(wet_face, 1, 1)
    positive = jnp.maximum(face_speed, 0.0)
    negative = jnp.minimum(face_speed, 0.0)
    advective = face_wet * (
        positive * (cell_left + 0.5 * (1.0 - face_speed) * minmod(step_back, step_here))
        + negative * (cell_right - 0.5 * (1.0 + face_speed) * minmod(step_ahead, step_here))
    )
    rho_step = window(rho_field, 2, 1) - window(rho_field, 1, 2)
    strat_face = jnp.maximum(0.5 * (window(rho_vert, 1, 2) + window(rho_vert, 2, 1)), strat_min)
    slope_face = jnp.clip(-rho_step / strat_face, -slope_max, slope_max)
    vert_face = 0.5 * (window(tracer_vert, 1, 2) + window(tracer_vert, 2, 1))
    isoneutral = -kappa_iso * face_wet * (cell_right - cell_left + slope_face * vert_face)
    flux_total = advective + isoneutral
    return window(flux_total, 0, 1) - window(flux_total, 1, 0)


def stencil(padded, east_cols, north_rows):
    layer_stack_sum = padded.shape[1]
    depth_levels = (
        total_depth
        * (lax.broadcasted_iota(jnp.float32, (layer_stack_sum, 1, 1), 0) + 0.5)
        / layer_stack_sum
    )
    tracers = padded[:2]
    ocean_presence_flags = padded[2]
    rho_field = seawater_heaviness(padded[0], padded[1], depth_levels)
    rho_vert = vertical_diff(rho_field)
    tracer_vert = vertical_diff(tracers)
    along_x = face_flux(
        tracers[:, :, 2:-2, :],
        tracer_vert[:, :, 2:-2, :],
        rho_field[:, 2:-2, :],
        rho_vert[:, 2:-2, :],
        ocean_presence_flags[:, 2:-2, :],
        east_cols,
        -1,
    )
    along_y = face_flux(
        tracers[:, :, :, 2:-2],
        tracer_vert[:, :, :, 2:-2],
        rho_field[:, :, 2:-2],
        rho_vert[:, :, 2:-2],
        ocean_presence_flags[:, :, 2:-2],
        north_rows,
        -2,
    )
    interior = tracers[:, :, 2:-2, 2:-2]
    return ocean_presence_flags[:, 2:-2, 2:-2] * (interior + along_x + along_y)


def body(
    heat_anomaly,
    saltiness_anomaly,
    zonal_stability_ratio,
    meridional_stability_ratio,
    ocean_layer_count,
):
    layer_stack_sum, latitude_band_sum, profile_sum = heat_anomaly.shape
    ocean_presence_flags = (
        lax.broadcasted_iota(jnp.int32, (layer_stack_sum, 1, 1), 0) < ocean_layer_count[None]
    ).astype(jnp.float32)
    scalar_quantities = jnp.stack([heat_anomaly, saltiness_anomaly, ocean_presence_flags])
    lon_padded = extended(scalar_quantities, (("lon", 3),), 2, True)
    padded = extended(lon_padded, (("lat", 2),), 2, False)
    whole_rows = lax.all_gather(
        scalar_quantities[:3, :, latitude_band_sum - 3 :, :], "lon", axis=3, tiled=True
    )
    flipped = jnp.flip(whole_rows, -1)
    offset = lax.axis_index("lon") * profile_sum
    rolled = jnp.concatenate([flipped[..., -1:], flipped], axis=-1)
    next_rows = lax.dynamic_slice_in_dim(rolled, offset, profile_sum, 3)
    ghost_rows = jnp.flip(next_rows[:, :, 0:2, :], 2)
    top_device = lax.axis_index("lat") == lax.axis_size("lat") - 1
    current = padded[:3, :, latitude_band_sum + 2 :, 2 : profile_sum + 2]
    padded = padded.at[:3, :, latitude_band_sum + 2 :, 2 : profile_sum + 2].set(
        jnp.where(top_device, ghost_rows, current)
    )
    west_column = passed_along(zonal_stability_ratio[:, :, profile_sum - 1], "lon", 1)
    east_cols = jnp.concatenate([west_column[:, :, None], zonal_stability_ratio], axis=2)
    south_row = passed_along_2(meridional_stability_ratio[:, latitude_band_sum - 1, :], "lat", 1)
    north_rows = jnp.concatenate([south_row[:, None, :], meridional_stability_ratio], axis=1)
    result = stencil(padded, east_cols, north_rows)
    return (result[0], result[1])


def solution(mesh):
    in_specs = (
        P(None, "lat", "lon"),
        P(None, "lat", "lon"),
        P(None, "lat", "lon"),
        P(None, "lat", "lon"),
        P("lat", "lon"),
    )
    out_specs = (P(None, "lat", "lon"), P(None, "lat", "lon"))
    return jax.shard_map(body, mesh=mesh, in_specs=in_specs, out_specs=out_specs, check_vma=False)
```

profile of v0, /device:TPU:0, one launch (start us, length us, event | category | flops | bytes accessed | tf_op | source)
XLA Modules:
  0.0 80.7 jit_solution(2995535945233324460)
XLA Ops:
  7.2 0.7 fusion.27
  8.0 1.1 %pad_maximum_fusion.2 = f32[3,16,32,128]{3,2,1,0:T(8,128)S(1)} fusion(f32[1,16,32,128]{3,2,1,0:T(8,128)S(1)} %fusion.27, f32[1,16,32,128]{3,2,1,0:T(8,128)} %bitcast.21, f32[1,16,32,128]{3,2,1,0:T(8,128)} %bitcast.22), kind=kLoop, calls=%fused_computation.15 | loop fusion | flops 393216 | bytes 1572864 | tf_op jit(solution)/shard_map/stack | solution.py:153
  9.0 0.7 slice.340
  9.7 0.3 fusion.31
  10.1 0.3 copy.82
  10.4 5.5 %collective-permute-start.1 = (f32[3,16,32,2]{2,1,3,0:T(8,128)S(1)}, f32[3,16,32,2]{2,1,3,0:T(8,128)S(1)}, u32[]{:S(2)}, u32[]{:S(2)}) collective-permute-start(f32[3,16,32,2]{2,1,3,0:T(8,128)S(1)} %copy.82), channel_id=1, source_target_pairs={{2,0},{4,2},{6,4},{8,6},{10,8},{12,10},{14,12},{16,14},{18,16},{20... | collective-permute-start | bytes 36872 | tf_op jit(solution)/shard_map/ppermute | solution.py:27
  15.9 0.3 copy.81
  16.3 0.2 copy.77
  16.4 3.4 %collective-permute-start.5 = (f32[16,128]{1,0:T(8,128)S(1)}, f32[16,128]{1,0:T(8,128)S(1)}, u32[]{:S(2)}, u32[]{:S(2)}) collective-permute-start(f32[16,128]{1,0:T(8,128)S(1)} %slice_bitcast_fusion.5), channel_id=1, source_target_pairs={{0,1},{2,3},{4,5},{6,7},{8,9},{10,11},{12,13},{14,15},{16,17},{18,... | collective-permute-start | bytes 24584 | tf_op jit(solution)/shard_map/ppermute | solution.py:40
  20.0 0.2 copy.83
  20.2 0.5 copy.70
  20.7 0.2 copy.76
  20.9 5.1 %collective-permute-done.4 = f32[16,32]{1,0:T(8,128)S(1)} collective-permute-done((f32[16,32]{1,0:T(8,128)S(1)}, f32[16,32]{1,0:T(8,128)S(1)}, u32[]{:S(2)}, u32[]{:S(2)}) %collective-permute-start.4) | collective-permute-done | bytes 2080 | tf_op jit(solution)/shard_map/ppermute | solution.py:34
  26.0 0.2 copy.75
  26.2 1.7 %broadcast_maximum_fusion = (f32[16,32,129]{2,0,1:T(8,128)}, f32[16,32,129]{2,0,1:T(8,128)}, f32[16,32,129]{2,0,1:T(8,128)}, f32[16,32,129]{2,0,1:T(8,128)}) fusion(f32[16,32,128]{2,0,1:T(8,128)S(1)} %copy.76, f32[16,32,1]{2,0,1:T(8,128)S(1)} %copy.75), kind=kLoop, calls=%fused_computation.65 | loop fusion | flops 462336 | bytes 1320960 | tf_op jit(solution)/shard_map/max | solution.py:93
  27.9 0.4 copy.71
  28.3 0.4 copy.69
  28.9 1.3 %collective-permute-start.3 = (f32[3,16,2,132]{3,1,2,0:T(8,128)S(1)}, f32[3,16,2,132]{3,1,2,0:T(8,128)S(1)}, u32[]{:S(2)}, u32[]{:S(2)}) collective-permute-start(f32[3,16,2,132]{3,1,2,0:T(8,128)S(1)} %get-tuple-element.23), channel_id=1, source_target_pairs={{1,0},{3,2},{5,4},{7,6},{9,8},{11,10},{13,12},{15,14},{17,16},{19,... | collective-permute-start | bytes 152072 | tf_op jit(solution)/shard_map/ppermute | solution.py:27
  30.2 4.7 %collective-permute-start.2 = (f32[3,16,2,132]{3,1,2,0:T(8,128)S(1)}, f32[3,16,2,132]{3,1,2,0:T(8,128)S(1)}, u32[]{:S(2)}, u32[]{:S(2)}) collective-permute-start(f32[3,16,2,132]{3,1,2,0:T(8,128)S(1)} %get-tuple-element.22), channel_id=1, source_target_pairs={{0,1},{2,3},{4,5},{6,7},{8,9},{10,11},{12,13},{14,15},{16,17},{18,... | collective-permute-start | bytes 152072 | tf_op jit(solution)/shard_map/ppermute | solution.py:26
  34.9 1.1 %broadcast_maximum_fusion.1 = (f32[16,33,128]{2,0,1:T(8,128)}, f32[16,33,128]{2,0,1:T(8,128)}, f32[16,33,128]{2,0,1:T(8,128)}, f32[16,33,128]{2,0,1:T(8,128)}) fusion(f32[16,32,128]{2,0,1:T(8,128)S(1)} %copy.77, f32[16,1,128]{2,0,1:T(8,128)S(1)} %bitcast.23), kind=kLoop, calls=%fused_computation.70 | loop fusion | flops 473088 | bytes 1351680 | tf_op jit(solution)/shard_map/max | solution.py:93
  36.0 0.9 %collective-permute-done.2 = f32[3,16,2,132]{3,1,2,0:T(8,128)S(1)} collective-permute-done((f32[3,16,2,132]{3,1,2,0:T(8,128)S(1)}, f32[3,16,2,132]{3,1,2,0:T(8,128)S(1)}, u32[]{:S(2)}, u32[]{:S(2)}) %collective-permute-start.2) | collective-permute-done | bytes 50720 | tf_op jit(solution)/shard_map/ppermute | solution.py:26
  36.9 1.9 %pad_maximum_fusion = f32[3,16,36,132]{3,1,2,0:T(8,128)S(1)} fusion(f32[3,16,2,132]{3,1,2,0:T(8,128)S(1)} %collective-permute-done.3, f32[3,16,32,2]{3,1,2,0:T(8,128)S(1)} %copy.71, f32[3,16,32,128]{3,1,2,0:T(8,128)S(1)} %copy.70, f32[3,16,32,2]{3,1,2,0:T(8,128)} %copy-done, f32[3,16,2,132]{3,1,2,0:T(8,128)S(1)} %collective-permute-done.2), kind=kLoop, calls=%fused_computation | loop fusion | flops 912384 | bytes 1824768 | tf_op jit(solution)/shard_map/concatenate | solution.py:28
  38.9 13.6 %all-gather.2.cloned.1.call-done = f32[3,16,3,2048]{3,2,1,0:T(4,128)} async-done(((f32[3,16,3,128]{3,2,1,0:T(4,128)}), f32[3,16,3,2048]{3,2,1,0:T(4,128)}) %all-gather.2.cloned.1.call-update) | async-done | bytes 1179664 | tf_op jit(solution)/shard_map/all_gather | solution.py:156
  52.4 0.9 %slice.341 = f32[3,16,3,1]{3,2,1,0:T(4,128)S(1)} slice(f32[3,16,3,2048]{3,2,1,0:T(4,128)} %all-gather.2.cloned.1.call-done), slice={[0:3], [0:16], [0:3], [0:1]} | slice | bytes 1152 | tf_op jit(solution)/shard_map/slice | solution.py:161
  53.4 8.6 %rev.8 = f32[3,16,3,2048]{3,2,1,0:T(4,128)S(1)} reverse(f32[3,16,3,2048]{3,2,1,0:T(4,128)} %all-gather.2.cloned.1.call-done), dimensions={3} | reverse | bytes 2359296 | tf_op jit(solution)/shard_map/jit(_flip)/rev | solution.py:159
  62.0 0.7 copy.73
  62.9 1.1 %scatter.4 = f32[3,16,36,132]{3,1,2,0:T(8,128)S(1)} dynamic-update-slice(f32[3,16,36,132]{3,1,2,0:T(8,128)S(1)} %pad_maximum_fusion, f32[3,16,2,128]{3,1,2,0:T(8,128)S(1)} %slice_select_fusion, s32[]{:T(128)} %constant.78.clone.1, s32[]{:T(128)} %constant.78.clone.1, s32[]{:T(128)} %constant.82.clone.1, s32[]{:T(128)} %constant.83.clone.1) | dynamic-update-slice | bytes 98308 | tf_op jit(solution)/shard_map/scatter | solution.py:166
  64.0 0.2 slice_subtract_fusion.9
  64.2 0.2 fusion
  64.4 0.3 multiply_subtract_fusion
  64.9 0.2 slice_multiply_fusion.1
  65.1 0.4 fusion.7
  65.5 0.2 slice_multiply_fusion
  65.9 0.3 fusion.25
  66.2 0.6 fusion.19
  66.9 0.3 fusion.5
  67.2 0.2 fusion.32
  67.6 0.3 pad_maximum_fusion.1
  67.9 0.5 copy-done.5
  68.6 0.7 fusion.11
  69.3 0.3 copy-done.1
  69.7 0.2 copy-done.2
  69.8 0.2 copy-done.3
  70.0 0.2 copy-done.4
  70.1 1.7 %fusion.4 = f32[2,16,32,129]{3,1,2,0:T(8,128)S(1)} fusion(f32[2,16,36,132]{3,1,2,0:T(8,128)S(1)} %pad_maximum_fusion.1, f32[3,16,36,132]{3,1,2,0:T(8,128)S(1)} %scatter.4, f32[2,16,32,131]{3,1,2,0:T(8,128)S(1)} %fusion.5, f32[16,32,129]{2,0,1:T(8,128)S(1)} %fusion.19, f32[16,32,129]{2,0,1:T(8,128)S(1)} %get-tuple-element.33, ...), kind=kLoop, calls=%fused_computation.10 | loop fusion | flops 3830784 | bytes 6076416 | tf_op jit(solution)/shard_map/add | solution.py:104
  71.8 0.4 fusion.13
  72.2 0.8 copy.79
  73.0 0.8 copy.80
  (39 shorter events, 1.4 us)
Async XLA Ops:
  7.2 45.3 %all-gather.2.cloned.1.call-start = ((), (), s32[]{:S(2)}) async-start(), calls=%async_computation | async-start | bytes 1671168 | tf_op jit(solution)/shard_map/all_gather | solution.py:156
  10.0 6.2 %copy-start.10 = (f32[16,32,128]{2,1,0:T(8,128)S(1)}, f32[16,32,128]{2,1,0:T(8,128)}, u32[]{:S(2)}) copy-start(f32[16,32,128]{2,1,0:T(8,128)} %param.10) | copy-start | bytes 786436
  10.0 9.8 %copy-start.9 = (f32[16,32,128]{2,1,0:T(8,128)S(1)}, f32[16,32,128]{2,1,0:T(8,128)}, u32[]{:S(2)}) copy-start(f32[16,32,128]{2,1,0:T(8,128)} %param.9) | copy-start | bytes 786436
  10.4 17.5 %collective-permute-start.1 = (f32[3,16,32,2]{2,1,3,0:T(8,128)S(1)}, f32[3,16,32,2]{2,1,3,0:T(8,128)S(1)}, u32[]{:S(2)}, u32[]{:S(2)}) collective-permute-start(f32[3,16,32,2]{2,1,3,0:T(8,128)S(1)} %copy.82), channel_id=1, source_target_pairs={{2,0},{4,2},{6,4},{8,6},{10,8},{12,10},{14,12},{16,14},{18,16},{20... | collective-permute-start | bytes 36872 | tf_op jit(solution)/shard_map/ppermute | solution.py:27
  16.2 12.1 %collective-permute-start = (f32[3,16,32,2]{2,1,3,0:T(8,128)S(1)}, f32[3,16,32,2]{2,1,3,0:T(8,128)S(1)}, u32[]{:S(2)}, u32[]{:S(2)}) collective-permute-start(f32[3,16,32,2]{2,1,3,0:T(8,128)S(1)} %copy.81), channel_id=1, source_target_pairs={{0,2},{2,4},{4,6},{6,8},{8,10},{10,12},{12,14},{14,16},{16,18},{18... | collective-permute-start | bytes 36872 | tf_op jit(solution)/shard_map/ppermute | solution.py:26
  16.4 18.5 %collective-permute-start.5 = (f32[16,128]{1,0:T(8,128)S(1)}, f32[16,128]{1,0:T(8,128)S(1)}, u32[]{:S(2)}, u32[]{:S(2)}) collective-permute-start(f32[16,128]{1,0:T(8,128)S(1)} %slice_bitcast_fusion.5), channel_id=1, source_target_pairs={{0,1},{2,3},{4,5},{6,7},{8,9},{10,11},{12,13},{14,15},{16,17},{18,... | collective-permute-start | bytes 24584 | tf_op jit(solution)/shard_map/ppermute | solution.py:40
  20.2 5.8 %collective-permute-start.4 = (f32[16,32]{1,0:T(8,128)S(1)}, f32[16,32]{1,0:T(8,128)S(1)}, u32[]{:S(2)}, u32[]{:S(2)}) collective-permute-start(f32[16,32]{1,0:T(8,128)S(1)} %bitcast.24), channel_id=1, source_target_pairs={{0,2},{2,4},{4,6},{6,8},{8,10},{10,12},{12,14},{14,16},{16,18},{18... | collective-permute-start | bytes 6152 | tf_op jit(solution)/shard_map/ppermute | solution.py:34
  28.7 7.3 %copy-start = (f32[3,16,32,2]{3,1,2,0:T(8,128)}, f32[3,16,32,2]{3,1,2,0:T(8,128)S(1)}, u32[]{:S(2)}) copy-start(f32[3,16,32,2]{3,1,2,0:T(8,128)S(1)} %copy.69) | copy-start | bytes 36868
  28.9 7.1 %collective-permute-start.3 = (f32[3,16,2,132]{3,1,2,0:T(8,128)S(1)}, f32[3,16,2,132]{3,1,2,0:T(8,128)S(1)}, u32[]{:S(2)}, u32[]{:S(2)}) collective-permute-start(f32[3,16,2,132]{3,1,2,0:T(8,128)S(1)} %get-tuple-element.23), channel_id=1, source_target_pairs={{1,0},{3,2},{5,4},{7,6},{9,8},{11,10},{13,12},{15,14},{17,16},{19,... | collective-permute-start | bytes 152072 | tf_op jit(solution)/shard_map/ppermute | solution.py:27
  30.2 6.8 %collective-permute-start.2 = (f32[3,16,2,132]{3,1,2,0:T(8,128)S(1)}, f32[3,16,2,132]{3,1,2,0:T(8,128)S(1)}, u32[]{:S(2)}, u32[]{:S(2)}) collective-permute-start(f32[3,16,2,132]{3,1,2,0:T(8,128)S(1)} %get-tuple-element.22), channel_id=1, source_target_pairs={{0,1},{2,3},{4,5},{6,7},{8,9},{10,11},{12,13},{14,15},{16,17},{18,... | collective-permute-start | bytes 152072 | tf_op jit(solution)/shard_map/ppermute | solution.py:26
  67.4 1.0 %copy-start.5 = (f32[16,33,128]{2,0,1:T(8,128)S(1)}, f32[16,33,128]{2,0,1:T(8,128)}, u32[]{:S(2)}) copy-start(f32[16,33,128]{2,0,1:T(8,128)} %get-tuple-element.40) | copy-start | bytes 811012
  67.4 1.0 %copy-start.6 = (f32[16,33,128]{2,0,1:T(8,128)S(1)}, f32[16,33,128]{2,0,1:T(8,128)}, u32[]{:S(2)}) copy-start(f32[16,33,128]{2,0,1:T(8,128)} %get-tuple-element.41) | copy-start | bytes 811012
  67.4 1.1 %copy-start.7 = (f32[16,33,128]{2,0,1:T(8,128)S(1)}, f32[16,33,128]{2,0,1:T(8,128)}, u32[]{:S(2)}) copy-start(f32[16,33,128]{2,0,1:T(8,128)} %get-tuple-element.42) | copy-start | bytes 811012
  67.4 1.2 %copy-start.8 = (f32[16,33,128]{2,0,1:T(8,128)S(1)}, f32[16,33,128]{2,0,1:T(8,128)}, u32[]{:S(2)}) copy-start(f32[16,33,128]{2,0,1:T(8,128)} %get-tuple-element.43) | copy-start | bytes 811012
  68.6 1.0 %copy-start.1 = (f32[16,32,129]{2,0,1:T(8,128)S(1)}, f32[16,32,129]{2,0,1:T(8,128)}, u32[]{:S(2)}) copy-start(f32[16,32,129]{2,0,1:T(8,128)} %get-tuple-element.34) | copy-start | bytes 792580
  68.6 1.2 %copy-start.2 = (f32[16,32,129]{2,0,1:T(8,128)S(1)}, f32[16,32,129]{2,0,1:T(8,128)}, u32[]{:S(2)}) copy-start(f32[16,32,129]{2,0,1:T(8,128)} %get-tuple-element.35) | copy-start | bytes 792580
  68.6 1.4 %copy-start.3 = (f32[16,32,129]{2,0,1:T(8,128)S(1)}, f32[16,32,129]{2,0,1:T(8,128)}, u32[]{:S(2)}) copy-start(f32[16,32,129]{2,0,1:T(8,128)} %get-tuple-element.36) | copy-start | bytes 792580
  68.6 1.5 %copy-start.4 = (f32[16,32,129]{2,0,1:T(8,128)S(1)}, f32[16,32,129]{2,0,1:T(8,128)}, u32[]{:S(2)}) copy-start(f32[16,32,129]{2,0,1:T(8,128)} %get-tuple-element.37) | copy-start | bytes 792580
Sparse Core Ops, SparseCore 0:
  10.7 41.6 all-gather.1
where the time goes:
time: 81.3 us; the launch traced here: 80.7 us
  waiting for transfers between devices  19.6 us (24%)
  local copies, waits for them, and re-layouts  18.5 us (23%)
  starting transfers between devices  15 us (18%)
  between operations  14.4 us (18%)
  other arithmetic  13.1 us (16%)
    all_gather x1, waiting for transfers between devices, body(): lax.all_gather(scalar_quantities[:3, :, latitude_band_sum - 3:, :], 'lon'...  13.6 us
    rev x2, local copies, waits for them, and re-layouts, body(): flipped = jnp.flip(whole_rows, -1)  9.33 us
    ppermute x2, starting transfers between devices, extended(): after = lax.ppermute(first, axis, down)  6.75 us
    ppermute x1, waiting for transfers between devices, passed_along(): lax.ppermute(array, axis, [(i, (i + by) % devices) for i in range(devices)])  5.11 us
    ppermute x2, starting transfers between devices, extended(): before = lax.ppermute(last, axis, up)  4.78 us
    unnamed x29, local copies, waits for them, and re-layouts  4.32 us
    ppermute x1, starting transfers between devices, passed_along_2(): return lax.ppermute(array, axis, pairs)  3.42 us
    max x2, other arithmetic, face_flux(): positive = jnp.maximum(face_speed, 0.0)  2.75 us
  transfers between devices with their start and end apart: 7, of which 3 were waited for; matrix products, arithmetic and copies ran while one was open for 10% of the time, Pallas kernels for 0%

commit v1 on v0

v1 whole, which is shorter than its diff:
```python
import functools

import jax
import jax.numpy as jnp
from jax import lax
from jax.experimental import pallas as pl
from jax.experimental.pallas import tpu as pltpu
from jax.sharding import PartitionSpec as P

heat_swelling_alpha = 0.1655
coef_beta = 0.76554
cabbeling_parameter = 0.05952
lambda_salt = 0.00054914
thermobaric_parameter = 0.0001497
press_salt = 1.109e-05
cross_coupling_contribution = 0.0024341
total_depth = 5000.0
kappa_iso = 0.1
strat_min = 0.1

LANES = 128
F32 = jnp.float32


def iota(shape, axis):
    return lax.broadcasted_iota(jnp.int32, shape, axis)


def roll(array, shift, axis=1):
    size = array.shape[axis]
    return pltpu.roll(array, shift % size, axis)


def minmod(x, y):
    return jnp.maximum(jnp.minimum(x, jnp.maximum(y, 0.0)), jnp.minimum(y, 0.0))


def level_factors(levels):
    depth = total_depth * (iota((levels, LANES), 0).astype(F32) + 0.5) / levels
    heat = -heat_swelling_alpha * (1.0 + thermobaric_parameter * depth)
    salt = coef_beta * (1.0 - press_salt * depth)
    return heat, salt


def density(t, s, factors):
    heat, salt = factors
    return t * (
        heat
        - (0.5 * heat_swelling_alpha * cabbeling_parameter) * t
        - cross_coupling_contribution * s
    ) + s * (salt - (0.5 * coef_beta * lambda_salt) * s)


def vertical(q, level):
    levels = q.shape[0]
    step = roll(q, -1, 0) - q
    below = roll(step, 1, 0)
    return jnp.where(level == levels - 1, below, step) + jnp.where(level == 0, step, below)


def column_row(t, s, n, factors, level):
    r = density(t, s, factors)
    return {
        "t": t,
        "s": s,
        "r": r,
        "tz": vertical(t, level),
        "sz": vertical(s, level),
        "rz": vertical(r, level),
        "n": n,
    }


def shifted(row, by):
    return {name: roll(value, by) for name, value in row.items()}


def weights(c, wet):
    size = jnp.abs(c)
    return jnp.where(wet, c, 0.0), jnp.where(wet, 0.5 * (size - c * c), 0.0)


def face_step(a, b, wet, name):
    return jnp.where(wet, b[name] - a[name], 0.0)


def face_base(a, b, c, wet, steps):
    wc, wg = weights(c, wet)
    steep = (a["r"] - b["r"]) / jnp.maximum(a["rz"] + b["rz"], 4.0 * strat_min)
    tilt = jnp.where(wet, jnp.clip(steep, -0.25, 0.25), 0.0) * (-kappa_iso)
    forward = c > 0.0
    base = [
        wc * jnp.where(forward, a[q], b[q]) - kappa_iso * d + tilt * (a[q + "z"] + b[q + "z"])
        for q, d in zip("ts", steps)
    ]
    return base, wg, forward


def strided(ref, row, levels, rows):
    return ref[pl.ds(row, levels, stride=rows), :]


def pack_kernel(levels, rows, t_ref, s_ref, c_ref, m_ref, n_ref, side_ref, north_ref, south_ref, fold_ref, own_ref):
    lane = iota((levels, LANES), 1)
    group = lane // 4

    def gather(ref):
        out = jnp.zeros((levels, LANES), F32)
        for j in range(rows):
            out = jnp.where(group == j, roll(strided(ref, j, levels, rows), 4 * j + 2), out)
        return out

    side_ref[0:levels, :] = gather(t_ref)
    side_ref[levels : 2 * levels, :] = gather(s_ref)
    side_ref[2 * levels : 3 * levels, :] = gather(c_ref)
    counts = n_ref[...].astype(F32)
    row = iota((rows, LANES), 0)
    lanes = iota((rows, LANES), 1)
    moved = jnp.concatenate(
        [roll(counts[j : j + 1], 4 * j + 2) for j in range(rows)], axis=0
    )
    line = jnp.sum(jnp.where(lanes // 4 == row, moved, 0.0), axis=0, keepdims=True)
    side_ref[3 * levels :, :] = jnp.broadcast_to(line, (8, LANES))

    def lines(out_ref, picks, tracers):
        at = 0
        for ref in tracers:
            for j in picks:
                out_ref[at : at + levels, :] = strided(ref, j, levels, rows)
                at += levels
        return at

    def tally(picks):
        return jnp.concatenate(
            [counts[j : j + 1] for j in picks] + [jnp.zeros((8 - len(picks), LANES), F32)], axis=0
        )

    at = lines(north_ref, (rows - 2, rows - 1), (t_ref, s_ref))
    north_ref[at : at + levels, :] = strided(m_ref, rows - 1, levels, rows)
    north_ref[at + levels :, :] = tally((rows - 2, rows - 1))
    at = lines(south_ref, (0, 1), (t_ref, s_ref))
    south_ref[at:, :] = tally((0, 1))
    own_ref[0:levels, :] = strided(m_ref, 0, levels, rows)
    own_ref[levels:, :] = strided(m_ref, rows - 2, levels, rows)

    def mirrored(x):
        index = (LANES - iota(x.shape, 1)) % LANES
        return jnp.take_along_axis(x, index, axis=1)

    at = 0
    for ref in (t_ref, s_ref):
        for j in (rows - 2, rows - 3):
            fold_ref[at : at + levels, :] = mirrored(strided(ref, j, levels, rows))
            at += levels
    fold_ref[at:, :] = mirrored(tally((rows - 2, rows - 3)))


NAMES = ("t", "s", "r", "tz", "sz", "rz")


def interior_kernel(levels, rows, t_ref, s_ref, c_ref, m_ref, n_ref, pt_ref, ps_ref):
    shape = (levels, LANES)
    level = iota(shape, 0)
    last_lane = iota((1, LANES), 1) == LANES - 1
    factors = level_factors(levels)
    zero = jnp.zeros(shape, F32)

    def step(j, carry):
        prev, m1, d2, limited2, base2, wg2, m2, acc2, acc1 = carry
        t, s = strided(t_ref, j, levels, rows), strided(s_ref, j, levels, rows)
        c, m = strided(c_ref, j, levels, rows), strided(m_ref, j, levels, rows)
        n = n_ref[pl.ds(j, 1), :]
        here = column_row(t, s, n, factors, level)
        east = shifted(here, -1)
        wet = level < jnp.minimum(n, jnp.where(last_lane, 0, east["n"]))
        steps = [face_step(here, east, wet, q) for q in "ts"]
        base, wg, forward = face_base(here, east, c, wet, steps)
        inside = level < n
        acc = []
        for q, d, flux in zip("ts", steps, base):
            limited = minmod(roll(d, 1), d)
            flux = flux + wg * jnp.where(forward, limited, roll(limited, -1))
            acc.append(jnp.where(inside, here[q], 0.0) + roll(flux, 1) - flux)
        wet = level < jnp.minimum(prev["n"], n)
        d1 = [face_step(prev, here, wet, q) for q in "ts"]
        base1, wg1, _ = face_base(prev, here, m1, wet, d1)
        limited1 = [minmod(x, y) for x, y in zip(d2, d1)]
        forward2 = m2 > 0.0
        flux2 = [b + wg2 * jnp.where(forward2, x, y) for b, x, y in zip(base2, limited2, limited1)]
        done = [x - f for x, f in zip(acc2, flux2)]
        acc1 = [x + f for x, f in zip(acc1, flux2)]
        pt_ref[pl.ds(j, 1)] = done[0][None]
        ps_ref[pl.ds(j, 1)] = done[1][None]
        return here, m, d1, limited1, base1, wg1, m1, acc1, acc

    nothing = [zero, zero]
    start = dict({name: zero for name in NAMES}, n=jnp.zeros((1, LANES), jnp.int32))
    carry = (start, zero, nothing, nothing, nothing, zero, zero, nothing, nothing)
    unroll = 4

    def block(i, carry):
        for u in range(unroll):
            carry = step(i * unroll + u, carry)
        return carry

    carry = lax.fori_loop(0, rows // unroll, block, carry)
    _, _, _, limited2, base2, wg2, m2, acc2, acc1 = carry
    flux2 = [b + wg2 * jnp.where(m2 > 0.0, x, 0.0) for b, x in zip(base2, limited2)]
    for ref, a2, a1, f in zip((pt_ref, ps_ref), acc2, acc1, flux2):
        ref[rows] = a2 - f
        ref[rows + 1] = a1 + f


def edge_kernel(
    levels, rows, top_ref, pt_ref, ps_ref, side_ref, north_ref, south_ref, own_ref,
    west_in, east_in, fold_column_in, below_in, above_in, fold_in, t_ref, s_ref,
):
    shape = (levels, LANES)
    level = iota(shape, 0).astype(F32)
    lane = iota(shape, 1)
    place = lane % 4
    factors = level_factors(levels)
    K = levels

    def faces(cells, speeds):
        wets = [level < jnp.minimum(a["n"], b["n"]) for a, b in zip(cells, cells[1:])]
        d = [[face_step(a, b, w, q) for q in "ts"] for a, b, w in zip(cells, cells[1:], wets)]
        limited = [[minmod(x, y) for x, y in zip(d[i], d[i + 1])] for i in (0, 1)]
        base, wg, forward = face_base(cells[1], cells[2], speeds[1], wets[1], d[1])
        flux = [b + wg * jnp.where(forward, x, y) for b, x, y in zip(base, *limited)]
        first = last = None
        if speeds[0] is not None:
            _, wg0 = weights(speeds[0], wets[0])
            first = [wg0 * jnp.where(speeds[0] > 0.0, 0.0, x) for x in limited[0]]
        if speeds[2] is not None:
            _, wg2 = weights(speeds[2], wets[2])
            last = [wg2 * jnp.where(speeds[2] > 0.0, x, 0.0) for x in limited[1]]
        return first, flux, last

    own, west, east = side_ref[...], west_in[...], east_in[...]

    def side(left, right):
        both = jnp.where(iota(left.shape, 1) % 4 < 2, left, right)
        row = column_row(both[:K], both[K : 2 * K], both[3 * K : 3 * K + 1], factors, iota(shape, 0))
        cells = [row] + [shifted(row, -i) for i in (1, 2, 3)]
        speed = both[2 * K : 3 * K]
        return faces(cells, [roll(speed, -i) for i in range(3)])

    _, west_flux, west_last = side(west, own)
    east_first, east_flux, _ = side(own, east)
    lon = []
    for fw, lw, fe, le in zip(west_flux, west_last, east_first, east_flux):
        group = jnp.where(
            place == 0,
            -fe,
            jnp.where(place == 1, roll(fe - le, 1), jnp.where(place == 2, roll(fw - lw, 2), roll(lw, 3))),
        )
        lon.append(group)

    def cell(array, which, fix=None):
        t, s = array[which * K : (which + 1) * K], array[(2 + which) * K : (3 + which) * K]
        return t, s

    def rows_of(array, at_counts, which):
        t, s = array[which * K : (which + 1) * K], array[(2 + which) * K : (3 + which) * K]
        n = array[at_counts + which : at_counts + which + 1]
        return column_row(t, s, n, factors, iota(shape, 0))

    below, south, north = below_in[...], south_ref[...], north_ref[...]
    own_speeds = own_ref[...]
    cells = [rows_of(below, 5 * K, 0), rows_of(below, 5 * K, 1), rows_of(south, 4 * K, 0), rows_of(south, 4 * K, 1)]
    _, south_flux, south_last = faces(cells, [None, below[4 * K : 5 * K], own_speeds[:K]])

    is_top = top_ref[0] > 0
    fold, column = fold_in[...], fold_column_in[...]
    parts = []
    for q in range(2):
        for j in (rows - 2, rows - 3):
            parts.append(roll(column[q * K : (q + 1) * K], -(4 * j + 2)))
    line = column[3 * K : 3 * K + 1]
    parts.append(
        jnp.concatenate(
            [roll(line, -(4 * (rows - 2) + 2)), roll(line, -(4 * (rows - 3) + 2)), jnp.zeros((6, LANES), F32)], axis=0
        )
    )
    fold = jnp.where(iota(fold.shape, 1) == 0, jnp.concatenate(parts, axis=0), fold)
    above = jnp.where(is_top, fold, above_in[...])
    cells = [rows_of(north, 5 * K, 0), rows_of(north, 5 * K, 1), rows_of(above, 4 * K, 0), rows_of(above, 4 * K, 1)]
    north_first, north_flux, _ = faces(cells, [own_speeds[K:], north[4 * K : 5 * K], None])

    edge_lanes = (lane >= LANES - 2) | (lane < 2)
    for q, (p_ref, out_ref) in enumerate(((pt_ref, t_ref), (ps_ref, s_ref))):
        extra = {
            0: south_flux[q] - south_last[q],
            1: south_last[q],
            rows - 2: -north_first[q],
            rows - 1: north_first[q] - north_flux[q],
        }
        for j in range(rows):
            value = p_ref[j + 2] + jnp.where(edge_lanes, roll(lon[q], LANES - 2 - 4 * j), 0.0)
            if j in extra:
                value = value + extra[j]
            out_ref[pl.ds(j, levels, stride=rows), :] = value


def body(nlat, nlon, t, s, c, m, n):
    levels, rows, _ = t.shape
    vmem = pl.BlockSpec(memory_space=pltpu.VMEM)
    flat = [x.reshape(levels * rows, LANES) for x in (t, s, c, m)]
    f = functools.partial
    out = lambda *shape: jax.ShapeDtypeStruct(shape, F32)
    K = levels
    side, north, south, fold, own = pl.pallas_call(
        f(pack_kernel, levels, rows),
        out_shape=(out(3 * K + 8, LANES), out(5 * K + 8, LANES), out(4 * K + 8, LANES), out(4 * K + 8, LANES), out(2 * K, LANES)),
        in_specs=[vmem] * 5,
        out_specs=(vmem,) * 5,
        name="pack",
    )(*flat, n)

    def at(lat, lon):
        return (lon % nlon) * nlat + lat

    ring = range(nlon)
    both = ("lon", "lat")
    west_in = lax.ppermute(side, "lon", [(i, (i + 1) % nlon) for i in ring])
    fold_in = lax.ppermute(fold, both, [(at(nlat - 1, i), at(nlat - 1, nlon - 1 - i)) for i in ring])
    fold_column_in = lax.ppermute(side, both, [(at(nlat - 1, i), at(nlat - 1, nlon - i)) for i in ring])
    east_in = lax.ppermute(side, "lon", [(i, (i - 1) % nlon) for i in ring])
    below_in = lax.ppermute(north, "lat", [(i, i + 1) for i in range(nlat - 1)])
    above_in = lax.ppermute(south, "lat", [(i + 1, i) for i in range(nlat - 1)])

    pt, ps = pl.pallas_call(
        f(interior_kernel, levels, rows),
        out_shape=(out(rows + 2, K, LANES),) * 2,
        in_specs=[vmem] * 5,
        out_specs=(vmem,) * 2,
        cost_estimate=pl.CostEstimate(flops=40_000_000, bytes_accessed=2_000_000, transcendentals=0),
        name="interior",
    )(*flat, n)

    top = (lax.axis_index("lat") == nlat - 1).astype(jnp.int32).reshape(1)
    t_next, s_next = pl.pallas_call(
        f(edge_kernel, levels, rows),
        out_shape=(out(levels * rows, LANES),) * 2,
        in_specs=[pl.BlockSpec(memory_space=pltpu.SMEM)] + [vmem] * 12,
        out_specs=(vmem,) * 2,
        name="edge",
    )(top, pt, ps, side, north, south, own, west_in, east_in, fold_column_in, below_in, above_in, fold_in)
    return t_next.reshape(t.shape), s_next.reshape(t.shape)


def solution(mesh):
    spec = P(None, "lat", "lon")
    return jax.shard_map(
        functools.partial(body, mesh.shape["lat"], mesh.shape["lon"]),
        mesh=mesh,
        in_specs=(spec,) * 4 + (P("lat", "lon"),),
        out_specs=(spec,) * 2,
        check_vma=False,
    )
```

time: 81.3 us -> 25.2 us (0.31)
  waiting for transfers between devices: 19.6 us -> 1.35 us
  local copies, waits for them, and re-layouts: 18.5 us -> 0.63 us
  between operations: 14.4 us -> 0.71 us
  other arithmetic: 13.1 us -> 0 us
  Pallas kernels: 0 us -> 9.6 us
  starting transfers between devices: 15 us -> 12.7 us
    all_gather x1 -> x0, waiting for transfers between devices: 13.6 us -> none  [body(): lax.all_gather(scalar_quantities[:3, :, latitude_band_sum - 3:, :], 'lon'...]
    pallas_call x0 -> x3, Pallas kernels: none -> 9.6 us  [the longest x1 4.67 us: body(): pl.pallas_call(f(interior_kernel, levels, rows), out_shape=(out(rows + 2,...]
    rev x2 -> x0, local copies, waits for them, and re-layouts: 9.33 us -> none  [body(): flipped = jnp.flip(whole_rows, -1)]
    ppermute x6, waiting for transfers between devices: 6.03 us -> 1.35 us  [the longest x1 1.34 us: body(): west_in = lax.ppermute(side, 'lon', [(i, (i + 1) % nlon) for i in ring])]
    unnamed x29 -> x12, local copies, waits for them, and re-layouts: 4.32 us -> 0.63 us
    max x2 -> x0, other arithmetic: 2.75 us -> none  [face_flux(): positive = jnp.maximum(face_speed, 0.0)]
    mul x10 -> x0, other arithmetic: 2.7 us -> none  [the longest x2 0.96 us: face_flux(): slope_face * vert_face]
    concatenate x4 -> x0, other arithmetic: 2.45 us -> none  [the longest x1 1.92 us: extended(): array = jnp.concatenate([before, array, after], axis=dim)]
  transfers between devices with their start and end apart: 7 -> 6, of which waited for: 3 -> 1; matrix products, arithmetic and copies ran while one was open for 10% -> 0% of each run, Pallas kernels for 0% -> 19%
where the time goes in v1:
time: 25.2 us; the launch traced here: 25 us
  starting transfers between devices  12.7 us (50%)
  Pallas kernels  9.6 us (38%)
  waiting for transfers between devices  1.35 us (5%)
  between operations  0.71 us (3%)
  local copies, waits for them, and re-layouts  0.63 us (2%)
    ppermute x1, starting transfers between devices, body(): below_in = lax.ppermute(north, 'lat', [(i, i + 1) for i in range(nlat - 1)])  5.6 us
    pallas_call x1, Pallas kernels, body(): pl.pallas_call(f(interior_kernel, levels, rows), out_shape=(out(rows + 2,...  4.67 us
    ppermute x1, starting transfers between devices, body(): east_in = lax.ppermute(side, 'lon', [(i, (i - 1) % nlon) for i in ring])  4.27 us
    pallas_call x1, Pallas kernels, body(): pl.pallas_call(f(edge_kernel, levels, rows), out_shape=(out(levels * rows...  2.57 us
    pallas_call x1, Pallas kernels, body(): pl.pallas_call(f(pack_kernel, levels, rows), out_shape=(out(3 * K + 8, LA...  2.36 us
    ppermute x1, waiting for transfers between devices, body(): west_in = lax.ppermute(side, 'lon', [(i, (i + 1) % nlon) for i in ring])  1.34 us
    ppermute x1, starting transfers between devices, body(): above_in = lax.ppermute(south, 'lat', [(i + 1, i) for i in range(nlat - 1)])  1.29 us
    ppermute x1, starting transfers between devices, body(): lax.ppermute(fold, both, [(at(nlat - 1, i), at(nlat - 1, nlon - 1 - i)) f...  0.66 us
  transfers between devices with their start and end apart: 6, of which 1 were waited for; matrix products, arithmetic and copies ran while one was open for 0% of the time, Pallas kernels for 19%

profile of v1, /device:TPU:0, one launch (start us, length us, event | category | flops | bytes accessed | tf_op | source)
XLA Modules:
  0.0 25.0 jit_solution(14629344279706109672)
XLA Ops:
  0.6 2.4 %pack.1 = (f32[56,128]{1,0:T(8,128)}, f32[88,128]{1,0:T(8,128)}, f32[72,128]{1,0:T(8,128)}, f32[72,128]{1,0:T(8,128)}, f32[32,128]{1,0:T(8,128)}) custom-call(f32[512,128]{1,0:T(8,128)} %bitcast.7, f32[512,128]{1,0:T(8,128)} %bitcast.9, f32[512,128]{1,0:T(8,128)} %bitcast.11, f32[512,128]{1,0:T(8,128)} %bitcast.13, s32[32,128]{1,0:T(8,128)} %n_ref.3), custom_call_target="tpu_custom_call" | custom-call | tf_op jit(solution)/shard_map/pack/pallas_call | solution.py:313
  3.0 0.7 %collective-permute-start.2 = (f32[56,128]{1,0:T(8,128)}, f32[56,128]{1,0:T(8,128)S(1)}, u32[]{:S(2)}, u32[]{:S(2)}) collective-permute-start(f32[56,128]{1,0:T(8,128)} %get-tuple-element.13.side_ref), channel_id=1, source_target_pairs={{1,1},{3,31},{5,29},{7,27},{9,25},{11,23},{13,21},{15,19},{17,17},... | collective-permute-start | bytes 86024 | tf_op jit(solution)/shard_map/ppermute | solution.py:328
  3.6 5.6 %collective-permute-start.3 = (f32[88,128]{1,0:T(8,128)}, f32[88,128]{1,0:T(8,128)S(1)}, u32[]{:S(2)}, u32[]{:S(2)}) collective-permute-start(f32[88,128]{1,0:T(8,128)} %get-tuple-element.14.north_ref), channel_id=1, source_target_pairs={{0,1},{2,3},{4,5},{6,7},{8,9},{10,11},{12,13},{14,15},{16,17},{18,... | collective-permute-start | bytes 135176 | tf_op jit(solution)/shard_map/ppermute | solution.py:330
  9.2 0.7 %collective-permute-start.5 = (f32[72,128]{1,0:T(8,128)}, f32[72,128]{1,0:T(8,128)S(1)}, u32[]{:S(2)}, u32[]{:S(2)}) collective-permute-start(f32[72,128]{1,0:T(8,128)} %get-tuple-element.17), channel_id=1, source_target_pairs={{1,31},{3,29},{5,27},{7,25},{9,23},{11,21},{13,19},{15,17},{17,15}... | collective-permute-start | bytes 110600 | tf_op jit(solution)/shard_map/ppermute | solution.py:327
  9.9 1.3 %collective-permute-start.4 = (f32[72,128]{1,0:T(8,128)}, f32[72,128]{1,0:T(8,128)S(1)}, u32[]{:S(2)}, u32[]{:S(2)}) collective-permute-start(f32[72,128]{1,0:T(8,128)} %get-tuple-element.15.south_ref), channel_id=1, source_target_pairs={{1,0},{3,2},{5,4},{7,6},{9,8},{11,10},{13,12},{15,14},{17,16},{19,... | collective-permute-start | bytes 110600 | tf_op jit(solution)/shard_map/ppermute | solution.py:331
  11.2 4.3 %collective-permute-start.1 = (f32[56,128]{1,0:T(8,128)}, f32[56,128]{1,0:T(8,128)S(1)}, u32[]{:S(2)}, u32[]{:S(2)}) collective-permute-start(f32[56,128]{1,0:T(8,128)} %get-tuple-element.13.side_ref), channel_id=1, source_target_pairs={{0,30},{2,0},{4,2},{6,4},{8,6},{10,8},{12,10},{14,12},{16,14},{18,... | collective-permute-start | bytes 86024 | tf_op jit(solution)/shard_map/ppermute | solution.py:329
  15.5 0.0 collective-permute-done.2.fold_column_in
  15.5 0.0 copy-start.3
  15.5 0.2 collective-permute-start
  15.7 4.7 %interior.1 = (f32[34,16,128]{2,1,0:T(8,128)}, f32[34,16,128]{2,1,0:T(8,128)}) custom-call(f32[512,128]{1,0:T(8,128)} %bitcast.8, f32[512,128]{1,0:T(8,128)} %bitcast.10, f32[512,128]{1,0:T(8,128)} %bitcast.12, f32[512,128]{1,0:T(8,128)} %bitcast.14, s32[32,128]{1,0:T(8,128)} %n_ref.3), custom_call_target="tpu_custom_call" | custom-call | flops 40000000 | bytes 2000000 | tf_op jit(solution)/shard_map/interior/pallas_call | solution.py:333
  20.4 0.0 copy-done.3
  20.4 0.0 collective-permute-done.1.east_in
  20.4 0.0 copy-start.4
  20.4 1.3 %collective-permute-done.west_in = f32[56,128]{1,0:T(8,128)S(1)} collective-permute-done((f32[56,128]{1,0:T(8,128)}, f32[56,128]{1,0:T(8,128)S(1)}, u32[]{:S(2)}, u32[]{:S(2)}) %collective-permute-start) | collective-permute-done | bytes 28704 | tf_op jit(solution)/shard_map/ppermute | solution.py:326
  21.7 0.0 copy-start.5
  21.7 0.0 collective-permute-done.5.fold_in
  21.7 0.0 copy-start.1
  21.7 0.0 collective-permute-done.4.above_in
  21.7 0.0 copy-start.2
  21.7 0.0 collective-permute-done.3.below_in
  21.7 0.0 copy-start
  21.8 0.0 copy-done.4
  21.8 0.6 %copy-done.5 = f32[56,128]{1,0:T(8,128)} copy-done((f32[56,128]{1,0:T(8,128)}, f32[56,128]{1,0:T(8,128)S(1)}, u32[]{:S(2)}) %copy-start.5) | copy-done | bytes 28696
  22.3 0.0 copy-done.1
  22.3 0.0 copy-done.2
  22.4 0.0 copy-done
  22.4 2.6 %edge.1 = (f32[512,128]{1,0:T(8,128)}, f32[512,128]{1,0:T(8,128)}) custom-call(s32[1]{0:T(128)} %bitcast.top_ref, f32[34,16,128]{2,1,0:T(8,128)} %get-tuple-element.11.pt_ref, f32[34,16,128]{2,1,0:T(8,128)} %get-tuple-element.12.ps_ref, f32[56,128]{1,0:T(8,128)} %get-tuple-element.13.side_ref, f32[88,128]{1,0:T(8,128)} %get-tuple-element.14.north_ref, ...), custom_call_target="tpu_custom_call" | custom-call | tf_op jit(solution)/shard_map/edge/pallas_call | solution.py:343
Async XLA Ops:
  3.0 12.5 %collective-permute-start.2 = (f32[56,128]{1,0:T(8,128)}, f32[56,128]{1,0:T(8,128)S(1)}, u32[]{:S(2)}, u32[]{:S(2)}) collective-permute-start(f32[56,128]{1,0:T(8,128)} %get-tuple-element.13.side_ref), channel_id=1, source_target_pairs={{1,1},{3,31},{5,29},{7,27},{9,25},{11,23},{13,21},{15,19},{17,17},... | collective-permute-start | bytes 86024 | tf_op jit(solution)/shard_map/ppermute | solution.py:328
  3.6 18.1 %collective-permute-start.3 = (f32[88,128]{1,0:T(8,128)}, f32[88,128]{1,0:T(8,128)S(1)}, u32[]{:S(2)}, u32[]{:S(2)}) collective-permute-start(f32[88,128]{1,0:T(8,128)} %get-tuple-element.14.north_ref), channel_id=1, source_target_pairs={{0,1},{2,3},{4,5},{6,7},{8,9},{10,11},{12,13},{14,15},{16,17},{18,... | collective-permute-start | bytes 135176 | tf_op jit(solution)/shard_map/ppermute | solution.py:330
  9.2 12.5 %collective-permute-start.5 = (f32[72,128]{1,0:T(8,128)}, f32[72,128]{1,0:T(8,128)S(1)}, u32[]{:S(2)}, u32[]{:S(2)}) collective-permute-start(f32[72,128]{1,0:T(8,128)} %get-tuple-element.17), channel_id=1, source_target_pairs={{1,31},{3,29},{5,27},{7,25},{9,23},{11,21},{13,19},{15,17},{17,15}... | collective-permute-start | bytes 110600 | tf_op jit(solution)/shard_map/ppermute | solution.py:327
  9.9 11.8 %collective-permute-start.4 = (f32[72,128]{1,0:T(8,128)}, f32[72,128]{1,0:T(8,128)S(1)}, u32[]{:S(2)}, u32[]{:S(2)}) collective-permute-start(f32[72,128]{1,0:T(8,128)} %get-tuple-element.15.south_ref), channel_id=1, source_target_pairs={{1,0},{3,2},{5,4},{7,6},{9,8},{11,10},{13,12},{15,14},{17,16},{19,... | collective-permute-start | bytes 110600 | tf_op jit(solution)/shard_map/ppermute | solution.py:331
  11.2 9.1 %collective-permute-start.1 = (f32[56,128]{1,0:T(8,128)}, f32[56,128]{1,0:T(8,128)S(1)}, u32[]{:S(2)}, u32[]{:S(2)}) collective-permute-start(f32[56,128]{1,0:T(8,128)} %get-tuple-element.13.side_ref), channel_id=1, source_target_pairs={{0,30},{2,0},{4,2},{6,4},{8,6},{10,8},{12,10},{14,12},{16,14},{18,... | collective-permute-start | bytes 86024 | tf_op jit(solution)/shard_map/ppermute | solution.py:329
  15.5 4.9 %copy-start.3 = (f32[56,128]{1,0:T(8,128)}, f32[56,128]{1,0:T(8,128)S(1)}, u32[]{:S(2)}) copy-start(f32[56,128]{1,0:T(8,128)S(1)} %collective-permute-done.2.fold_column_in) | copy-start | bytes 86020
  15.5 6.2 %collective-permute-start = (f32[56,128]{1,0:T(8,128)}, f32[56,128]{1,0:T(8,128)S(1)}, u32[]{:S(2)}, u32[]{:S(2)}) collective-permute-start(f32[56,128]{1,0:T(8,128)} %get-tuple-element.13.side_ref), channel_id=1, source_target_pairs={{0,2},{2,4},{4,6},{6,8},{8,10},{10,12},{12,14},{14,16},{16,18},{18... | collective-permute-start | bytes 86024 | tf_op jit(solution)/shard_map/ppermute | solution.py:326
  20.4 1.4 %copy-start.4 = (f32[56,128]{1,0:T(8,128)}, f32[56,128]{1,0:T(8,128)S(1)}, u32[]{:S(2)}) copy-start(f32[56,128]{1,0:T(8,128)S(1)} %collective-permute-done.1.east_in) | copy-start | bytes 86020
  21.7 0.6 %copy-start.5 = (f32[56,128]{1,0:T(8,128)}, f32[56,128]{1,0:T(8,128)S(1)}, u32[]{:S(2)}) copy-start(f32[56,128]{1,0:T(8,128)S(1)} %collective-permute-done.west_in) | copy-start | bytes 86020
  21.7 0.6 %copy-start.1 = (f32[72,128]{1,0:T(8,128)}, f32[72,128]{1,0:T(8,128)S(1)}, u32[]{:S(2)}) copy-start(f32[72,128]{1,0:T(8,128)S(1)} %collective-permute-done.5.fold_in) | copy-start | bytes 110596
  21.7 0.6 %copy-start.2 = (f32[72,128]{1,0:T(8,128)}, f32[72,128]{1,0:T(8,128)S(1)}, u32[]{:S(2)}) copy-start(f32[72,128]{1,0:T(8,128)S(1)} %collective-permute-done.4.above_in) | copy-start | bytes 110596
  21.7 0.6 %copy-start = (f32[88,128]{1,0:T(8,128)}, f32[88,128]{1,0:T(8,128)S(1)}, u32[]{:S(2)}) copy-start(f32[88,128]{1,0:T(8,128)S(1)} %collective-permute-done.3.below_in) | copy-start | bytes 135172

commit v2 on v1

v2 whole, which is shorter than its diff:
```python
import functools

import jax
import jax.numpy as jnp
from jax import lax
from jax.experimental import pallas as pl
from jax.experimental.pallas import tpu as pltpu
from jax.sharding import PartitionSpec as P

heat_swelling_alpha = 0.1655
coef_beta = 0.76554
cabbeling_parameter = 0.05952
lambda_salt = 0.00054914
thermobaric_parameter = 0.0001497
press_salt = 1.109e-05
cross_coupling_contribution = 0.0024341
total_depth = 5000.0
kappa_iso = 0.1
strat_min = 0.1

LANES = 128
VMEM = 8 * 1024 * 1024
UNROLL = 8
F32 = jnp.float32


def iota(shape, axis):
    return lax.broadcasted_iota(jnp.int32, shape, axis)


def roll(array, shift, axis=1):
    size = array.shape[axis]
    return pltpu.roll(array, shift % size, axis)


def minmod(x, y):
    return jnp.maximum(jnp.minimum(x, jnp.maximum(y, 0.0)), jnp.minimum(y, 0.0))


def level_factors(levels):
    depth = total_depth * (iota((levels, LANES), 0).astype(F32) + 0.5) / levels
    heat = -heat_swelling_alpha * (1.0 + thermobaric_parameter * depth)
    salt = coef_beta * (1.0 - press_salt * depth)
    return heat, salt


def density(t, s, factors):
    heat, salt = factors
    return t * (
        heat
        - (0.5 * heat_swelling_alpha * cabbeling_parameter) * t
        - cross_coupling_contribution * s
    ) + s * (salt - (0.5 * coef_beta * lambda_salt) * s)


def vertical(q, level):
    levels = q.shape[0]
    step = roll(q, -1, 0) - q
    below = roll(step, 1, 0)
    return jnp.where(level == levels - 1, below, step) + jnp.where(level == 0, step, below)


def column_row(t, s, n, factors, level):
    r = density(t, s, factors)
    return {
        "t": t,
        "s": s,
        "r": r,
        "tz": vertical(t, level),
        "sz": vertical(s, level),
        "rz": vertical(r, level),
        "n": n,
    }


def shifted(row, by):
    return {name: roll(value, by) for name, value in row.items()}


def weights(c, wet):
    size = jnp.abs(c)
    return jnp.where(wet, c, 0.0), jnp.where(wet, 0.5 * (size - c * c), 0.0)


def face_step(a, b, wet, name):
    return jnp.where(wet, b[name] - a[name], 0.0)


def face_base(a, b, c, wet, steps):
    wc, wg = weights(c, wet)
    steep = (a["r"] - b["r"]) / jnp.maximum(a["rz"] + b["rz"], 4.0 * strat_min)
    tilt = jnp.where(wet, jnp.clip(steep, -0.25, 0.25), 0.0) * (-kappa_iso)
    forward = c > 0.0
    base = [
        wc * jnp.where(forward, a[q], b[q]) - kappa_iso * d + tilt * (a[q + "z"] + b[q + "z"])
        for q, d in zip("ts", steps)
    ]
    return base, wg, forward


def strided(ref, row):
    levels, rows, _ = ref.shape
    return ref.reshape(levels * rows, LANES)[pl.ds(row, levels, stride=rows), :]


def put(ref, row, value):
    levels, rows, _ = ref.shape
    ref.reshape(levels * rows, LANES)[pl.ds(row, levels, stride=rows), :] = value


def pack_kernel(
    levels, rows, lat_size, t_hbm, s_hbm, c_hbm, m_hbm, n_hbm,
    t_ref, s_ref, c_ref, m_ref, n_ref, side_ref, lat_ref, fold_ref, column_ref, own_ref, *more,
):
    *more, t_in, s_in, c_in, sems = more
    K = levels
    pairs = ((t_hbm, t_in), (s_hbm, s_in), (c_hbm, c_in), (n_hbm, n_ref), (m_hbm, m_ref))
    copies = [pltpu.make_async_copy(src, dst, sems.at[i]) for i, (src, dst) in enumerate(pairs)]
    for copy in copies:
        copy.start()
    lane = iota((levels, LANES), 1)
    group = lane // 4

    def gather(ref, rows_ref):
        out = jnp.zeros((levels, LANES), F32)
        for j in range(rows):
            row = strided(ref, j)
            rows_ref[j] = row
            out = jnp.where(group == j, roll(row, 4 * j + 2), out)
        return out

    def mirrored(x):
        index = (LANES - iota(x.shape, 1)) % LANES
        return jnp.take_along_axis(x, index, axis=1)

    def tracer_rows(out_ref, tracer, ref, picks, change=lambda x: x):
        for i, j in enumerate(picks):
            at = (2 * tracer + i) * K
            out_ref[at : at + K, :] = change(ref[j])

    south, north, fold = (0, 1), (rows - 2, rows - 1), (rows - 2, rows - 3)
    is_top = lax.axis_index("lat") == lat_size - 1
    for tracer, (ref, source) in enumerate(((t_ref, t_in), (s_ref, s_in))):
        copies[tracer].wait()
        side_ref[tracer * K : (tracer + 1) * K, :] = gather(source, ref)
        tracer_rows(fold_ref, tracer, ref, fold, mirrored)
        if more:
            tracer_rows(lat_ref, tracer, ref, north)
            tracer_rows(more[0], tracer, ref, south)
        else:
            for i in range(2):
                at = (2 * tracer + i) * K
                lat_ref[at : at + K, :] = jnp.where(is_top, ref[south[i]], ref[north[i]])

    copies[2].wait()
    side_ref[2 * K : 3 * K, :] = gather(c_in, c_ref)
    copies[3].wait()
    counts = n_ref[...].astype(F32)
    moved = jnp.concatenate([roll(counts[j : j + 1], 4 * j + 2) for j in range(rows)], axis=0)
    line = jnp.sum(
        jnp.where(iota((rows, LANES), 1) // 4 == iota((rows, LANES), 0), moved, 0.0), axis=0, keepdims=True
    )
    side_ref[3 * K :, :] = jnp.broadcast_to(line, (8, LANES))

    def tally(picks):
        return jnp.concatenate(
            [counts[j : j + 1] for j in picks] + [jnp.zeros((8 - len(picks), LANES), F32)], axis=0
        )

    fold_ref[4 * K :, :] = mirrored(tally(fold))
    first = jnp.zeros((levels, LANES), F32)
    for i, (ref, j) in enumerate((ref, j) for ref in (t_ref, s_ref) for j in fold):
        first = jnp.where(lane == i, roll(ref[j], i), first)
    column_ref[:K, :] = first
    column_ref[K : K + 8, :] = tally(fold)
    if more:
        lat_ref[5 * K :, :] = tally(north)
        more[0][4 * K : 5 * K, :] = jnp.zeros((K, LANES), F32)
        more[0][5 * K :, :] = tally(south)
    else:
        lat_ref[5 * K :, :] = jnp.where(is_top, tally(south), tally(north))
    copies[4].wait()
    lat_ref[4 * K : 5 * K, :] = strided(m_ref, rows - 1)
    for i, j in enumerate((0, rows - 2, rows - 1)):
        own_ref[i * K : (i + 1) * K, :] = strided(m_ref, j)


NAMES = ("t", "s", "r", "tz", "sz", "rz")


def interior_kernel(levels, rows, t_ref, s_ref, c_ref, m_ref, n_ref, pt_ref, ps_ref):
    shape = (levels, LANES)
    level = iota(shape, 0)
    last_lane = iota((1, LANES), 1) == LANES - 1
    factors = level_factors(levels)
    zero = jnp.zeros(shape, F32)

    def step(j, carry):
        prev, m1, d2, limited2, base2, wg2, m2, acc2, acc1 = carry
        t, s, c, m = t_ref[j], s_ref[j], c_ref[j], strided(m_ref, j)
        n = n_ref[pl.ds(j, 1), :]
        here = column_row(t, s, n, factors, level)
        east = shifted(here, -1)
        wet = level < jnp.minimum(n, jnp.where(last_lane, 0, east["n"]))
        steps = [face_step(here, east, wet, q) for q in "ts"]
        base, wg, forward = face_base(here, east, c, wet, steps)
        inside = level < n
        acc = []
        for q, d, flux in zip("ts", steps, base):
            limited = minmod(roll(d, 1), d)
            flux = flux + wg * jnp.where(forward, limited, roll(limited, -1))
            acc.append(jnp.where(inside, here[q], 0.0) + roll(flux, 1) - flux)
        wet = level < jnp.minimum(prev["n"], n)
        d1 = [face_step(prev, here, wet, q) for q in "ts"]
        base1, wg1, _ = face_base(prev, here, m1, wet, d1)
        limited1 = [minmod(x, y) for x, y in zip(d2, d1)]
        forward2 = m2 > 0.0
        flux2 = [b + wg2 * jnp.where(forward2, x, y) for b, x, y in zip(base2, limited2, limited1)]
        done = [x - f for x, f in zip(acc2, flux2)]
        acc1 = [x + f for x, f in zip(acc1, flux2)]
        pt_ref[pl.ds(j, 1)] = done[0][None]
        ps_ref[pl.ds(j, 1)] = done[1][None]
        return here, m, d1, limited1, base1, wg1, m1, acc1, acc

    nothing = [zero, zero]
    start = dict({name: zero for name in NAMES}, n=jnp.zeros((1, LANES), jnp.int32))
    carry = (start, zero, nothing, nothing, nothing, zero, zero, nothing, nothing)

    def block(i, carry):
        for u in range(UNROLL):
            carry = step(i * UNROLL + u, carry)
        return carry

    carry = lax.fori_loop(0, rows // UNROLL, block, carry)
    _, _, _, limited2, base2, wg2, m2, acc2, acc1 = carry
    flux2 = [b + wg2 * jnp.where(m2 > 0.0, x, 0.0) for b, x in zip(base2, limited2)]
    for ref, a2, a1, f in zip((pt_ref, ps_ref), acc2, acc1, flux2):
        ref[rows] = a2 - f
        ref[rows + 1] = a1 + f


def edge_kernel(
    levels, rows, lat_size, lon_size, pt_ref, ps_ref, side_ref, t_ref, s_ref, n_ref, own_ref,
    core_in, inter_in, below_in, above_in, fold_in, column_in, own_column, t_out, s_out,
    t_new, s_new, sems,
):
    shape = (levels, LANES)
    level = iota(shape, 0).astype(F32)
    lane = iota(shape, 1)
    place = lane % 4
    factors = level_factors(levels)
    K = levels
    row_at = lax.axis_index("lat")
    is_top, is_bottom = row_at == lat_size - 1, row_at == 0
    is_odd = lax.axis_index("lon") % 2 == 1

    def faces(cells, speeds):
        wets = [level < jnp.minimum(a["n"], b["n"]) for a, b in zip(cells, cells[1:])]
        d = [[face_step(a, b, w, q) for q in "ts"] for a, b, w in zip(cells, cells[1:], wets)]
        limited = [[minmod(x, y) for x, y in zip(d[i], d[i + 1])] for i in (0, 1)]
        base, wg, forward = face_base(cells[1], cells[2], speeds[1], wets[1], d[1])
        flux = [b + wg * jnp.where(forward, x, y) for b, x, y in zip(base, *limited)]
        first = last = None
        if speeds[0] is not None:
            _, wg0 = weights(speeds[0], wets[0])
            first = [wg0 * jnp.where(speeds[0] > 0.0, 0.0, x) for x in limited[0]]
        if speeds[2] is not None:
            _, wg2 = weights(speeds[2], wets[2])
            last = [wg2 * jnp.where(speeds[2] > 0.0, x, 0.0) for x in limited[1]]
        return first, flux, last

    def cell_row(t, s, n):
        return column_row(t, s, n, factors, iota(shape, 0))

    own, core, inter = side_ref[...], core_in[...], inter_in[...]
    west, east = jnp.where(is_odd, core, inter), jnp.where(is_odd, inter, core)

    def side(left, right):
        both = jnp.where(iota(left.shape, 1) % 4 < 2, left, right)
        row = cell_row(both[:K], both[K : 2 * K], both[3 * K : 3 * K + 1])
        cells = [row] + [shifted(row, -i) for i in (1, 2, 3)]
        speed = both[2 * K : 3 * K]
        return faces(cells, [roll(speed, -i) for i in range(3)])

    _, west_flux, west_last = side(west, own)
    east_first, east_flux, _ = side(own, east)
    lon = []
    for fw, lw, fe, le in zip(west_flux, west_last, east_flux, east_first):
        group = jnp.where(
            place == 0,
            -le,
            jnp.where(place == 1, roll(le - fe, 1), jnp.where(place == 2, roll(fw - lw, 2), roll(lw, 3))),
        )
        lon.append(group)

    counts = n_ref[...].astype(F32)

    def own_row(j):
        return cell_row(t_ref[j], s_ref[j], counts[j : j + 1])

    def sent_row(array, which, at_counts):
        t, s = array[which * K : (which + 1) * K], array[(2 + which) * K : (3 + which) * K]
        return cell_row(t, s, array[at_counts + which : at_counts + which + 1])

    below = jnp.where(is_bottom, 0.0, below_in[...])
    cells = [sent_row(below, 0, 5 * K), sent_row(below, 1, 5 * K), own_row(0), own_row(1)]
    _, south_flux, south_last = faces(cells, [None, below[4 * K : 5 * K], own_ref[:K]])

    pivot = (lax.axis_index("lon") * 2) % lon_size == 0
    column = jnp.where(pivot, own_column[...], column_in[...])
    parts = [roll(column[:K], -i) for i in range(4)] + [column[K : K + 8]]
    fold = fold_in[...]
    fold = jnp.where(iota(fold.shape, 1) == 0, jnp.concatenate(parts, axis=0), fold)
    above = above_in[...]
    above = jnp.where(is_top, fold, jnp.concatenate([above[: 4 * K], above[5 * K :]], axis=0))
    cells = [own_row(rows - 2), own_row(rows - 1), sent_row(above, 0, 4 * K), sent_row(above, 1, 4 * K)]
    north_first, north_flux, _ = faces(cells, [own_ref[K : 2 * K], own_ref[2 * K :], None])

    edge_lanes = (lane >= LANES - 2) | (lane < 2)

    copies = []
    for q, (p_ref, new_ref, out_ref) in enumerate(((pt_ref, t_new, t_out), (ps_ref, s_new, s_out))):

        extra = {
            0: south_flux[q] - south_last[q],
            1: south_last[q],
            rows - 2: -north_first[q],
            rows - 1: north_first[q] - north_flux[q],
        }
        for j in range(rows):
            value = p_ref[j + 2] + jnp.where(edge_lanes, roll(lon[q], LANES - 2 - 4 * j), 0.0)
            put(new_ref, j, value + extra[j] if j in extra else value)
        copies.append(pltpu.make_async_copy(new_ref, out_ref, sems.at[q]))
        copies[q].start()
    for copy in copies:
        copy.wait()


def body(nlat, nlon, t, s, c, m, n):
    levels, rows, _ = t.shape
    vmem, hbm = pl.BlockSpec(memory_space=pltpu.VMEM), pl.BlockSpec(memory_space=pltpu.HBM)
    f = functools.partial
    out = lambda *shape: jax.ShapeDtypeStruct(shape, F32)
    K = levels
    params = pltpu.CompilerParams(vmem_limit_bytes=VMEM)
    swap = nlat == 2
    field, lat_shape = out(rows, K, LANES), out(5 * K + 8, LANES)
    shapes = [field] * 3 + [out(*m.shape), jax.ShapeDtypeStruct(n.shape, n.dtype)]
    shapes += [out(3 * K + 8, LANES), lat_shape, out(4 * K + 8, LANES), out(5 * K, LANES), out(3 * K, LANES)]
    shapes += [] if swap else [lat_shape]
    t_v, s_v, c_v, m_v, n_v, side, lat, fold, column, own, *more = pl.pallas_call(
        f(pack_kernel, levels, rows, nlat),
        out_shape=tuple(shapes),
        in_specs=[hbm] * 5,
        out_specs=(vmem,) * len(shapes),
        scratch_shapes=[pltpu.VMEM(t.shape, F32)] * 3 + [pltpu.SemaphoreType.DMA((5,))],
        compiler_params=params,
        name="pack",
    )(*[pltpu.with_memory_space_constraint(x, pltpu.HBM) for x in (t, s, c, m, n)])

    def across(array, partner):
        to = {(j, i): (j, i ^ 1 if i ^ 1 < nlon else i) for j in range(nlat - 1) for i in range(nlon)}
        top = nlat - 1
        for i in range(nlon):
            to[top, i] = (top, partner(i) % nlon)
        for i in range(nlon):
            if to[top, i] == (top, i) and to.get((0, i), (0, i)) != (0, i):
                other = to[0, i]
                to[top, i], to[0, i], to[other] = (0, i), other, (top, i)
        pairs = [(i * nlat + j, to[j, i][1] * nlat + to[j, i][0]) for i in range(nlon) for j in range(nlat)]
        return lax.ppermute(array, ("lon", "lat"), pairs)

    ring, rung = range(nlon), range(nlat)
    core_in = lax.ppermute(side, "lon", [(i, i ^ 1) for i in ring])
    inter_in = lax.ppermute(side, "lon", [(i, (i + (1 if i % 2 else -1)) % nlon) for i in ring])
    below_in = above_in = lax.ppermute(lat, "lat", [(i, (i + 1) % nlat) for i in rung])
    if not swap:
        above_in = lax.ppermute(more[0], "lat", [(i, (i - 1) % nlat) for i in rung])
    fold_in = across(fold, lambda i: nlon - 1 - i)
    column_in = across(column, lambda i: nlon - i)

    pt, ps = pl.pallas_call(
        f(interior_kernel, levels, rows),
        out_shape=(out(rows + 2, K, LANES),) * 2,
        in_specs=[vmem] * 5,
        out_specs=(vmem,) * 2,
        cost_estimate=pl.CostEstimate(flops=40_000_000, bytes_accessed=2_000_000, transcendentals=0),
        compiler_params=params,
        name="interior",
    )(t_v, s_v, c_v, m_v, n_v)

    return pl.pallas_call(
        f(edge_kernel, levels, rows, nlat, nlon),
        out_shape=(out(*t.shape),) * 2,
        in_specs=[vmem] * 14,
        out_specs=(hbm,) * 2,
        scratch_shapes=[pltpu.VMEM(t.shape, F32)] * 2 + [pltpu.SemaphoreType.DMA((2,))],
        compiler_params=params,
        name="edge",
    )(pt, ps, side, t_v, s_v, n_v, own, core_in, inter_in, below_in, above_in, fold_in, column_in, column)


def solution(mesh):
    spec = P(None, "lat", "lon")
    return jax.shard_map(
        functools.partial(body, mesh.shape["lat"], mesh.shape["lon"]),
        mesh=mesh,
        in_specs=(spec,) * 4 + (P("lat", "lon"),),
        out_specs=(spec,) * 2,
        check_vma=False,
    )
```

time: 25.2 us -> 14.7 us (0.58)
  the two profiles are of different devices: /device:TPU:0 before, /device:TPU:5 now
where the time goes in v2:
time: 14.7 us; the launch traced here: 14.6 us
  starting transfers between devices  7.2 us (49%)
  Pallas kernels  5 us (34%)
  waiting for transfers between devices  1.72 us (12%)
  between operations  0.67 us (5%)
    ppermute x2, starting transfers between devices, across(): return lax.ppermute(array, ('lon', 'lat'), pairs)  5.52 us
    pallas_call x1, Pallas kernels, body(): pl.pallas_call(f(pack_kernel, levels, rows, nlat), out_shape=tuple(shapes...  1.82 us
    ppermute x2, waiting for transfers between devices, across(): return lax.ppermute(array, ('lon', 'lat'), pairs)  1.72 us
    pallas_call x1, Pallas kernels, body(): pl.pallas_call(f(interior_kernel, levels, rows), out_shape=(out(rows + 2,...  1.72 us
    pallas_call x1, Pallas kernels, body(): pl.pallas_call(f(edge_kernel, levels, rows, nlat, nlon), out_shape=(out(*...  1.47 us
    ppermute x1, starting transfers between devices, body(): core_in = lax.ppermute(side, 'lon', [(i, i ^ 1) for i in ring])  1.26 us
    ppermute x1, starting transfers between devices, body(): lax.ppermute(side, 'lon', [(i, (i + (1 if i % 2 else -1)) % nlon) for i i...  0.34 us
  transfers between devices with their start and end apart: 5, of which 1 were waited for; matrix products, arithmetic and copies ran while one was open for 0% of the time, Pallas kernels for 12%

profile of v2, /device:TPU:5, one launch (start us, length us, event | category | flops | bytes accessed | tf_op | source)
XLA Modules:
  0.0 14.6 jit_solution(4101877367694385715)
XLA Ops:
  0.6 1.8 %pack.1 = (f32[32,16,128]{2,1,0:T(8,128)S(1)}, f32[32,16,128]{2,1,0:T(8,128)S(1)}, f32[32,16,128]{2,1,0:T(8,128)S(1)}, f32[16,32,128]{2,1,0:T(8,128)S(1)}, s32[3...) custom-call(f32[16,32,128]{2,1,0:T(8,128)} %t_hbm.1, ...), custom_call_target="tpu_custom_call" | custom-call | tf_op jit(solution)/shard_map/pack/pallas_call | solution.py:351
  2.5 0.1 collective-permute-start.2
  2.5 4.5 %collective-permute-start.4 = (f32[80,128]{1,0:T(8,128)S(1)}, f32[80,128]{1,0:T(8,128)S(1)}, u32[]{:S(2)}, u32[]{:S(2)}) collective-permute-start(f32[80,128]{1,0:T(8,128)S(1)} %get-tuple-element.25.own_column), channel_id=1, source_target_pairs={{0,2},{1,0},{2,1},{3,31},{4,6},{5,29},{6,4},{7,27},{8,10},{9,25},{... | collective-permute-start | bytes 122888 | tf_op jit(solution)/shard_map/ppermute | solution.py:371
  7.0 1.1 %collective-permute-start.3 = (f32[72,128]{1,0:T(8,128)S(1)}, f32[72,128]{1,0:T(8,128)S(1)}, u32[]{:S(2)}, u32[]{:S(2)}) collective-permute-start(f32[72,128]{1,0:T(8,128)S(1)} %get-tuple-element.24), channel_id=1, source_target_pairs={{0,2},{1,31},{2,0},{3,29},{4,6},{5,27},{6,4},{7,25},{8,10},{9,23},... | collective-permute-start | bytes 110600 | tf_op jit(solution)/shard_map/ppermute | solution.py:371
  8.1 0.3 %collective-permute-start.1 = (f32[56,128]{1,0:T(8,128)S(1)}, f32[56,128]{1,0:T(8,128)S(1)}, u32[]{:S(2)}, u32[]{:S(2)}) collective-permute-start(f32[56,128]{1,0:T(8,128)S(1)} %get-tuple-element.21.side_ref), channel_id=1, source_target_pairs={{0,30},{2,4},{4,2},{6,8},{8,6},{10,12},{12,10},{14,16},{16,14},{18... | collective-permute-start | bytes 86024 | tf_op jit(solution)/shard_map/ppermute | solution.py:375
  8.4 1.3 %collective-permute-start = (f32[56,128]{1,0:T(8,128)S(1)}, f32[56,128]{1,0:T(8,128)S(1)}, u32[]{:S(2)}, u32[]{:S(2)}) collective-permute-start(f32[56,128]{1,0:T(8,128)S(1)} %get-tuple-element.21.side_ref), channel_id=1, source_target_pairs={{0,2},{2,0},{4,6},{6,4},{8,10},{10,8},{12,14},{14,12},{16,18},{18,... | collective-permute-start | bytes 86024 | tf_op jit(solution)/shard_map/ppermute | solution.py:374
  9.7 1.7 %interior.1 = (f32[34,16,128]{2,1,0:T(8,128)S(1)}, f32[34,16,128]{2,1,0:T(8,128)S(1)}) custom-call(f32[32,16,128]{2,1,0:T(8,128)S(1)} %get-tuple-element.14.t_ref, f32[32,16,128]{2,1,0:T(8,128)S(1)} %get-tuple-element.15.s_ref, f32[32,16,128]{2,1,0:T(8,128)S(1)} %get-tuple-element.16.c_ref, f32[16,32,128]{2,1,0:T(8,128)S(1)} %get-tuple-element.17.m_ref, ...), custom_call_target="tpu_custom_call" | custom-call | flops 40000000 | bytes 2000000 | tf_op jit(solution)/shard_map/interior/pallas_call | solution.py:382
  11.4 0.0 collective-permute-done.1.inter_in
  11.4 0.0 collective-permute-done.core_in
  11.4 1.7 %collective-permute-done.3.fold_in = f32[72,128]{1,0:T(8,128)S(1)} collective-permute-done((f32[72,128]{1,0:T(8,128)S(1)}, f32[72,128]{1,0:T(8,128)S(1)}, u32[]{:S(2)}, u32[]{:S(2)}) %collective-permute-start.3) | collective-permute-done | bytes 36896 | tf_op jit(solution)/shard_map/ppermute | solution.py:371
  13.1 0.0 collective-permute-done.4.column_in
  13.1 0.0 collective-permute-done.2.below_in.above_in
  13.1 1.5 %edge.1 = (f32[16,32,128]{2,1,0:T(8,128)}, f32[16,32,128]{2,1,0:T(8,128)}) custom-call(f32[34,16,128]{2,1,0:T(8,128)S(1)} %get-tuple-element.19.pt_ref, f32[34,16,128]{2,1,0:T(8,128)S(1)} %get-tuple-element.20.ps_ref, f32[56,128]{1,0:T(8,128)S(1)} %get-tuple-element.21.side_ref, f32[32,16,128]{2,1,0:T(8,128)S(1)} %get-tuple-element.14.t_ref, ...), custom_call_target="tpu_custom_call" | custom-call | tf_op jit(solution)/shard_map/edge/pallas_call | solution.py:392
Async XLA Ops:
  2.5 10.7 %collective-permute-start.2 = (f32[88,128]{1,0:T(8,128)S(1)}, f32[88,128]{1,0:T(8,128)S(1)}, u32[]{:S(2)}, u32[]{:S(2)}) collective-permute-start(f32[88,128]{1,0:T(8,128)S(1)} %get-tuple-element.23), channel_id=1, source_target_pairs={{0,1},{1,0},{2,3},{3,2},{4,5},{5,4},{6,7},{7,6},{8,9},{9,8},{10,11... | collective-permute-start | bytes 135176 | tf_op jit(solution)/shard_map/ppermute | solution.py:376
  2.5 10.6 %collective-permute-start.4 = (f32[80,128]{1,0:T(8,128)S(1)}, f32[80,128]{1,0:T(8,128)S(1)}, u32[]{:S(2)}, u32[]{:S(2)}) collective-permute-start(f32[80,128]{1,0:T(8,128)S(1)} %get-tuple-element.25.own_column), channel_id=1, source_target_pairs={{0,2},{1,0},{2,1},{3,31},{4,6},{5,29},{6,4},{7,27},{8,10},{9,25},{... | collective-permute-start | bytes 122888 | tf_op jit(solution)/shard_map/ppermute | solution.py:371
  7.0 6.1 %collective-permute-start.3 = (f32[72,128]{1,0:T(8,128)S(1)}, f32[72,128]{1,0:T(8,128)S(1)}, u32[]{:S(2)}, u32[]{:S(2)}) collective-permute-start(f32[72,128]{1,0:T(8,128)S(1)} %get-tuple-element.24), channel_id=1, source_target_pairs={{0,2},{1,31},{2,0},{3,29},{4,6},{5,27},{6,4},{7,25},{8,10},{9,23},... | collective-permute-start | bytes 110600 | tf_op jit(solution)/shard_map/ppermute | solution.py:371
  8.1 3.3 %collective-permute-start.1 = (f32[56,128]{1,0:T(8,128)S(1)}, f32[56,128]{1,0:T(8,128)S(1)}, u32[]{:S(2)}, u32[]{:S(2)}) collective-permute-start(f32[56,128]{1,0:T(8,128)S(1)} %get-tuple-element.21.side_ref), channel_id=1, source_target_pairs={{0,30},{2,4},{4,2},{6,8},{8,6},{10,12},{12,10},{14,16},{16,14},{18... | collective-permute-start | bytes 86024 | tf_op jit(solution)/shard_map/ppermute | solution.py:375
  8.4 3.0 %collective-permute-start = (f32[56,128]{1,0:T(8,128)S(1)}, f32[56,128]{1,0:T(8,128)S(1)}, u32[]{:S(2)}, u32[]{:S(2)}) collective-permute-start(f32[56,128]{1,0:T(8,128)S(1)} %get-tuple-element.21.side_ref), channel_id=1, source_target_pairs={{0,2},{2,0},{4,6},{6,4},{8,10},{10,8},{12,14},{14,12},{16,18},{18,... | collective-permute-start | bytes 86024 | tf_op jit(solution)/shard_map/ppermute | solution.py:374

commit v3 on v2

--- a/solution.py
+++ b/solution.py
@@ -112,22 +112,33 @@
     levels, rows, lat_size, t_hbm, s_hbm, c_hbm, m_hbm, n_hbm,
     t_ref, s_ref, c_ref, m_ref, n_ref, side_ref, lat_ref, fold_ref, column_ref, own_ref, *more,
 ):
-    *more, t_in, s_in, c_in, sems = more
+    *more, sems = more
     K = levels
-    pairs = ((t_hbm, t_in), (s_hbm, s_in), (c_hbm, c_in), (n_hbm, n_ref), (m_hbm, m_ref))
+    pairs = ((t_hbm, t_ref), (s_hbm, s_ref), (c_hbm, c_ref), (n_hbm, n_ref), (m_hbm, m_ref))
     copies = [pltpu.make_async_copy(src, dst, sems.at[i]) for i, (src, dst) in enumerate(pairs)]
     for copy in copies:
         copy.start()
     lane = iota((levels, LANES), 1)
     group = lane // 4
 
-    def gather(ref, rows_ref):
-        out = jnp.zeros((levels, LANES), F32)
-        for j in range(rows):
-            row = strided(ref, j)
-            rows_ref[j] = row
-            out = jnp.where(group == j, roll(row, 4 * j + 2), out)
-        return out
+    slot = iota((8, LANES), 0)
+    own = [iota((8, LANES), 1) // 4 == slot + 8 * block for block in range(rows // 8)]
+
+    def gather(ref):
+        tiles = []
+        for base in range(0, K, 8):
+            out = jnp.zeros((8, LANES), F32)
+            for k in range(8):
+                spread = jnp.zeros((8, LANES), F32)
+                for block, mine in enumerate(own):
+                    eight = ref[base + k, 8 * block : 8 * block + 8, :]
+                    moved = pltpu.roll(eight, 32 * block + 2, 1, stride=4, stride_axis=0)
+                    spread = jnp.where(mine, moved, spread)
+                for by in (4, 2, 1):
+                    spread = spread + roll(spread, by, 0)
+                out = jnp.where(slot == k, spread, out)
+            tiles.append(out)
+        return jnp.concatenate(tiles, axis=0)
 
     def mirrored(x):
         index = (LANES - iota(x.shape, 1)) % LANES
@@ -136,13 +147,13 @@
     def tracer_rows(out_ref, tracer, ref, picks, change=lambda x: x):
         for i, j in enumerate(picks):
             at = (2 * tracer + i) * K
-            out_ref[at : at + K, :] = change(ref[j])
+            out_ref[at : at + K, :] = change(strided(ref, j))
 
     south, north, fold = (0, 1), (rows - 2, rows - 1), (rows - 2, rows - 3)
     is_top = lax.axis_index("lat") == lat_size - 1
-    for tracer, (ref, source) in enumerate(((t_ref, t_in), (s_ref, s_in))):
+    for tracer, ref in enumerate((t_ref, s_ref)):
         copies[tracer].wait()
-        side_ref[tracer * K : (tracer + 1) * K, :] = gather(source, ref)
+        side_ref[tracer * K : (tracer + 1) * K, :] = gather(ref)
         tracer_rows(fold_ref, tracer, ref, fold, mirrored)
         if more:
             tracer_rows(lat_ref, tracer, ref, north)
@@ -150,10 +161,10 @@
         else:
             for i in range(2):
                 at = (2 * tracer + i) * K
-                lat_ref[at : at + K, :] = jnp.where(is_top, ref[south[i]], ref[north[i]])
+                lat_ref[at : at + K, :] = jnp.where(is_top, strided(ref, south[i]), strided(ref, north[i]))
 
     copies[2].wait()
-    side_ref[2 * K : 3 * K, :] = gather(c_in, c_ref)
+    side_ref[2 * K : 3 * K, :] = gather(c_ref)
     copies[3].wait()
     counts = n_ref[...].astype(F32)
     moved = jnp.concatenate([roll(counts[j : j + 1], 4 * j + 2) for j in range(rows)], axis=0)
@@ -170,7 +181,7 @@
     fold_ref[4 * K :, :] = mirrored(tally(fold))
     first = jnp.zeros((levels, LANES), F32)
     for i, (ref, j) in enumerate((ref, j) for ref in (t_ref, s_ref) for j in fold):
-        first = jnp.where(lane == i, roll(ref[j], i), first)
+        first = jnp.where(lane == i, roll(strided(ref, j), i), first)
     column_ref[:K, :] = first
     column_ref[K : K + 8, :] = tally(fold)
     if more:
@@ -197,7 +208,7 @@
 
     def step(j, carry):
         prev, m1, d2, limited2, base2, wg2, m2, acc2, acc1 = carry
-        t, s, c, m = t_ref[j], s_ref[j], c_ref[j], strided(m_ref, j)
+        t, s, c, m = (strided(ref, j) for ref in (t_ref, s_ref, c_ref, m_ref))
         n = n_ref[pl.ds(j, 1), :]
         here = column_row(t, s, n, factors, level)
         east = shifted(here, -1)
@@ -218,8 +229,9 @@
         flux2 = [b + wg2 * jnp.where(forward2, x, y) for b, x, y in zip(base2, limited2, limited1)]
         done = [x - f for x, f in zip(acc2, flux2)]
         acc1 = [x + f for x, f in zip(acc1, flux2)]
-        pt_ref[pl.ds(j, 1)] = done[0][None]
-        ps_ref[pl.ds(j, 1)] = done[1][None]
+        at = (j + rows - 2) % rows
+        put(pt_ref, at, done[0])
+        put(ps_ref, at, done[1])
         return here, m, d1, limited1, base1, wg1, m1, acc1, acc
 
     nothing = [zero, zero]
@@ -235,8 +247,8 @@
     _, _, _, limited2, base2, wg2, m2, acc2, acc1 = carry
     flux2 = [b + wg2 * jnp.where(m2 > 0.0, x, 0.0) for b, x in zip(base2, limited2)]
     for ref, a2, a1, f in zip((pt_ref, ps_ref), acc2, acc1, flux2):
-        ref[rows] = a2 - f
-        ref[rows + 1] = a1 + f
+        put(ref, rows - 2, a2 - f)
+        put(ref, rows - 1, a1 + f)
 
 
 def edge_kernel(
@@ -296,7 +308,7 @@
     counts = n_ref[...].astype(F32)
 
     def own_row(j):
-        return cell_row(t_ref[j], s_ref[j], counts[j : j + 1])
+        return cell_row(strided(t_ref, j), strided(s_ref, j), counts[j : j + 1])
 
     def sent_row(array, which, at_counts):
         t, s = array[which * K : (which + 1) * K], array[(2 + which) * K : (3 + which) * K]
@@ -316,20 +328,27 @@
     cells = [own_row(rows - 2), own_row(rows - 1), sent_row(above, 0, 4 * K), sent_row(above, 1, 4 * K)]
     north_first, north_flux, _ = faces(cells, [own_ref[K : 2 * K], own_ref[2 * K :], None])
 
-    edge_lanes = (lane >= LANES - 2) | (lane < 2)
-
+    slot = iota((8, LANES), 0)
+    last = LANES // 4 - 1
+    own_lanes = [last - iota((8, LANES), 1) // 4 == slot + 8 * block for block in range(rows // 8)]
+    reverse = 4 * (last - lane // 4) + place
     copies = []
     for q, (p_ref, new_ref, out_ref) in enumerate(((pt_ref, t_new, t_out), (ps_ref, s_new, s_out))):
-
+        sides = jnp.take_along_axis(lon[q], reverse, axis=1)
+        for k in range(levels):
+            line = jnp.broadcast_to(sides[k : k + 1], (8, LANES))
+            for block, mine in enumerate(own_lanes):
+                moved = pltpu.roll(jnp.where(mine, line, 0.0), 32 * block + 2, 1, stride=4, stride_axis=0)
+                at = slice(8 * block, 8 * block + 8)
+                new_ref[k, at, :] = p_ref[k, at, :] + moved
         extra = {
             0: south_flux[q] - south_last[q],
             1: south_last[q],
             rows - 2: -north_first[q],
             rows - 1: north_first[q] - north_flux[q],
         }
-        for j in range(rows):
-            value = p_ref[j + 2] + jnp.where(edge_lanes, roll(lon[q], LANES - 2 - 4 * j), 0.0)
-            put(new_ref, j, value + extra[j] if j in extra else value)
+        for j, value in extra.items():
+            put(new_ref, j, strided(new_ref, j) + value)
         copies.append(pltpu.make_async_copy(new_ref, out_ref, sems.at[q]))
         copies[q].start()
     for copy in copies:
@@ -345,7 +364,7 @@
     params = pltpu.CompilerParams(vmem_limit_bytes=VMEM)
     swap = nlat == 2
     field, lat_shape = out(rows, K, LANES), out(5 * K + 8, LANES)
-    shapes = [field] * 3 + [out(*m.shape), jax.ShapeDtypeStruct(n.shape, n.dtype)]
+    shapes = [out(*t.shape)] * 4 + [jax.ShapeDtypeStruct(n.shape, n.dtype)]
     shapes += [out(3 * K + 8, LANES), lat_shape, out(4 * K + 8, LANES), out(5 * K, LANES), out(3 * K, LANES)]
     shapes += [] if swap else [lat_shape]
     t_v, s_v, c_v, m_v, n_v, side, lat, fold, column, own, *more = pl.pallas_call(
@@ -353,7 +372,7 @@
         out_shape=tuple(shapes),
         in_specs=[hbm] * 5,
         out_specs=(vmem,) * len(shapes),
-        scratch_shapes=[pltpu.VMEM(t.shape, F32)] * 3 + [pltpu.SemaphoreType.DMA((5,))],
+        scratch_shapes=[pltpu.SemaphoreType.DMA((5,))],
         compiler_params=params,
         name="pack",
     )(*[pltpu.with_memory_space_constraint(x, pltpu.HBM) for x in (t, s, c, m, n)])
@@ -381,7 +400,7 @@
 
     pt, ps = pl.pallas_call(
         f(interior_kernel, levels, rows),
-        out_shape=(out(rows + 2, K, LANES),) * 2,
+        out_shape=(out(*t.shape),) * 2,
         in_specs=[vmem] * 5,
         out_specs=(vmem,) * 2,
         cost_estimate=pl.CostEstimate(flops=40_000_000, bytes_accessed=2_000_000, transcendentals=0),

time: 14.7 us -> 14.3 us (0.973)
  waiting for transfers between devices: 1.72 us -> 1.22 us
    pallas_call x1, Pallas kernels: 1.72 us -> 2.22 us  [body(): pl.pallas_call(f(interior_kernel, levels, rows), out_shape=(out(*t.shape)...]
    ppermute x2, waiting for transfers between devices: 1.72 us -> 1.21 us  [across(): return lax.ppermute(array, ('lon', 'lat'), pairs)]
    pallas_call x1, Pallas kernels: 1.82 us -> 1.59 us  [body(): pl.pallas_call(f(pack_kernel, levels, rows, nlat), out_shape=tuple(shapes...]
    pallas_call x1, Pallas kernels: 1.47 us -> 1.28 us  [body(): pl.pallas_call(f(edge_kernel, levels, rows, nlat, nlon), out_shape=(out(*...]
  transfers between devices with their start and end apart: 5 -> 5, of which waited for: 1 -> 1; matrix products, arithmetic and copies ran while one was open for 0% -> 0% of each run, Pallas kernels for 12% -> 16%
where the time goes in v3:
time: 14.3 us; the launch traced here: 14.2 us
  starting transfers between devices  7.2 us (50%)
  Pallas kernels  5.09 us (36%)
  waiting for transfers between devices  1.22 us (9%)
  between operations  0.67 us (5%)
    ppermute x2, starting transfers between devices, across(): return lax.ppermute(array, ('lon', 'lat'), pairs)  5.52 us
    pallas_call x1, Pallas kernels, body(): pl.pallas_call(f(interior_kernel, levels, rows), out_shape=(out(*t.shape)...  2.22 us
    pallas_call x1, Pallas kernels, body(): pl.pallas_call(f(pack_kernel, levels, rows, nlat), out_shape=tuple(shapes...  1.59 us
    pallas_call x1, Pallas kernels, body(): pl.pallas_call(f(edge_kernel, levels, rows, nlat, nlon), out_shape=(out(*...  1.28 us
    ppermute x1, starting transfers between devices, body(): core_in = lax.ppermute(side, 'lon', [(i, i ^ 1) for i in ring])  1.26 us
    ppermute x2, waiting for transfers between devices, across(): return lax.ppermute(array, ('lon', 'lat'), pairs)  1.21 us
    ppermute x1, starting transfers between devices, body(): lax.ppermute(side, 'lon', [(i, (i + (1 if i % 2 else -1)) % nlon) for i i...  0.34 us
  transfers between devices with their start and end apart: 5, of which 1 were waited for; matrix products, arithmetic and copies ran while one was open for 0% of the time, Pallas kernels for 16%

profile of v3, /device:TPU:5, one launch (start us, length us, event | category | flops | bytes accessed | tf_op | source)
XLA Modules:
  0.0 14.2 jit_solution(8344278011572818707)
XLA Ops:
  0.6 1.6 %pack.1 = (f32[16,32,128]{2,1,0:T(8,128)S(1)}, f32[16,32,128]{2,1,0:T(8,128)S(1)}, f32[16,32,128]{2,1,0:T(8,128)S(1)}, f32[16,32,128]{2,1,0:T(8,128)S(1)}, s32[3...) custom-call(f32[16,32,128]{2,1,0:T(8,128)} %t_hbm.1, ...), custom_call_target="tpu_custom_call" | custom-call | tf_op jit(solution)/shard_map/pack/pallas_call | solution.py:370
  2.2 0.1 collective-permute-start.2
  2.3 4.5 %collective-permute-start.4 = (f32[80,128]{1,0:T(8,128)S(1)}, f32[80,128]{1,0:T(8,128)S(1)}, u32[]{:S(2)}, u32[]{:S(2)}) collective-permute-start(f32[80,128]{1,0:T(8,128)S(1)} %get-tuple-element.25.own_column), channel_id=1, source_target_pairs={{0,2},{1,0},{2,1},{3,31},{4,6},{5,29},{6,4},{7,27},{8,10},{9,25},{... | collective-permute-start | bytes 122888 | tf_op jit(solution)/shard_map/ppermute | solution.py:390
  6.8 1.1 %collective-permute-start.3 = (f32[72,128]{1,0:T(8,128)S(1)}, f32[72,128]{1,0:T(8,128)S(1)}, u32[]{:S(2)}, u32[]{:S(2)}) collective-permute-start(f32[72,128]{1,0:T(8,128)S(1)} %get-tuple-element.24), channel_id=1, source_target_pairs={{0,2},{1,31},{2,0},{3,29},{4,6},{5,27},{6,4},{7,25},{8,10},{9,23},... | collective-permute-start | bytes 110600 | tf_op jit(solution)/shard_map/ppermute | solution.py:390
  7.8 0.3 %collective-permute-start.1 = (f32[56,128]{1,0:T(8,128)S(1)}, f32[56,128]{1,0:T(8,128)S(1)}, u32[]{:S(2)}, u32[]{:S(2)}) collective-permute-start(f32[56,128]{1,0:T(8,128)S(1)} %get-tuple-element.21.side_ref), channel_id=1, source_target_pairs={{0,30},{2,4},{4,2},{6,8},{8,6},{10,12},{12,10},{14,16},{16,14},{18... | collective-permute-start | bytes 86024 | tf_op jit(solution)/shard_map/ppermute | solution.py:394
  8.2 1.3 %collective-permute-start = (f32[56,128]{1,0:T(8,128)S(1)}, f32[56,128]{1,0:T(8,128)S(1)}, u32[]{:S(2)}, u32[]{:S(2)}) collective-permute-start(f32[56,128]{1,0:T(8,128)S(1)} %get-tuple-element.21.side_ref), channel_id=1, source_target_pairs={{0,2},{2,0},{4,6},{6,4},{8,10},{10,8},{12,14},{14,12},{16,18},{18,... | collective-permute-start | bytes 86024 | tf_op jit(solution)/shard_map/ppermute | solution.py:393
  9.4 2.2 %interior.1 = (f32[16,32,128]{2,1,0:T(8,128)S(1)}, f32[16,32,128]{2,1,0:T(8,128)S(1)}) custom-call(f32[16,32,128]{2,1,0:T(8,128)S(1)} %get-tuple-element.14.t_ref, f32[16,32,128]{2,1,0:T(8,128)S(1)} %get-tuple-element.15.s_ref, f32[16,32,128]{2,1,0:T(8,128)S(1)} %get-tuple-element.16.c_ref, f32[16,32,128]{2,1,0:T(8,128)S(1)} %get-tuple-element.17.m_ref, ...), custom_call_target="tpu_custom_call" | custom-call | flops 40000000 | bytes 2000000 | tf_op jit(solution)/shard_map/interior/pallas_call | solution.py:401
  11.7 0.0 collective-permute-done.1.inter_in
  11.7 0.0 collective-permute-done.core_in
  11.7 1.2 %collective-permute-done.3.fold_in = f32[72,128]{1,0:T(8,128)S(1)} collective-permute-done((f32[72,128]{1,0:T(8,128)S(1)}, f32[72,128]{1,0:T(8,128)S(1)}, u32[]{:S(2)}, u32[]{:S(2)}) %collective-permute-start.3) | collective-permute-done | bytes 36896 | tf_op jit(solution)/shard_map/ppermute | solution.py:390
  12.9 0.0 collective-permute-done.4.column_in
  12.9 0.0 collective-permute-done.2.below_in.above_in
  12.9 1.3 %edge.1 = (f32[16,32,128]{2,1,0:T(8,128)}, f32[16,32,128]{2,1,0:T(8,128)}) custom-call(f32[16,32,128]{2,1,0:T(8,128)S(1)} %get-tuple-element.19.pt_ref, f32[16,32,128]{2,1,0:T(8,128)S(1)} %get-tuple-element.20.ps_ref, f32[56,128]{1,0:T(8,128)S(1)} %get-tuple-element.21.side_ref, f32[16,32,128]{2,1,0:T(8,128)S(1)} %get-tuple-element.14.t_ref, ...), custom_call_target="tpu_custom_call" | custom-call | tf_op jit(solution)/shard_map/edge/pallas_call | solution.py:411
Async XLA Ops:
  2.2 10.7 %collective-permute-start.2 = (f32[88,128]{1,0:T(8,128)S(1)}, f32[88,128]{1,0:T(8,128)S(1)}, u32[]{:S(2)}, u32[]{:S(2)}) collective-permute-start(f32[88,128]{1,0:T(8,128)S(1)} %get-tuple-element.23), channel_id=1, source_target_pairs={{0,1},{1,0},{2,3},{3,2},{4,5},{5,4},{6,7},{7,6},{8,9},{9,8},{10,11... | collective-permute-start | bytes 135176 | tf_op jit(solution)/shard_map/ppermute | solution.py:395
  2.3 10.6 %collective-permute-start.4 = (f32[80,128]{1,0:T(8,128)S(1)}, f32[80,128]{1,0:T(8,128)S(1)}, u32[]{:S(2)}, u32[]{:S(2)}) collective-permute-start(f32[80,128]{1,0:T(8,128)S(1)} %get-tuple-element.25.own_column), channel_id=1, source_target_pairs={{0,2},{1,0},{2,1},{3,31},{4,6},{5,29},{6,4},{7,27},{8,10},{9,25},{... | collective-permute-start | bytes 122888 | tf_op jit(solution)/shard_map/ppermute | solution.py:390
  6.8 6.1 %collective-permute-start.3 = (f32[72,128]{1,0:T(8,128)S(1)}, f32[72,128]{1,0:T(8,128)S(1)}, u32[]{:S(2)}, u32[]{:S(2)}) collective-permute-start(f32[72,128]{1,0:T(8,128)S(1)} %get-tuple-element.24), channel_id=1, source_target_pairs={{0,2},{1,31},{2,0},{3,29},{4,6},{5,27},{6,4},{7,25},{8,10},{9,23},... | collective-permute-start | bytes 110600 | tf_op jit(solution)/shard_map/ppermute | solution.py:390
  7.8 3.8 %collective-permute-start.1 = (f32[56,128]{1,0:T(8,128)S(1)}, f32[56,128]{1,0:T(8,128)S(1)}, u32[]{:S(2)}, u32[]{:S(2)}) collective-permute-start(f32[56,128]{1,0:T(8,128)S(1)} %get-tuple-element.21.side_ref), channel_id=1, source_target_pairs={{0,30},{2,4},{4,2},{6,8},{8,6},{10,12},{12,10},{14,16},{16,14},{18... | collective-permute-start | bytes 86024 | tf_op jit(solution)/shard_map/ppermute | solution.py:394
  8.2 3.5 %collective-permute-start = (f32[56,128]{1,0:T(8,128)S(1)}, f32[56,128]{1,0:T(8,128)S(1)}, u32[]{:S(2)}, u32[]{:S(2)}) collective-permute-start(f32[56,128]{1,0:T(8,128)S(1)} %get-tuple-element.21.side_ref), channel_id=1, source_target_pairs={{0,2},{2,0},{4,6},{6,4},{8,10},{10,8},{12,14},{14,12},{16,18},{18,... | collective-permute-start | bytes 86024 | tf_op jit(solution)/shard_map/ppermute | solution.py:393

commit v4 on v3

--- a/solution.py
+++ b/solution.py
@@ -21,6 +21,7 @@
 LANES = 128
 VMEM = 8 * 1024 * 1024
 UNROLL = 8
+HEAD = 8
 F32 = jnp.float32
 
 
@@ -110,7 +111,7 @@
 
 def pack_kernel(
     levels, rows, lat_size, t_hbm, s_hbm, c_hbm, m_hbm, n_hbm,
-    t_ref, s_ref, c_ref, m_ref, n_ref, side_ref, lat_ref, fold_ref, column_ref, own_ref, *more,
+    t_ref, s_ref, c_ref, m_ref, n_ref, side_ref, lat_ref, far_ref, column_ref, own_ref, *more,
 ):
     *more, sems = more
     K = levels
@@ -140,6 +141,11 @@
             tiles.append(out)
         return jnp.concatenate(tiles, axis=0)
 
+    def put_side(at, value):
+        size = value.shape[0]
+        side_ref[at : at + size, :] = value
+        far_ref[4 * K + 8 + at : 4 * K + 8 + at + size, :] = value
+
     def mirrored(x):
         index = (LANES - iota(x.shape, 1)) % LANES
         return jnp.take_along_axis(x, index, axis=1)
@@ -153,8 +159,8 @@
     is_top = lax.axis_index("lat") == lat_size - 1
     for tracer, ref in enumerate((t_ref, s_ref)):
         copies[tracer].wait()
-        side_ref[tracer * K : (tracer + 1) * K, :] = gather(ref)
-        tracer_rows(fold_ref, tracer, ref, fold, mirrored)
+        put_side(tracer * K, gather(ref))
+        tracer_rows(far_ref, tracer, ref, fold, mirrored)
         if more:
             tracer_rows(lat_ref, tracer, ref, north)
             tracer_rows(more[0], tracer, ref, south)
@@ -164,21 +170,21 @@
                 lat_ref[at : at + K, :] = jnp.where(is_top, strided(ref, south[i]), strided(ref, north[i]))
 
     copies[2].wait()
-    side_ref[2 * K : 3 * K, :] = gather(c_ref)
+    put_side(2 * K, gather(c_ref))
     copies[3].wait()
     counts = n_ref[...].astype(F32)
     moved = jnp.concatenate([roll(counts[j : j + 1], 4 * j + 2) for j in range(rows)], axis=0)
     line = jnp.sum(
         jnp.where(iota((rows, LANES), 1) // 4 == iota((rows, LANES), 0), moved, 0.0), axis=0, keepdims=True
     )
-    side_ref[3 * K :, :] = jnp.broadcast_to(line, (8, LANES))
+    put_side(3 * K, jnp.broadcast_to(line, (8, LANES)))
 
     def tally(picks):
         return jnp.concatenate(
             [counts[j : j + 1] for j in picks] + [jnp.zeros((8 - len(picks), LANES), F32)], axis=0
         )
 
-    fold_ref[4 * K :, :] = mirrored(tally(fold))
+    far_ref[4 * K : 4 * K + 8, :] = mirrored(tally(fold))
     first = jnp.zeros((levels, LANES), F32)
     for i, (ref, j) in enumerate((ref, j) for ref in (t_ref, s_ref) for j in fold):
         first = jnp.where(lane == i, roll(strided(ref, j), i), first)
@@ -196,10 +202,33 @@
         own_ref[i * K : (i + 1) * K, :] = strided(m_ref, j)
 
 
+def relay_kernel(far_ref, _, out_ref):
+    K = out_ref.shape[0] - 8
+    lane = iota((K, LANES), 1)
+    out = far_ref[:K, :]
+    for i in (1, 2, 3):
+        out = jnp.where(lane == i, roll(far_ref[i * K : (i + 1) * K, :], i), out)
+    out_ref[:K, :] = out
+    out_ref[K:, :] = far_ref[4 * K : 4 * K + 8, :]
+
+
 NAMES = ("t", "s", "r", "tz", "sz", "rz")
-
-
-def interior_kernel(levels, rows, t_ref, s_ref, c_ref, m_ref, n_ref, pt_ref, ps_ref):
+STATE = 19
+
+
+def south_kernel(levels, rows, last, lat_size, on_top, t_ref, s_ref, c_ref, m_ref, n_ref, *more):
+    pt_ref, ps_ref, state_out = more[3:6]
+
+    @pl.when((lax.axis_index("lat") == lat_size - 1) == on_top)
+    def _():
+        interior_kernel(levels, rows, 0, last, t_ref, s_ref, c_ref, m_ref, n_ref, pt_ref, ps_ref, state_out)
+
+
+def interior_kernel(levels, rows, first, last, t_ref, s_ref, c_ref, m_ref, n_ref, *more):
+    if first:
+        _, _, _, state_in, pt_ref, ps_ref = more
+    else:
+        pt_ref, ps_ref, state_out = more
     shape = (levels, LANES)
     level = iota(shape, 0)
     last_lane = iota((1, LANES), 1) == LANES - 1
@@ -234,16 +263,32 @@
         put(ps_ref, at, done[1])
         return here, m, d1, limited1, base1, wg1, m1, acc1, acc
 
-    nothing = [zero, zero]
-    start = dict({name: zero for name in NAMES}, n=jnp.zeros((1, LANES), jnp.int32))
-    carry = (start, zero, nothing, nothing, nothing, zero, zero, nothing, nothing)
+    def pack(carry):
+        prev, m1, d2, limited2, base2, wg2, m2, acc2, acc1 = carry
+        return [prev[name] for name in NAMES] + [m1, *d2, *limited2, *base2, wg2, m2, *acc2, *acc1]
+
+    def unpack(flat, n):
+        prev = dict(zip(NAMES, flat), n=n)
+        m1, d2, limited2, base2, wg2, m2, acc2, acc1 = (
+            flat[6], flat[7:9], flat[9:11], flat[11:13], flat[13], flat[14], flat[15:17], flat[17:19]
+        )
+        return prev, m1, d2, limited2, base2, wg2, m2, acc2, acc1
+
+    if first:
+        carry = unpack([state_in[i] for i in range(STATE)], n_ref[first - 1 : first, :])
+    else:
+        carry = unpack([zero] * STATE, jnp.zeros((1, LANES), jnp.int32))
 
     def block(i, carry):
         for u in range(UNROLL):
-            carry = step(i * UNROLL + u, carry)
+            carry = step(first + i * UNROLL + u, carry)
         return carry
 
-    carry = lax.fori_loop(0, rows // UNROLL, block, carry)
+    carry = lax.fori_loop(0, (last - first) // UNROLL, block, carry)
+    if last < rows:
+        for i, value in enumerate(pack(carry)):
+            state_out[i] = value
+        return
     _, _, _, limited2, base2, wg2, m2, acc2, acc1 = carry
     flux2 = [b + wg2 * jnp.where(m2 > 0.0, x, 0.0) for b, x in zip(base2, limited2)]
     for ref, a2, a1, f in zip((pt_ref, ps_ref), acc2, acc1, flux2):
@@ -253,7 +298,7 @@
 
 def edge_kernel(
     levels, rows, lat_size, lon_size, pt_ref, ps_ref, side_ref, t_ref, s_ref, n_ref, own_ref,
-    core_in, inter_in, below_in, above_in, fold_in, column_in, own_column, t_out, s_out,
+    near_in, core_in, far_in, below_in, above_in, column_in, relay_in, own_column, t_out, s_out,
     t_new, s_new, sems,
 ):
     shape = (levels, LANES)
@@ -264,7 +309,9 @@
     K = levels
     row_at = lax.axis_index("lat")
     is_top, is_bottom = row_at == lat_size - 1, row_at == 0
-    is_odd = lax.axis_index("lon") % 2 == 1
+    lon_at = lax.axis_index("lon")
+    is_odd = lon_at % 2 == 1
+    wraps = (lon_at == 0) | (lon_at == lon_size - 1)
 
     def faces(cells, speeds):
         wets = [level < jnp.minimum(a["n"], b["n"]) for a, b in zip(cells, cells[1:])]
@@ -284,7 +331,8 @@
     def cell_row(t, s, n):
         return column_row(t, s, n, factors, iota(shape, 0))
 
-    own, core, inter = side_ref[...], core_in[...], inter_in[...]
+    own, core = side_ref[...], core_in[...]
+    inter = jnp.where(is_top & ~wraps, near_in[...], far_in[4 * K + 8 :, :])
     west, east = jnp.where(is_odd, core, inter), jnp.where(is_odd, inter, core)
 
     def side(left, right):
@@ -318,10 +366,10 @@
     cells = [sent_row(below, 0, 5 * K), sent_row(below, 1, 5 * K), own_row(0), own_row(1)]
     _, south_flux, south_last = faces(cells, [None, below[4 * K : 5 * K], own_ref[:K]])
 
-    pivot = (lax.axis_index("lon") * 2) % lon_size == 0
-    column = jnp.where(pivot, own_column[...], column_in[...])
+    pivot = (lon_at * 2) % lon_size == 0
+    column = jnp.where(is_odd, relay_in[...], jnp.where(pivot, own_column[: K + 8, :], column_in[: K + 8, :]))
     parts = [roll(column[:K], -i) for i in range(4)] + [column[K : K + 8]]
-    fold = fold_in[...]
+    fold = far_in[: 4 * K + 8, :]
     fold = jnp.where(iota(fold.shape, 1) == 0, jnp.concatenate(parts, axis=0), fold)
     above = above_in[...]
     above = jnp.where(is_top, fold, jnp.concatenate([above[: 4 * K], above[5 * K :]], axis=0))
@@ -365,9 +413,9 @@
     swap = nlat == 2
     field, lat_shape = out(rows, K, LANES), out(5 * K + 8, LANES)
     shapes = [out(*t.shape)] * 4 + [jax.ShapeDtypeStruct(n.shape, n.dtype)]
-    shapes += [out(3 * K + 8, LANES), lat_shape, out(4 * K + 8, LANES), out(5 * K, LANES), out(3 * K, LANES)]
+    shapes += [out(3 * K + 8, LANES), lat_shape, out(7 * K + 16, LANES), out(4 * K, LANES), out(3 * K, LANES)]
     shapes += [] if swap else [lat_shape]
-    t_v, s_v, c_v, m_v, n_v, side, lat, fold, column, own, *more = pl.pallas_call(
+    t_v, s_v, c_v, m_v, n_v, side, lat, far, column, own, *more = pl.pallas_call(
         f(pack_kernel, levels, rows, nlat),
         out_shape=tuple(shapes),
         in_specs=[hbm] * 5,
@@ -377,46 +425,98 @@
         name="pack",
     )(*[pltpu.with_memory_space_constraint(x, pltpu.HBM) for x in (t, s, c, m, n)])
 
-    def across(array, partner):
-        to = {(j, i): (j, i ^ 1 if i ^ 1 < nlon else i) for j in range(nlat - 1) for i in range(nlon)}
-        top = nlat - 1
+    top = nlat - 1
+
+    def exchange(array, top_to, others_to, helper=lambda i: i):
+        to = {(j, i): (j, others_to(i)) for j in range(top) for i in range(nlon)}
         for i in range(nlon):
-            to[top, i] = (top, partner(i) % nlon)
-        for i in range(nlon):
-            if to[top, i] == (top, i) and to.get((0, i), (0, i)) != (0, i):
-                other = to[0, i]
-                to[top, i], to[0, i], to[other] = (0, i), other, (top, i)
+            partner, via = top_to(i), helper(i)
+            if partner is not None:
+                to[top, i] = (top, partner)
+            elif to.get((0, via)) == (0, via ^ 1) and to.get((0, via ^ 1)) == (0, via):
+                to[top, i], to[0, via], to[0, via ^ 1] = (0, via), (0, via ^ 1), (top, i)
+            else:
+                to[top, i] = (top, i)
         pairs = [(i * nlat + j, to[j, i][1] * nlat + to[j, i][0]) for i in range(nlon) for j in range(nlat)]
         return lax.ppermute(array, ("lon", "lat"), pairs)
 
+    def chips(i):
+        return (i + (1 if i % 2 else -1)) % nlon
+
+    def columns(i):
+        if i % 2:
+            return i ^ 1 if columns(i ^ 1) == i else None
+        return i ^ 1 if 2 * i % nlon == 0 else nlon - i
+
     ring, rung = range(nlon), range(nlat)
-    core_in = lax.ppermute(side, "lon", [(i, i ^ 1) for i in ring])
-    inter_in = lax.ppermute(side, "lon", [(i, (i + (1 if i % 2 else -1)) % nlon) for i in ring])
+    far_in = exchange(far, lambda i: nlon - 1 - i, chips)
+
+    middle = HEAD
+    fields = (t_v, s_v, c_v, m_v, n_v)
+    results = (out(*t.shape), out(*t.shape), out(STATE, K, LANES))
+    cost = pl.CostEstimate(flops=20_000_000, bytes_accessed=1_000_000, transcendentals=0)
+    pt, ps, state, lat, side, column = pl.pallas_call(
+        f(south_kernel, levels, rows, middle, nlat, False),
+        out_shape=results + tuple(out(*x.shape) for x in (lat, side, column)),
+        in_specs=[vmem] * 8,
+        out_specs=(vmem,) * 6,
+        input_output_aliases={5: 3, 6: 4, 7: 5},
+        cost_estimate=cost,
+        compiler_params=params,
+        name="south_of_others",
+    )(*fields, lat, side, column)
     below_in = above_in = lax.ppermute(lat, "lat", [(i, (i + 1) % nlat) for i in rung])
     if not swap:
         above_in = lax.ppermute(more[0], "lat", [(i, (i - 1) % nlat) for i in rung])
-    fold_in = across(fold, lambda i: nlon - 1 - i)
-    column_in = across(column, lambda i: nlon - i)
+    near_in = exchange(
+        side,
+        lambda i: chips(i) if 0 < i < nlon - 1 else None,
+        lambda i: i ^ 1,
+        lambda i: i + nlon // 4 if i == 0 else i - nlon // 4,
+    )
+    core_in = lax.ppermute(side, "lon", [(i, i ^ 1) for i in ring])
+    column_in = exchange(column, columns, lambda i: i ^ 1)
+
+    pt, ps, state = pl.pallas_call(
+        f(south_kernel, levels, rows, middle, nlat, True),
+        out_shape=results,
+        in_specs=[vmem] * 8,
+        out_specs=(vmem,) * 3,
+        input_output_aliases={5: 0, 6: 1, 7: 2},
+        cost_estimate=cost,
+        compiler_params=params,
+        name="south_of_top",
+    )(*fields, pt, ps, state)
+    relay = pl.pallas_call(
+        relay_kernel,
+        out_shape=out(K + 8, LANES),
+        in_specs=[vmem] * 2,
+        out_specs=vmem,
+        compiler_params=params,
+        name="relay",
+    )(far_in, state)
+    relay_in = lax.ppermute(relay, "lon", [(i, i ^ 1) for i in ring])
 
     pt, ps = pl.pallas_call(
-        f(interior_kernel, levels, rows),
-        out_shape=(out(*t.shape),) * 2,
-        in_specs=[vmem] * 5,
+        f(interior_kernel, levels, rows, middle, rows),
+        out_shape=(out(*t.shape), out(*t.shape)),
+        in_specs=[vmem] * 9,
         out_specs=(vmem,) * 2,
-        cost_estimate=pl.CostEstimate(flops=40_000_000, bytes_accessed=2_000_000, transcendentals=0),
+        input_output_aliases={5: 0, 6: 1},
+        cost_estimate=pl.CostEstimate(flops=20_000_000, bytes_accessed=1_000_000, transcendentals=0),
         compiler_params=params,
-        name="interior",
-    )(t_v, s_v, c_v, m_v, n_v)
+        name="interior_north",
+    )(*fields, pt, ps, relay, state)
 
     return pl.pallas_call(
         f(edge_kernel, levels, rows, nlat, nlon),
         out_shape=(out(*t.shape),) * 2,
-        in_specs=[vmem] * 14,
+        in_specs=[vmem] * 15,
         out_specs=(hbm,) * 2,
         scratch_shapes=[pltpu.VMEM(t.shape, F32)] * 2 + [pltpu.SemaphoreType.DMA((2,))],
         compiler_params=params,
         name="edge",
-    )(pt, ps, side, t_v, s_v, n_v, own, core_in, inter_in, below_in, above_in, fold_in, column_in, column)
+    )(pt, ps, side, t_v, s_v, n_v, own, near_in, core_in, far_in, below_in, above_in, column_in, relay_in, column)
 
 
 def solution(mesh):

time: 14.3 us -> 13.8 us (0.965)
  the two profiles are of different devices: /device:TPU:5 before, /device:TPU:0 now
where the time goes in v4:
time: 13.8 us; the launch traced here: 13.6 us
  starting transfers between devices  7.49 us (54%)
  Pallas kernels  5.15 us (37%)
  between operations  0.68 us (5%)
  waiting for transfers between devices  0.31 us (2%)
    ppermute x3, starting transfers between devices, exchange(): return lax.ppermute(array, ('lon', 'lat'), pairs)  6.27 us
    pallas_call x1, Pallas kernels, body(): pl.pallas_call(f(interior_kernel, levels, rows, middle, rows), out_shape=...  1.68 us
    pallas_call x1, Pallas kernels, body(): pl.pallas_call(f(pack_kernel, levels, rows, nlat), out_shape=tuple(shapes...  1.59 us
    pallas_call x1, Pallas kernels, body(): pl.pallas_call(f(edge_kernel, levels, rows, nlat, nlon), out_shape=(out(*...  1.28 us
    ppermute x1, starting transfers between devices, body(): lax.ppermute(lat, 'lat', [(i, (i + 1) % nlat) for i in rung])  0.98 us
    pallas_call x1, Pallas kernels, body(): pl.pallas_call(f(south_kernel, levels, rows, middle, nlat, False), out_sh...  0.53 us
    ppermute x1, waiting for transfers between devices, body(): lax.ppermute(lat, 'lat', [(i, (i + 1) % nlat) for i in rung])  0.3 us
  transfers between devices with their start and end apart: 6, of which 1 were waited for; matrix products, arithmetic and copies ran while one was open for 0% of the time, Pallas kernels for 17%

profile of v4, /device:TPU:0, one launch (start us, length us, event | category | flops | bytes accessed | tf_op | source)
XLA Modules:
  0.0 13.6 jit_solution(3866614151194487394)
XLA Ops:
  0.6 1.6 %pack.1 = (f32[16,32,128]{2,1,0:T(8,128)S(1)}, f32[16,32,128]{2,1,0:T(8,128)S(1)}, f32[16,32,128]{2,1,0:T(8,128)S(1)}, f32[16,32,128]{2,1,0:T(8,128)S(1)}, s32[3...) custom-call(f32[16,32,128]{2,1,0:T(8,128)} %t_hbm.1, ...), custom_call_target="tpu_custom_call" | custom-call | tf_op jit(solution)/shard_map/pack/pallas_call | solution.py:418
  2.2 5.5 %collective-permute-start = (f32[128,128]{1,0:T(8,128)S(1)}, f32[128,128]{1,0:T(8,128)S(1)}, u32[]{:S(2)}, u32[]{:S(2)}) collective-permute-start(f32[128,128]{1,0:T(8,128)S(1)} %get-tuple-element.36), channel_id=1, source_target_pairs={{0,30},{1,31},{2,4},{3,29},{4,2},{5,27},{6,8},{7,25},{8,6},{9,23},... | collective-permute-start | bytes 196616 | tf_op jit(solution)/shard_map/ppermute | solution.py:441
  7.7 0.5 %south_of_others.1 = (f32[16,32,128]{2,1,0:T(8,128)S(1)}, f32[16,32,128]{2,1,0:T(8,128)S(1)}, f32[19,16,128]{2,1,0:T(8,128)S(1)}, f32[88,128]{1,0:T(8,128)S(1)},...) custom-call(f32[16,32,128]{2,1,0:T(8,128)S(1)} %get-tuple-element.23.t_r, ...), custom_call_target="tpu_custom_call", output_to_operand_aliasing={{3}: (5, {}), {4}: (6, {}), {5}: (7, {})} | custom-call | flops 20000000 | bytes 1000000 | tf_op jit(solution)/shard_map/south_of_others/pallas_call | solution.py:458
  8.2 1.0 %collective-permute-start.3 = (f32[88,128]{1,0:T(8,128)S(1)}, f32[88,128]{1,0:T(8,128)S(1)}, u32[]{:S(2)}, u32[]{:S(2)}) collective-permute-start(f32[88,128]{1,0:T(8,128)S(1)} %get-tuple-element.42), channel_id=1, source_target_pairs={{0,1},{1,0},{2,3},{3,2},{4,5},{5,4},{6,7},{7,6},{8,9},{9,8},{10,11... | collective-permute-start | bytes 135176 | tf_op jit(solution)/shard_map/ppermute | solution.py:468
  9.2 0.4 %collective-permute-start.4 = (f32[64,128]{1,0:T(8,128)S(1)}, f32[64,128]{1,0:T(8,128)S(1)}, u32[]{:S(2)}, u32[]{:S(2)}) collective-permute-start(f32[64,128]{1,0:T(8,128)S(1)} %get-tuple-element.43.own_column), channel_id=1, source_target_pairs={{0,2},{1,3},{2,0},{3,1},{4,7},{5,29},{6,4},{7,6},{8,11},{9,25},{10... | collective-permute-start | bytes 98312 | tf_op jit(solution)/shard_map/ppermute | solution.py:441
  9.6 0.1 collective-permute-start.2
  9.7 0.4 %collective-permute-start.1 = (f32[56,128]{1,0:T(8,128)S(1)}, f32[56,128]{1,0:T(8,128)S(1)}, u32[]{:S(2)}, u32[]{:S(2)}) collective-permute-start(f32[56,128]{1,0:T(8,128)S(1)} %get-tuple-element.40.side_ref), channel_id=1, source_target_pairs={{0,2},{1,8},{2,0},{3,5},{4,6},{5,3},{6,4},{7,9},{8,10},{9,7},{10,1... | collective-permute-start | bytes 86024 | tf_op jit(solution)/shard_map/ppermute | solution.py:441
  10.1 0.0 collective-permute-done.far_ref.far_in
  10.1 0.1 relay.1.more_2_
  10.2 0.1 collective-permute-start.5
  10.3 1.7 %interior_north.1 = (f32[16,32,128]{2,1,0:T(8,128)S(1)}, f32[16,32,128]{2,1,0:T(8,128)S(1)}) custom-call(f32[16,32,128]{2,1,0:T(8,128)S(1)} %get-tuple-element.23.t_ref, f32[16,32,128]{2,1,0:T(8,128)S(1)} %get-tuple-element.24.s_ref, f32[16,32,128]{2,1,0:T(8,128)S(1)} %get-tuple-element.25.c_ref, ...), custom_call_target="tpu_custom_call", output_to_operand_aliasing={{0}: (5, {}), {1}: (6, {})} | custom-call | flops 20000000 | bytes 1000000 | tf_op jit(solution)/shard_map/interior_north/pallas_call | solution.py:500
  12.0 0.0 collective-permute-done.2.core_in
  12.0 0.0 collective-permute-done.1.near_in
  12.0 0.0 collective-permute-done.4.column_in
  12.1 0.3 %collective-permute-done.3.below_in.above_in = f32[88,128]{1,0:T(8,128)S(1)} collective-permute-done((f32[88,128]{1,0:T(8,128)S(1)}, f32[88,128]{1,0:T(8,128)S(1)}, u32[]{:S(2)}, u32[]{:S(2)}) %collective-permute-start.3) | collective-permute-done | bytes 45088 | tf_op jit(solution)/shard_map/ppermute | solution.py:468
  12.4 0.0 collective-permute-done.5.relay_in
  12.4 1.3 %edge.1 = (f32[16,32,128]{2,1,0:T(8,128)}, f32[16,32,128]{2,1,0:T(8,128)}) custom-call(f32[16,32,128]{2,1,0:T(8,128)S(1)} %get-tuple-element.38.pt_ref, f32[16,32,128]{2,1,0:T(8,128)S(1)} %get-tuple-element.39.ps_ref, f32[56,128]{1,0:T(8,128)S(1)} %get-tuple-element.40.side_ref, f32[16,32,128]{2,1,0:T(8,128)S(1)} %get-tuple-element.23.t_ref, ...), custom_call_target="tpu_custom_call" | custom-call | tf_op jit(solution)/shard_map/edge/pallas_call | solution.py:511
  (1 shorter events, 0.0 us)
Async XLA Ops:
  2.2 7.9 %collective-permute-start = (f32[128,128]{1,0:T(8,128)S(1)}, f32[128,128]{1,0:T(8,128)S(1)}, u32[]{:S(2)}, u32[]{:S(2)}) collective-permute-start(f32[128,128]{1,0:T(8,128)S(1)} %get-tuple-element.36), channel_id=1, source_target_pairs={{0,30},{1,31},{2,4},{3,29},{4,2},{5,27},{6,8},{7,25},{8,6},{9,23},... | collective-permute-start | bytes 196616 | tf_op jit(solution)/shard_map/ppermute | solution.py:441
  8.2 4.1 %collective-permute-start.3 = (f32[88,128]{1,0:T(8,128)S(1)}, f32[88,128]{1,0:T(8,128)S(1)}, u32[]{:S(2)}, u32[]{:S(2)}) collective-permute-start(f32[88,128]{1,0:T(8,128)S(1)} %get-tuple-element.42), channel_id=1, source_target_pairs={{0,1},{1,0},{2,3},{3,2},{4,5},{5,4},{6,7},{7,6},{8,9},{9,8},{10,11... | collective-permute-start | bytes 135176 | tf_op jit(solution)/shard_map/ppermute | solution.py:468
  9.2 2.8 %collective-permute-start.4 = (f32[64,128]{1,0:T(8,128)S(1)}, f32[64,128]{1,0:T(8,128)S(1)}, u32[]{:S(2)}, u32[]{:S(2)}) collective-permute-start(f32[64,128]{1,0:T(8,128)S(1)} %get-tuple-element.43.own_column), channel_id=1, source_target_pairs={{0,2},{1,3},{2,0},{3,1},{4,7},{5,29},{6,4},{7,6},{8,11},{9,25},{10... | collective-permute-start | bytes 98312 | tf_op jit(solution)/shard_map/ppermute | solution.py:441
  9.6 2.4 %collective-permute-start.2 = (f32[56,128]{1,0:T(8,128)S(1)}, f32[56,128]{1,0:T(8,128)S(1)}, u32[]{:S(2)}, u32[]{:S(2)}) collective-permute-start(f32[56,128]{1,0:T(8,128)S(1)} %get-tuple-element.40.side_ref), channel_id=1, source_target_pairs={{0,2},{2,0},{4,6},{6,4},{8,10},{10,8},{12,14},{14,12},{16,18},{18,... | collective-permute-start | bytes 86024 | tf_op jit(solution)/shard_map/ppermute | solution.py:477
  9.7 2.3 %collective-permute-start.1 = (f32[56,128]{1,0:T(8,128)S(1)}, f32[56,128]{1,0:T(8,128)S(1)}, u32[]{:S(2)}, u32[]{:S(2)}) collective-permute-start(f32[56,128]{1,0:T(8,128)S(1)} %get-tuple-element.40.side_ref), channel_id=1, source_target_pairs={{0,2},{1,8},{2,0},{3,5},{4,6},{5,3},{6,4},{7,9},{8,10},{9,7},{10,1... | collective-permute-start | bytes 86024 | tf_op jit(solution)/shard_map/ppermute | solution.py:441
  10.2 2.1 %collective-permute-start.5 = (f32[24,128]{1,0:T(8,128)S(1)}, f32[24,128]{1,0:T(8,128)S(1)}, u32[]{:S(2)}, u32[]{:S(2)}) collective-permute-start(f32[24,128]{1,0:T(8,128)S(1)} %relay.1.more_2_), channel_id=1, source_target_pairs={{0,2},{2,0},{4,6},{6,4},{8,10},{10,8},{12,14},{14,12},{16,18},{18,... | collective-permute-start | bytes 36872 | tf_op jit(solution)/shard_map/ppermute | solution.py:498

commit v5 on v4

--- a/solution.py
+++ b/solution.py
@@ -21,7 +21,8 @@
 LANES = 128
 VMEM = 8 * 1024 * 1024
 UNROLL = 8
-HEAD = 8
+HEAD = 16
+SPARE = 8
 F32 = jnp.float32
 
 
@@ -111,11 +112,12 @@
 
 def pack_kernel(
     levels, rows, lat_size, t_hbm, s_hbm, c_hbm, m_hbm, n_hbm,
-    t_ref, s_ref, c_ref, m_ref, n_ref, side_ref, lat_ref, far_ref, column_ref, own_ref, *more,
+    t_ref, s_ref, c_ref, m_ref, n_ref, side_ref, core_ref, chip_ref, lat_ref, far_ref, column_ref, own_ref, *more,
 ):
     *more, sems = more
     K = levels
     pairs = ((t_hbm, t_ref), (s_hbm, s_ref), (c_hbm, c_ref), (n_hbm, n_ref), (m_hbm, m_ref))
+    pairs = [(src, dst if dst is n_ref else dst.at[:, :rows]) for src, dst in pairs]
     copies = [pltpu.make_async_copy(src, dst, sems.at[i]) for i, (src, dst) in enumerate(pairs)]
     for copy in copies:
         copy.start()
@@ -141,11 +143,6 @@
             tiles.append(out)
         return jnp.concatenate(tiles, axis=0)
 
-    def put_side(at, value):
-        size = value.shape[0]
-        side_ref[at : at + size, :] = value
-        far_ref[4 * K + 8 + at : 4 * K + 8 + at + size, :] = value
-
     def mirrored(x):
         index = (LANES - iota(x.shape, 1)) % LANES
         return jnp.take_along_axis(x, index, axis=1)
@@ -157,9 +154,12 @@
 
     south, north, fold = (0, 1), (rows - 2, rows - 1), (rows - 2, rows - 3)
     is_top = lax.axis_index("lat") == lat_size - 1
+    is_odd = lax.axis_index("lon") % 2 == 1
+    place = iota((levels, LANES), 1) % 4
+    sides = []
     for tracer, ref in enumerate((t_ref, s_ref)):
         copies[tracer].wait()
-        put_side(tracer * K, gather(ref))
+        sides.append(gather(ref))
         tracer_rows(far_ref, tracer, ref, fold, mirrored)
         if more:
             tracer_rows(lat_ref, tracer, ref, north)
@@ -170,14 +170,25 @@
                 lat_ref[at : at + K, :] = jnp.where(is_top, strided(ref, south[i]), strided(ref, north[i]))
 
     copies[2].wait()
-    put_side(2 * K, gather(c_ref))
+    sides.append(gather(c_ref))
     copies[3].wait()
     counts = n_ref[...].astype(F32)
     moved = jnp.concatenate([roll(counts[j : j + 1], 4 * j + 2) for j in range(rows)], axis=0)
     line = jnp.sum(
         jnp.where(iota((rows, LANES), 1) // 4 == iota((rows, LANES), 0), moved, 0.0), axis=0, keepdims=True
     )
-    put_side(3 * K, jnp.broadcast_to(line, (8, LANES)))
+    heat, salt, speed = sides
+    line = jnp.broadcast_to(line, (levels, LANES))
+    for i, value in enumerate((heat, salt, speed)):
+        side_ref[i * K : (i + 1) * K, :] = value
+    side_ref[3 * K :, :] = line[:8]
+    to_east = jnp.where(place < 2, heat, roll(salt, 2)), jnp.where(place == 2, roll(speed, 1), line)
+    to_west = jnp.where(place < 2, roll(salt, -2), heat), line
+    for i, (e, w) in enumerate(zip(to_east, to_west)):
+        core_ref[i * K : (i + 1) * K, :] = jnp.where(is_odd, w, e)
+        chip = jnp.where(is_odd, e, w)
+        chip_ref[i * K : (i + 1) * K, :] = chip
+        far_ref[4 * K + 8 + i * K : 4 * K + 8 + (i + 1) * K, :] = chip
 
     def tally(picks):
         return jnp.concatenate(
@@ -216,10 +227,11 @@
 STATE = 19
 
 
-def south_kernel(levels, rows, last, lat_size, on_top, t_ref, s_ref, c_ref, m_ref, n_ref, *more):
-    pt_ref, ps_ref, state_out = more[3:6]
-
-    @pl.when((lax.axis_index("lat") == lat_size - 1) == on_top)
+def south_kernel(levels, rows, last, early, t_ref, s_ref, c_ref, m_ref, n_ref, *more):
+    *more, pt_ref, ps_ref, state_out = more[:-1] if early else more
+    at_origin = (lax.axis_index("lat") == 0) & (lax.axis_index("lon") < 2)
+
+    @pl.when(at_origin if early else jnp.logical_not(at_origin))
     def _():
         interior_kernel(levels, rows, 0, last, t_ref, s_ref, c_ref, m_ref, n_ref, pt_ref, ps_ref, state_out)
 
@@ -331,19 +343,30 @@
     def cell_row(t, s, n):
         return column_row(t, s, n, factors, iota(shape, 0))
 
-    own, core = side_ref[...], core_in[...]
-    inter = jnp.where(is_top & ~wraps, near_in[...], far_in[4 * K + 8 :, :])
-    west, east = jnp.where(is_odd, core, inter), jnp.where(is_odd, inter, core)
-
-    def side(left, right):
-        both = jnp.where(iota(left.shape, 1) % 4 < 2, left, right)
-        row = cell_row(both[:K], both[K : 2 * K], both[3 * K : 3 * K + 1])
+    own_t, own_s, own_c = (side_ref[i * K : (i + 1) * K, :] for i in range(3))
+    own_n = side_ref[3 * K : 3 * K + 1, :]
+    core = core_in[...]
+    chip = jnp.where(is_top & ~wraps, near_in[...], far_in[4 * K + 8 :, :])
+    west, east = jnp.where(is_odd, core, chip), jnp.where(is_odd, chip, core)
+    first_two = place < 2
+
+    def side(t, s, n, speed):
+        row = cell_row(t, s, n)
         cells = [row] + [shifted(row, -i) for i in (1, 2, 3)]
-        speed = both[2 * K : 3 * K]
         return faces(cells, [roll(speed, -i) for i in range(3)])
 
-    _, west_flux, west_last = side(west, own)
-    east_first, east_flux, _ = side(own, east)
+    _, west_flux, west_last = side(
+        jnp.where(first_two, west[:K], own_t),
+        jnp.where(first_two, roll(west[:K], -2), own_s),
+        jnp.where(first_two[:1], west[K : K + 1], own_n),
+        jnp.where(place == 1, roll(west[K:], -1), own_c),
+    )
+    east_first, east_flux, _ = side(
+        jnp.where(first_two, own_t, east[:K]),
+        jnp.where(first_two, own_s, roll(east[:K], 2)),
+        jnp.where(first_two[:1], own_n, east[K : K + 1]),
+        own_c,
+    )
     lon = []
     for fw, lw, fe, le in zip(west_flux, west_last, east_flux, east_first):
         group = jnp.where(
@@ -397,7 +420,7 @@
         }
         for j, value in extra.items():
             put(new_ref, j, strided(new_ref, j) + value)
-        copies.append(pltpu.make_async_copy(new_ref, out_ref, sems.at[q]))
+        copies.append(pltpu.make_async_copy(new_ref.at[:, :rows], out_ref, sems.at[q]))
         copies[q].start()
     for copy in copies:
         copy.wait()
@@ -412,10 +435,12 @@
     params = pltpu.CompilerParams(vmem_limit_bytes=VMEM)
     swap = nlat == 2
     field, lat_shape = out(rows, K, LANES), out(5 * K + 8, LANES)
-    shapes = [out(*t.shape)] * 4 + [jax.ShapeDtypeStruct(n.shape, n.dtype)]
-    shapes += [out(3 * K + 8, LANES), lat_shape, out(7 * K + 16, LANES), out(4 * K, LANES), out(3 * K, LANES)]
+    room = out(levels, rows + SPARE, LANES)
+    shapes = [room] * 4 + [jax.ShapeDtypeStruct(n.shape, n.dtype)]
+    shapes += [out(3 * K + 8, LANES), out(2 * K, LANES), out(2 * K, LANES), lat_shape, out(6 * K + 8, LANES)]
+    shapes += [out(2 * K + 8, LANES), out(3 * K, LANES)]
     shapes += [] if swap else [lat_shape]
-    t_v, s_v, c_v, m_v, n_v, side, lat, far, column, own, *more = pl.pallas_call(
+    t_v, s_v, c_v, m_v, n_v, side, core, chip, lat, far, column, own, *more = pl.pallas_call(
         f(pack_kernel, levels, rows, nlat),
         out_shape=tuple(shapes),
         in_specs=[hbm] * 5,
@@ -443,49 +468,50 @@
     def chips(i):
         return (i + (1 if i % 2 else -1)) % nlon
 
-    def columns(i):
-        if i % 2:
-            return i ^ 1 if columns(i ^ 1) == i else None
-        return i ^ 1 if 2 * i % nlon == 0 else nlon - i
+    columns = {i: i ^ 1 if 2 * i % nlon == 0 else nlon - i for i in range(0, nlon, 2)}
+    lone = [i for i in range(1, nlon, 2) if columns[i - 1] != i]
+    columns |= {i: i - 1 for i in range(1, nlon, 2) if i not in lone}
+    for part in ([i for i in lone if 2 * i < nlon], [i for i in lone if 2 * i > nlon]):
+        columns |= dict(zip(part, part[1:] + part[:1]))
+
+    middle = HEAD
+    fields = (t_v, s_v, c_v, m_v, n_v)
+    south_out = (room, room, out(STATE, K, LANES))
+    cost = pl.CostEstimate(flops=20_000_000, bytes_accessed=1_000_000, transcendentals=0)
+    pt, ps, state, far = pl.pallas_call(
+        f(south_kernel, levels, rows, middle, True),
+        out_shape=south_out + (out(*far.shape),),
+        in_specs=[vmem] * 6,
+        out_specs=(vmem,) * 4,
+        input_output_aliases={5: 3},
+        cost_estimate=cost,
+        compiler_params=params,
+        name="south_at_origin",
+    )(*fields, far)
 
     ring, rung = range(nlon), range(nlat)
     far_in = exchange(far, lambda i: nlon - 1 - i, chips)
-
-    middle = HEAD
-    fields = (t_v, s_v, c_v, m_v, n_v)
-    results = (out(*t.shape), out(*t.shape), out(STATE, K, LANES))
-    cost = pl.CostEstimate(flops=20_000_000, bytes_accessed=1_000_000, transcendentals=0)
-    pt, ps, state, lat, side, column = pl.pallas_call(
-        f(south_kernel, levels, rows, middle, nlat, False),
-        out_shape=results + tuple(out(*x.shape) for x in (lat, side, column)),
-        in_specs=[vmem] * 8,
-        out_specs=(vmem,) * 6,
-        input_output_aliases={5: 3, 6: 4, 7: 5},
-        cost_estimate=cost,
-        compiler_params=params,
-        name="south_of_others",
-    )(*fields, lat, side, column)
     below_in = above_in = lax.ppermute(lat, "lat", [(i, (i + 1) % nlat) for i in rung])
     if not swap:
         above_in = lax.ppermute(more[0], "lat", [(i, (i - 1) % nlat) for i in rung])
     near_in = exchange(
-        side,
+        chip,
         lambda i: chips(i) if 0 < i < nlon - 1 else None,
         lambda i: i ^ 1,
         lambda i: i + nlon // 4 if i == 0 else i - nlon // 4,
     )
-    core_in = lax.ppermute(side, "lon", [(i, i ^ 1) for i in ring])
-    column_in = exchange(column, columns, lambda i: i ^ 1)
+    core_in = lax.ppermute(core, "lon", [(i, i ^ 1) for i in ring])
+    column_in = exchange(column, columns.get, lambda i: i ^ 1)
 
     pt, ps, state = pl.pallas_call(
-        f(south_kernel, levels, rows, middle, nlat, True),
-        out_shape=results,
+        f(south_kernel, levels, rows, middle, False),
+        out_shape=south_out,
         in_specs=[vmem] * 8,
         out_specs=(vmem,) * 3,
         input_output_aliases={5: 0, 6: 1, 7: 2},
         cost_estimate=cost,
         compiler_params=params,
-        name="south_of_top",
+        name="south_elsewhere",
     )(*fields, pt, ps, state)
     relay = pl.pallas_call(
         relay_kernel,
@@ -499,7 +525,7 @@
 
     pt, ps = pl.pallas_call(
         f(interior_kernel, levels, rows, middle, rows),
-        out_shape=(out(*t.shape), out(*t.shape)),
+        out_shape=(room, room),
         in_specs=[vmem] * 9,
         out_specs=(vmem,) * 2,
         input_output_aliases={5: 0, 6: 1},
@@ -513,7 +539,7 @@
         out_shape=(out(*t.shape),) * 2,
         in_specs=[vmem] * 15,
         out_specs=(hbm,) * 2,
-        scratch_shapes=[pltpu.VMEM(t.shape, F32)] * 2 + [pltpu.SemaphoreType.DMA((2,))],
+        scratch_shapes=[pltpu.VMEM(room.shape, F32)] * 2 + [pltpu.SemaphoreType.DMA((2,))],
         compiler_params=params,
         name="edge",
     )(pt, ps, side, t_v, s_v, n_v, own, near_in, core_in, far_in, below_in, above_in, column_in, relay_in, column)

time: 13.8 us -> 13.2 us (0.957)
  Pallas kernels: 5.15 us -> 4.59 us
  starting transfers between devices: 7.49 us -> 7.21 us
  waiting for transfers between devices: 0.31 us -> 0.58 us
    ppermute x3, starting transfers between devices: 6.27 us -> 5.18 us  [exchange(): return lax.ppermute(array, ('lon', 'lat'), pairs)]
    pallas_call x1, Pallas kernels: 1.68 us -> 0.82 us  [body(): pl.pallas_call(f(interior_kernel, levels, rows, middle, rows), out_shape=...]
    ppermute x1, starting transfers between devices: 0.98 us -> 1.52 us  [body(): lax.ppermute(lat, 'lat', [(i, (i + 1) % nlat) for i in rung])]
    pallas_call x2, Pallas kernels: 0.53 us -> 0.83 us  [the longest x1 0.83 us: body(): pl.pallas_call(f(south_kernel, levels, rows, middle, True), out_shape=sou...]
    ppermute x1, starting transfers between devices: 0.11 us -> 0.4 us  [body(): core_in = lax.ppermute(core, 'lon', [(i, i ^ 1) for i in ring])]
    ppermute x1, waiting for transfers between devices: 0.3 us -> 0.56 us  [body(): lax.ppermute(lat, 'lat', [(i, (i + 1) % nlat) for i in rung])]
  transfers between devices with their start and end apart: 6 -> 6, of which waited for: 1 -> 1; matrix products, arithmetic and copies ran while one was open for 0% -> 0% of each run, Pallas kernels for 17% -> 7%
where the time goes in v5:
time: 13.2 us; the launch traced here: 13.1 us
  starting transfers between devices  7.21 us (55%)
  Pallas kernels  4.59 us (35%)
  between operations  0.68 us (5%)
  waiting for transfers between devices  0.58 us (4%)
    ppermute x3, starting transfers between devices, exchange(): return lax.ppermute(array, ('lon', 'lat'), pairs)  5.18 us
    pallas_call x1, Pallas kernels, body(): pl.pallas_call(f(pack_kernel, levels, rows, nlat), out_shape=tuple(shapes...  1.56 us
    ppermute x1, starting transfers between devices, body(): lax.ppermute(lat, 'lat', [(i, (i + 1) % nlat) for i in rung])  1.52 us
    pallas_call x1, Pallas kernels, body(): pl.pallas_call(f(edge_kernel, levels, rows, nlat, nlon), out_shape=(out(*...  1.3 us
    pallas_call x1, Pallas kernels, body(): pl.pallas_call(f(south_kernel, levels, rows, middle, True), out_shape=sou...  0.83 us
    pallas_call x1, Pallas kernels, body(): pl.pallas_call(f(interior_kernel, levels, rows, middle, rows), out_shape=...  0.82 us
    ppermute x1, waiting for transfers between devices, body(): lax.ppermute(lat, 'lat', [(i, (i + 1) % nlat) for i in rung])  0.56 us
    ppermute x1, starting transfers between devices, body(): core_in = lax.ppermute(core, 'lon', [(i, i ^ 1) for i in ring])  0.4 us
  transfers between devices with their start and end apart: 6, of which 1 were waited for; matrix products, arithmetic and copies ran while one was open for 0% of the time, Pallas kernels for 7%

profile of v5, /device:TPU:0, one launch (start us, length us, event | category | flops | bytes accessed | tf_op | source)
XLA Modules:
  0.0 13.1 jit_solution(10134661388118520587)
XLA Ops:
  0.6 1.6 %pack.1 = (f32[16,40,128]{2,1,0:T(8,128)S(1)}, f32[16,40,128]{2,1,0:T(8,128)S(1)}, f32[16,40,128]{2,1,0:T(8,128)S(1)}, f32[16,40,128]{2,1,0:T(8,128)S(1)}, s32[3...) custom-call(f32[16,32,128]{2,1,0:T(8,128)} %t_hbm.1, ...), custom_call_target="tpu_custom_call" | custom-call | tf_op jit(solution)/shard_map/pack/pallas_call | solution.py:443
  2.2 0.8 %south_at_origin.1 = (f32[16,40,128]{2,1,0:T(8,128)S(1)}, f32[16,40,128]{2,1,0:T(8,128)S(1)}, f32[19,16,128]{2,1,0:T(8,128)S(1)}, f32[104,128]{1,0:T(8,128)S(1)}) custom-call(f32[16,40,128]{2,1,0:T(8,128)S(1)} %get-tuple-element.23.t_ref, f32[16,40,128]{2,1,0:T(8,128)S(1)} %get-tuple-element.24.s_ref, ...), custom_call_target="tpu_custom_call", output_to_operand_aliasing={{3}: (5, {})} | custom-call | flops 20000000 | bytes 1000000 | tf_op jit(solution)/shard_map/south_at_origin/pallas_call | solution.py:481
  3.0 4.7 %collective-permute-start = (f32[104,128]{1,0:T(8,128)S(1)}, f32[104,128]{1,0:T(8,128)S(1)}, u32[]{:S(2)}, u32[]{:S(2)}) collective-permute-start(f32[104,128]{1,0:T(8,128)S(1)} %get-tuple-element.34), channel_id=1, source_target_pairs={{0,30},{1,31},{2,4},{3,29},{4,2},{5,27},{6,8},{7,25},{8,6},{9,23},... | collective-permute-start | bytes 159752 | tf_op jit(solution)/shard_map/ppermute | solution.py:466
  7.7 1.5 %collective-permute-start.3 = (f32[88,128]{1,0:T(8,128)S(1)}, f32[88,128]{1,0:T(8,128)S(1)}, u32[]{:S(2)}, u32[]{:S(2)}) collective-permute-start(f32[88,128]{1,0:T(8,128)S(1)} %get-tuple-element.42), channel_id=1, source_target_pairs={{0,1},{1,0},{2,3},{3,2},{4,5},{5,4},{6,7},{7,6},{8,9},{9,8},{10,11... | collective-permute-start | bytes 135176 | tf_op jit(solution)/shard_map/ppermute | solution.py:494
  9.2 0.4 %collective-permute-start.4 = (f32[40,128]{1,0:T(8,128)S(1)}, f32[40,128]{1,0:T(8,128)S(1)}, u32[]{:S(2)}, u32[]{:S(2)}) collective-permute-start(f32[40,128]{1,0:T(8,128)S(1)} %get-tuple-element.43.own_column), channel_id=1, source_target_pairs={{0,2},{1,3},{2,0},{3,1},{4,6},{5,29},{6,4},{7,11},{8,10},{9,25},{1... | collective-permute-start | bytes 61448 | tf_op jit(solution)/shard_map/ppermute | solution.py:466
  9.6 0.1 collective-permute-start.1
  9.7 0.4 %collective-permute-start.2 = (f32[32,128]{1,0:T(8,128)S(1)}, f32[32,128]{1,0:T(8,128)S(1)}, u32[]{:S(2)}, u32[]{:S(2)}) collective-permute-start(f32[32,128]{1,0:T(8,128)S(1)} %get-tuple-element.41), channel_id=1, source_target_pairs={{0,2},{2,0},{4,6},{6,4},{8,10},{10,8},{12,14},{14,12},{16,18},{18,... | collective-permute-start | bytes 49160 | tf_op jit(solution)/shard_map/ppermute | solution.py:503
  10.1 0.0 collective-permute-done.far_ref.far_in
  10.1 0.1 relay.1.more_2_
  10.2 0.1 collective-permute-start.5
  10.3 0.8 %interior_north.1 = (f32[16,40,128]{2,1,0:T(8,128)S(1)}, f32[16,40,128]{2,1,0:T(8,128)S(1)}) custom-call(f32[16,40,128]{2,1,0:T(8,128)S(1)} %get-tuple-element.23.t_ref, f32[16,40,128]{2,1,0:T(8,128)S(1)} %get-tuple-element.24.s_ref, f32[16,40,128]{2,1,0:T(8,128)S(1)} %get-tuple-element.25.c_ref, ...), custom_call_target="tpu_custom_call", output_to_operand_aliasing={{0}: (5, {}), {1}: (6, {})} | custom-call | flops 20000000 | bytes 1000000 | tf_op jit(solution)/shard_map/interior_north/pallas_call | solution.py:526
  11.2 0.0 collective-permute-done.1.near_in
  11.2 0.0 collective-permute-done.2.core_in
  11.2 0.0 collective-permute-done.4.column_in
  11.2 0.6 %collective-permute-done.3.below_in.above_in = f32[88,128]{1,0:T(8,128)S(1)} collective-permute-done((f32[88,128]{1,0:T(8,128)S(1)}, f32[88,128]{1,0:T(8,128)S(1)}, u32[]{:S(2)}, u32[]{:S(2)}) %collective-permute-start.3) | collective-permute-done | bytes 45088 | tf_op jit(solution)/shard_map/ppermute | solution.py:494
  11.8 0.0 collective-permute-done.5.relay_in
  11.8 1.3 %edge.1 = (f32[16,32,128]{2,1,0:T(8,128)}, f32[16,32,128]{2,1,0:T(8,128)}) custom-call(f32[16,40,128]{2,1,0:T(8,128)S(1)} %get-tuple-element.36.pt_ref, f32[16,40,128]{2,1,0:T(8,128)S(1)} %get-tuple-element.37.ps_ref, f32[56,128]{1,0:T(8,128)S(1)} %get-tuple-element.38.side_ref, f32[16,40,128]{2,1,0:T(8,128)S(1)} %get-tuple-element.23.t_ref, ...), custom_call_target="tpu_custom_call" | custom-call | tf_op jit(solution)/shard_map/edge/pallas_call | solution.py:537
  (1 shorter events, 0.0 us)
Async XLA Ops:
  3.0 7.1 %collective-permute-start = (f32[104,128]{1,0:T(8,128)S(1)}, f32[104,128]{1,0:T(8,128)S(1)}, u32[]{:S(2)}, u32[]{:S(2)}) collective-permute-start(f32[104,128]{1,0:T(8,128)S(1)} %get-tuple-element.34), channel_id=1, source_target_pairs={{0,30},{1,31},{2,4},{3,29},{4,2},{5,27},{6,8},{7,25},{8,6},{9,23},... | collective-permute-start | bytes 159752 | tf_op jit(solution)/shard_map/ppermute | solution.py:466
  7.7 4.0 %collective-permute-start.3 = (f32[88,128]{1,0:T(8,128)S(1)}, f32[88,128]{1,0:T(8,128)S(1)}, u32[]{:S(2)}, u32[]{:S(2)}) collective-permute-start(f32[88,128]{1,0:T(8,128)S(1)} %get-tuple-element.42), channel_id=1, source_target_pairs={{0,1},{1,0},{2,3},{3,2},{4,5},{5,4},{6,7},{7,6},{8,9},{9,8},{10,11... | collective-permute-start | bytes 135176 | tf_op jit(solution)/shard_map/ppermute | solution.py:494
  9.2 2.0 %collective-permute-start.4 = (f32[40,128]{1,0:T(8,128)S(1)}, f32[40,128]{1,0:T(8,128)S(1)}, u32[]{:S(2)}, u32[]{:S(2)}) collective-permute-start(f32[40,128]{1,0:T(8,128)S(1)} %get-tuple-element.43.own_column), channel_id=1, source_target_pairs={{0,2},{1,3},{2,0},{3,1},{4,6},{5,29},{6,4},{7,11},{8,10},{9,25},{1... | collective-permute-start | bytes 61448 | tf_op jit(solution)/shard_map/ppermute | solution.py:466
  9.6 1.5 %collective-permute-start.1 = (f32[32,128]{1,0:T(8,128)S(1)}, f32[32,128]{1,0:T(8,128)S(1)}, u32[]{:S(2)}, u32[]{:S(2)}) collective-permute-start(f32[32,128]{1,0:T(8,128)S(1)} %get-tuple-element.40), channel_id=1, source_target_pairs={{0,2},{1,8},{2,0},{3,5},{4,6},{5,3},{6,4},{7,9},{8,10},{9,7},{10,1... | collective-permute-start | bytes 49160 | tf_op jit(solution)/shard_map/ppermute | solution.py:466
  9.7 1.4 %collective-permute-start.2 = (f32[32,128]{1,0:T(8,128)S(1)}, f32[32,128]{1,0:T(8,128)S(1)}, u32[]{:S(2)}, u32[]{:S(2)}) collective-permute-start(f32[32,128]{1,0:T(8,128)S(1)} %get-tuple-element.41), channel_id=1, source_target_pairs={{0,2},{2,0},{4,6},{6,4},{8,10},{10,8},{12,14},{14,12},{16,18},{18,... | collective-permute-start | bytes 49160 | tf_op jit(solution)/shard_map/ppermute | solution.py:503
  10.2 1.5 %collective-permute-start.5 = (f32[24,128]{1,0:T(8,128)S(1)}, f32[24,128]{1,0:T(8,128)S(1)}, u32[]{:S(2)}, u32[]{:S(2)}) collective-permute-start(f32[24,128]{1,0:T(8,128)S(1)} %relay.1.more_2_), channel_id=1, source_target_pairs={{0,2},{2,0},{4,6},{6,4},{8,10},{10,8},{12,14},{14,12},{16,18},{18,... | collective-permute-start | bytes 36872 | tf_op jit(solution)/shard_map/ppermute | solution.py:524

commit v6 on v5

--- a/solution.py
+++ b/solution.py
@@ -308,37 +308,35 @@
         put(ref, rows - 1, a1 + f)
 
 
-def edge_kernel(
-    levels, rows, lat_size, lon_size, pt_ref, ps_ref, side_ref, t_ref, s_ref, n_ref, own_ref,
-    near_in, core_in, far_in, below_in, above_in, column_in, relay_in, own_column, t_out, s_out,
-    t_new, s_new, sems,
+def edge_faces(cells, speeds):
+    level = iota(cells[0]["t"].shape, 0).astype(F32)
+    wets = [level < jnp.minimum(a["n"], b["n"]) for a, b in zip(cells, cells[1:])]
+    d = [[face_step(a, b, w, q) for q in "ts"] for a, b, w in zip(cells, cells[1:], wets)]
+    limited = [[minmod(x, y) for x, y in zip(d[i], d[i + 1])] for i in (0, 1)]
+    base, wg, forward = face_base(cells[1], cells[2], speeds[1], wets[1], d[1])
+    flux = [b + wg * jnp.where(forward, x, y) for b, x, y in zip(base, *limited)]
+    first = last = None
+    if speeds[0] is not None:
+        _, wg0 = weights(speeds[0], wets[0])
+        first = [wg0 * jnp.where(speeds[0] > 0.0, 0.0, x) for x in limited[0]]
+    if speeds[2] is not None:
+        _, wg2 = weights(speeds[2], wets[2])
+        last = [wg2 * jnp.where(speeds[2] > 0.0, x, 0.0) for x in limited[1]]
+    return first, flux, last
+
+
+def longitude_kernel(
+    levels, rows, lat_size, lon_size, pt_ref, ps_ref, side_ref, near_in, core_in, far_in, t_new, s_new
 ):
     shape = (levels, LANES)
-    level = iota(shape, 0).astype(F32)
     lane = iota(shape, 1)
     place = lane % 4
     factors = level_factors(levels)
     K = levels
-    row_at = lax.axis_index("lat")
-    is_top, is_bottom = row_at == lat_size - 1, row_at == 0
+    is_top = lax.axis_index("lat") == lat_size - 1
     lon_at = lax.axis_index("lon")
     is_odd = lon_at % 2 == 1
     wraps = (lon_at == 0) | (lon_at == lon_size - 1)
-
-    def faces(cells, speeds):
-        wets = [level < jnp.minimum(a["n"], b["n"]) for a, b in zip(cells, cells[1:])]
-        d = [[face_step(a, b, w, q) for q in "ts"] for a, b, w in zip(cells, cells[1:], wets)]
-        limited = [[minmod(x, y) for x, y in zip(d[i], d[i + 1])] for i in (0, 1)]
-        base, wg, forward = face_base(cells[1], cells[2], speeds[1], wets[1], d[1])
-        flux = [b + wg * jnp.where(forward, x, y) for b, x, y in zip(base, *limited)]
-        first = last = None
-        if speeds[0] is not None:
-            _, wg0 = weights(speeds[0], wets[0])
-            first = [wg0 * jnp.where(speeds[0] > 0.0, 0.0, x) for x in limited[0]]
-        if speeds[2] is not None:
-            _, wg2 = weights(speeds[2], wets[2])
-            last = [wg2 * jnp.where(speeds[2] > 0.0, x, 0.0) for x in limited[1]]
-        return first, flux, last
 
     def cell_row(t, s, n):
         return column_row(t, s, n, factors, iota(shape, 0))
@@ -353,7 +351,7 @@
     def side(t, s, n, speed):
         row = cell_row(t, s, n)
         cells = [row] + [shifted(row, -i) for i in (1, 2, 3)]
-        return faces(cells, [roll(speed, -i) for i in range(3)])
+        return edge_faces(cells, [roll(speed, -i) for i in range(3)])
 
     _, west_flux, west_last = side(
         jnp.where(first_two, west[:K], own_t),
@@ -376,6 +374,42 @@
         )
         lon.append(group)
 
+    slot = iota((8, LANES), 0)
+    last = LANES // 4 - 1
+    own_lanes = [last - iota((8, LANES), 1) // 4 == slot + 8 * block for block in range(rows // 8)]
+    reverse = 4 * (last - lane // 4) + place
+    for q, (p_ref, new_ref) in enumerate(((pt_ref, t_new), (ps_ref, s_new))):
+        sides = jnp.take_along_axis(lon[q], reverse, axis=1)
+        for k in range(levels):
+            line = jnp.broadcast_to(sides[k : k + 1], (8, LANES))
+            for block, mine in enumerate(own_lanes):
+                moved = pltpu.roll(jnp.where(mine, line, 0.0), 32 * block + 2, 1, stride=4, stride_axis=0)
+                at = slice(8 * block, 8 * block + 8)
+                new_ref[k, at, :] = p_ref[k, at, :] + moved
+
+
+def latitude_kernel(
+    levels, rows, lat_size, lon_size, t_new, s_new, t_ref, s_ref, n_ref, own_ref,
+    far_in, below_in, above_in, column_in, relay_in, own_column, t_out, s_out, ends_ref, sems,
+):
+    shape = (levels, LANES)
+    factors = level_factors(levels)
+    K = levels
+    row_at = lax.axis_index("lat")
+    is_top, is_bottom = row_at == lat_size - 1, row_at == 0
+    lon_at = lax.axis_index("lon")
+    is_odd = lon_at % 2 == 1
+    middle = pl.ds(8, rows - 16)
+    copies = [
+        pltpu.make_async_copy(new_ref.at[:, middle], out_ref.at[:, middle], sems.at[q])
+        for q, (new_ref, out_ref) in enumerate(((t_new, t_out), (s_new, s_out)))
+    ]
+    for copy in copies:
+        copy.start()
+
+    def cell_row(t, s, n):
+        return column_row(t, s, n, factors, iota(shape, 0))
+
     counts = n_ref[...].astype(F32)
 
     def own_row(j):
@@ -387,7 +421,7 @@
 
     below = jnp.where(is_bottom, 0.0, below_in[...])
     cells = [sent_row(below, 0, 5 * K), sent_row(below, 1, 5 * K), own_row(0), own_row(1)]
-    _, south_flux, south_last = faces(cells, [None, below[4 * K : 5 * K], own_ref[:K]])
+    _, south_flux, south_last = edge_faces(cells, [None, below[4 * K : 5 * K], own_ref[:K]])
 
     pivot = (lon_at * 2) % lon_size == 0
     column = jnp.where(is_odd, relay_in[...], jnp.where(pivot, own_column[: K + 8, :], column_in[: K + 8, :]))
@@ -397,31 +431,26 @@
     above = above_in[...]
     above = jnp.where(is_top, fold, jnp.concatenate([above[: 4 * K], above[5 * K :]], axis=0))
     cells = [own_row(rows - 2), own_row(rows - 1), sent_row(above, 0, 4 * K), sent_row(above, 1, 4 * K)]
-    north_first, north_flux, _ = faces(cells, [own_ref[K : 2 * K], own_ref[2 * K :], None])
-
-    slot = iota((8, LANES), 0)
-    last = LANES // 4 - 1
-    own_lanes = [last - iota((8, LANES), 1) // 4 == slot + 8 * block for block in range(rows // 8)]
-    reverse = 4 * (last - lane // 4) + place
-    copies = []
-    for q, (p_ref, new_ref, out_ref) in enumerate(((pt_ref, t_new, t_out), (ps_ref, s_new, s_out))):
-        sides = jnp.take_along_axis(lon[q], reverse, axis=1)
-        for k in range(levels):
-            line = jnp.broadcast_to(sides[k : k + 1], (8, LANES))
-            for block, mine in enumerate(own_lanes):
-                moved = pltpu.roll(jnp.where(mine, line, 0.0), 32 * block + 2, 1, stride=4, stride_axis=0)
-                at = slice(8 * block, 8 * block + 8)
-                new_ref[k, at, :] = p_ref[k, at, :] + moved
+    north_first, north_flux, _ = edge_faces(cells, [own_ref[K : 2 * K], own_ref[2 * K :], None])
+
+    for q, (new_ref, out_ref) in enumerate(((t_new, t_out), (s_new, s_out))):
+        ends = ends_ref.at[q]
+        ends[:, :8, :] = new_ref[:, :8, :]
+        ends[:, 8:16, :] = new_ref[:, rows - 8 : rows, :]
         extra = {
             0: south_flux[q] - south_last[q],
             1: south_last[q],
-            rows - 2: -north_first[q],
-            rows - 1: north_first[q] - north_flux[q],
+            14: -north_first[q],
+            15: north_first[q] - north_flux[q],
         }
         for j, value in extra.items():
-            put(new_ref, j, strided(new_ref, j) + value)
-        copies.append(pltpu.make_async_copy(new_ref.at[:, :rows], out_ref, sems.at[q]))
-        copies[q].start()
+            put(ends, j, strided(ends, j) + value)
+        for i, at in enumerate((0, rows - 8)):
+            copy = pltpu.make_async_copy(
+                ends.at[:, pl.ds(8 * i, 8)], out_ref.at[:, pl.ds(at, 8)], sems.at[2 + 2 * q + i]
+            )
+            copy.start()
+            copies.append(copy)
     for copy in copies:
         copy.wait()
 
@@ -534,15 +563,26 @@
         name="interior_north",
     )(*fields, pt, ps, relay, state)
 
+    t_new, s_new = pl.pallas_call(
+        f(longitude_kernel, levels, rows, nlat, nlon),
+        out_shape=(room, room),
+        in_specs=[vmem] * 6,
+        out_specs=(vmem,) * 2,
+        input_output_aliases={0: 0, 1: 1},
+        cost_estimate=pl.CostEstimate(flops=5_000_000, bytes_accessed=1_000_000, transcendentals=0),
+        compiler_params=params,
+        name="longitude_edges",
+    )(pt, ps, side, near_in, core_in, far_in)
+
     return pl.pallas_call(
-        f(edge_kernel, levels, rows, nlat, nlon),
+        f(latitude_kernel, levels, rows, nlat, nlon),
         out_shape=(out(*t.shape),) * 2,
-        in_specs=[vmem] * 15,
+        in_specs=[vmem] * 12,
         out_specs=(hbm,) * 2,
-        scratch_shapes=[pltpu.VMEM(room.shape, F32)] * 2 + [pltpu.SemaphoreType.DMA((2,))],
-        compiler_params=params,
-        name="edge",
-    )(pt, ps, side, t_v, s_v, n_v, own, near_in, core_in, far_in, below_in, above_in, column_in, relay_in, column)
+        scratch_shapes=[pltpu.VMEM((2, K, 24, LANES), F32), pltpu.SemaphoreType.DMA((6,))],
+        compiler_params=params,
+        name="latitude_edges",
+    )(t_new, s_new, t_v, s_v, n_v, own, far_in, below_in, above_in, column_in, relay_in, column)
 
 
 def solution(mesh):

time: 13.2 us -> 12.8 us (0.970)
  waiting for transfers between devices: 0.58 us -> 0.02 us
  Pallas kernels: 4.59 us -> 4.75 us
    ppermute x1, waiting for transfers between devices: 0.56 us -> 0.01 us  [body(): lax.ppermute(lat, 'lat', [(i, (i + 1) % nlat) for i in rung])]
    pallas_call x1 -> x2, Pallas kernels: 1.3 us -> 1.47 us  [the longest x1 0.88 us: body(): pl.pallas_call(f(latitude_kernel, levels, rows, nlat, nlon), out_shape=(o...]
  transfers between devices with their start and end apart: 6 -> 6, of which waited for: 1 -> 0; matrix products, arithmetic and copies ran while one was open for 0% -> 0% of each run, Pallas kernels for 7% -> 12%
where the time goes in v6:
time: 12.8 us; the launch traced here: 12.7 us
  starting transfers between devices  7.21 us (56%)
  Pallas kernels  4.75 us (37%)
  between operations  0.71 us (6%)
    ppermute x3, starting transfers between devices, exchange(): return lax.ppermute(array, ('lon', 'lat'), pairs)  5.18 us
    pallas_call x1, Pallas kernels, body(): pl.pallas_call(f(pack_kernel, levels, rows, nlat), out_shape=tuple(shapes...  1.56 us
    ppermute x1, starting transfers between devices, body(): lax.ppermute(lat, 'lat', [(i, (i + 1) % nlat) for i in rung])  1.52 us
    pallas_call x1, Pallas kernels, body(): pl.pallas_call(f(latitude_kernel, levels, rows, nlat, nlon), out_shape=(o...  0.88 us
    pallas_call x1, Pallas kernels, body(): pl.pallas_call(f(south_kernel, levels, rows, middle, True), out_shape=sou...  0.83 us
    pallas_call x1, Pallas kernels, body(): pl.pallas_call(f(interior_kernel, levels, rows, middle, rows), out_shape=...  0.82 us
    pallas_call x1, Pallas kernels, body(): pl.pallas_call(f(longitude_kernel, levels, rows, nlat, nlon), out_shape=(...  0.59 us
    ppermute x1, starting transfers between devices, body(): core_in = lax.ppermute(core, 'lon', [(i, i ^ 1) for i in ring])  0.4 us
  transfers between devices with their start and end apart: 6, of which 0 were waited for; matrix products, arithmetic and copies ran while one was open for 0% of the time, Pallas kernels for 12%

profile of v6, /device:TPU:0, one launch (start us, length us, event | category | flops | bytes accessed | tf_op | source)
XLA Modules:
  0.0 12.7 jit_solution(1564195323024785970)
XLA Ops:
  0.6 1.6 %pack.1 = (f32[16,40,128]{2,1,0:T(8,128)S(1)}, f32[16,40,128]{2,1,0:T(8,128)S(1)}, f32[16,40,128]{2,1,0:T(8,128)S(1)}, f32[16,40,128]{2,1,0:T(8,128)S(1)}, s32[3...) custom-call(f32[16,32,128]{2,1,0:T(8,128)} %t_hbm.1, ...), custom_call_target="tpu_custom_call" | custom-call | tf_op jit(solution)/shard_map/pack/pallas_call | solution.py:472
  2.2 0.8 %south_at_origin.1 = (f32[16,40,128]{2,1,0:T(8,128)S(1)}, f32[16,40,128]{2,1,0:T(8,128)S(1)}, f32[19,16,128]{2,1,0:T(8,128)S(1)}, f32[104,128]{1,0:T(8,128)S(1)}) custom-call(f32[16,40,128]{2,1,0:T(8,128)S(1)} %get-tuple-element.25.t_ref, f32[16,40,128]{2,1,0:T(8,128)S(1)} %get-tuple-element.26.s_ref, ...), custom_call_target="tpu_custom_call", output_to_operand_aliasing={{3}: (5, {})} | custom-call | flops 20000000 | bytes 1000000 | tf_op jit(solution)/shard_map/south_at_origin/pallas_call | solution.py:510
  3.0 4.7 %collective-permute-start = (f32[104,128]{1,0:T(8,128)S(1)}, f32[104,128]{1,0:T(8,128)S(1)}, u32[]{:S(2)}, u32[]{:S(2)}) collective-permute-start(f32[104,128]{1,0:T(8,128)S(1)} %get-tuple-element.36), channel_id=1, source_target_pairs={{0,30},{1,31},{2,4},{3,29},{4,2},{5,27},{6,8},{7,25},{8,6},{9,23},... | collective-permute-start | bytes 159752 | tf_op jit(solution)/shard_map/ppermute | solution.py:495
  7.7 1.5 %collective-permute-start.3 = (f32[88,128]{1,0:T(8,128)S(1)}, f32[88,128]{1,0:T(8,128)S(1)}, u32[]{:S(2)}, u32[]{:S(2)}) collective-permute-start(f32[88,128]{1,0:T(8,128)S(1)} %get-tuple-element.46), channel_id=1, source_target_pairs={{0,1},{1,0},{2,3},{3,2},{4,5},{5,4},{6,7},{7,6},{8,9},{9,8},{10,11... | collective-permute-start | bytes 135176 | tf_op jit(solution)/shard_map/ppermute | solution.py:523
  9.2 0.4 %collective-permute-start.4 = (f32[40,128]{1,0:T(8,128)S(1)}, f32[40,128]{1,0:T(8,128)S(1)}, u32[]{:S(2)}, u32[]{:S(2)}) collective-permute-start(f32[40,128]{1,0:T(8,128)S(1)} %get-tuple-element.47.own_column), channel_id=1, source_target_pairs={{0,2},{1,3},{2,0},{3,1},{4,6},{5,29},{6,4},{7,11},{8,10},{9,25},{1... | collective-permute-start | bytes 61448 | tf_op jit(solution)/shard_map/ppermute | solution.py:495
  9.6 0.1 collective-permute-start.1
  9.7 0.4 %collective-permute-start.2 = (f32[32,128]{1,0:T(8,128)S(1)}, f32[32,128]{1,0:T(8,128)S(1)}, u32[]{:S(2)}, u32[]{:S(2)}) collective-permute-start(f32[32,128]{1,0:T(8,128)S(1)} %get-tuple-element.42), channel_id=1, source_target_pairs={{0,2},{2,0},{4,6},{6,4},{8,10},{10,8},{12,14},{14,12},{16,18},{18,... | collective-permute-start | bytes 49160 | tf_op jit(solution)/shard_map/ppermute | solution.py:532
  10.1 0.0 collective-permute-done.far_ref.far_in
  10.1 0.1 relay.1.more_2_
  10.2 0.1 collective-permute-start.5
  10.3 0.8 %interior_north.1 = (f32[16,40,128]{2,1,0:T(8,128)S(1)}, f32[16,40,128]{2,1,0:T(8,128)S(1)}) custom-call(f32[16,40,128]{2,1,0:T(8,128)S(1)} %get-tuple-element.25.t_ref, f32[16,40,128]{2,1,0:T(8,128)S(1)} %get-tuple-element.26.s_ref, f32[16,40,128]{2,1,0:T(8,128)S(1)} %get-tuple-element.27.c_ref, ...), custom_call_target="tpu_custom_call", output_to_operand_aliasing={{0}: (5, {}), {1}: (6, {})} | custom-call | flops 20000000 | bytes 1000000 | tf_op jit(solution)/shard_map/interior_north/pallas_call | solution.py:555
  11.2 0.0 collective-permute-done.1.near_in
  11.2 0.0 collective-permute-done.2.core_in
  11.2 0.6 %longitude_edges.1 = (f32[16,40,128]{2,1,0:T(8,128)S(1)}, f32[16,40,128]{2,1,0:T(8,128)S(1)}) custom-call(f32[16,40,128]{2,1,0:T(8,128)S(1)} %get-tuple-element.38.pt_ref, f32[16,40,128]{2,1,0:T(8,128)S(1)} %get-tuple-element.39.ps_ref, f32[56,128]{1,0:T(8,128)S(1)} %get-tuple-element.40.side_ref, ...), custom_call_target="tpu_custom_call", output_to_operand_aliasing={{0}: (0, {}), {1}: (1, {})} | custom-call | flops 5000000 | bytes 1000000 | tf_op jit(solution)/shard_map/longitude_edges/pallas_call | solution.py:566
  11.8 0.0 collective-permute-done.4.column_in
  11.8 0.0 collective-permute-done.3.below_in.above_in
  11.8 0.0 collective-permute-done.5.relay_in
  11.8 0.9 %latitude_edges.1 = (f32[16,32,128]{2,1,0:T(8,128)}, f32[16,32,128]{2,1,0:T(8,128)}) custom-call(f32[16,40,128]{2,1,0:T(8,128)S(1)} %get-tuple-element.43.t_new, f32[16,40,128]{2,1,0:T(8,128)S(1)} %get-tuple-element.44.s_new, f32[16,40,128]{2,1,0:T(8,128)S(1)} %get-tuple-element.25.t_ref, f32[16,40,128]{2,1,0:T(8,128)S(1)} %get-tuple-element.26.s_ref, ...), custom_call_target="tpu_custom_call" | custom-call | tf_op jit(solution)/shard_map/latitude_edges/pallas_call | solution.py:577
  (1 shorter events, 0.0 us)
Async XLA Ops:
  3.0 7.1 %collective-permute-start = (f32[104,128]{1,0:T(8,128)S(1)}, f32[104,128]{1,0:T(8,128)S(1)}, u32[]{:S(2)}, u32[]{:S(2)}) collective-permute-start(f32[104,128]{1,0:T(8,128)S(1)} %get-tuple-element.36), channel_id=1, source_target_pairs={{0,30},{1,31},{2,4},{3,29},{4,2},{5,27},{6,8},{7,25},{8,6},{9,23},... | collective-permute-start | bytes 159752 | tf_op jit(solution)/shard_map/ppermute | solution.py:495
  7.7 4.1 %collective-permute-start.3 = (f32[88,128]{1,0:T(8,128)S(1)}, f32[88,128]{1,0:T(8,128)S(1)}, u32[]{:S(2)}, u32[]{:S(2)}) collective-permute-start(f32[88,128]{1,0:T(8,128)S(1)} %get-tuple-element.46), channel_id=1, source_target_pairs={{0,1},{1,0},{2,3},{3,2},{4,5},{5,4},{6,7},{7,6},{8,9},{9,8},{10,11... | collective-permute-start | bytes 135176 | tf_op jit(solution)/shard_map/ppermute | solution.py:523
  9.2 2.5 %collective-permute-start.4 = (f32[40,128]{1,0:T(8,128)S(1)}, f32[40,128]{1,0:T(8,128)S(1)}, u32[]{:S(2)}, u32[]{:S(2)}) collective-permute-start(f32[40,128]{1,0:T(8,128)S(1)} %get-tuple-element.47.own_column), channel_id=1, source_target_pairs={{0,2},{1,3},{2,0},{3,1},{4,6},{5,29},{6,4},{7,11},{8,10},{9,25},{1... | collective-permute-start | bytes 61448 | tf_op jit(solution)/shard_map/ppermute | solution.py:495
  9.6 1.5 %collective-permute-start.1 = (f32[32,128]{1,0:T(8,128)S(1)}, f32[32,128]{1,0:T(8,128)S(1)}, u32[]{:S(2)}, u32[]{:S(2)}) collective-permute-start(f32[32,128]{1,0:T(8,128)S(1)} %get-tuple-element.41), channel_id=1, source_target_pairs={{0,2},{1,8},{2,0},{3,5},{4,6},{5,3},{6,4},{7,9},{8,10},{9,7},{10,1... | collective-permute-start | bytes 49160 | tf_op jit(solution)/shard_map/ppermute | solution.py:495
  9.7 1.4 %collective-permute-start.2 = (f32[32,128]{1,0:T(8,128)S(1)}, f32[32,128]{1,0:T(8,128)S(1)}, u32[]{:S(2)}, u32[]{:S(2)}) collective-permute-start(f32[32,128]{1,0:T(8,128)S(1)} %get-tuple-element.42), channel_id=1, source_target_pairs={{0,2},{2,0},{4,6},{6,4},{8,10},{10,8},{12,14},{14,12},{16,18},{18,... | collective-permute-start | bytes 49160 | tf_op jit(solution)/shard_map/ppermute | solution.py:532
  10.2 1.6 %collective-permute-start.5 = (f32[24,128]{1,0:T(8,128)S(1)}, f32[24,128]{1,0:T(8,128)S(1)}, u32[]{:S(2)}, u32[]{:S(2)}) collective-permute-start(f32[24,128]{1,0:T(8,128)S(1)} %relay.1.more_2_), channel_id=1, source_target_pairs={{0,2},{2,0},{4,6},{6,4},{8,10},{10,8},{12,14},{14,12},{16,18},{18,... | collective-permute-start | bytes 36872 | tf_op jit(solution)/shard_map/ppermute | solution.py:553

commit v7 on v6

--- a/solution.py
+++ b/solution.py
@@ -21,7 +21,7 @@
 LANES = 128
 VMEM = 8 * 1024 * 1024
 UNROLL = 8
-HEAD = 16
+HEAD = 24
 SPARE = 8
 F32 = jnp.float32
 
@@ -124,24 +124,13 @@
     lane = iota((levels, LANES), 1)
     group = lane // 4
 
-    slot = iota((8, LANES), 0)
-    own = [iota((8, LANES), 1) // 4 == slot + 8 * block for block in range(rows // 8)]
+    group = lane // 4
 
     def gather(ref):
-        tiles = []
-        for base in range(0, K, 8):
-            out = jnp.zeros((8, LANES), F32)
-            for k in range(8):
-                spread = jnp.zeros((8, LANES), F32)
-                for block, mine in enumerate(own):
-                    eight = ref[base + k, 8 * block : 8 * block + 8, :]
-                    moved = pltpu.roll(eight, 32 * block + 2, 1, stride=4, stride_axis=0)
-                    spread = jnp.where(mine, moved, spread)
-                for by in (4, 2, 1):
-                    spread = spread + roll(spread, by, 0)
-                out = jnp.where(slot == k, spread, out)
-            tiles.append(out)
-        return jnp.concatenate(tiles, axis=0)
+        out = jnp.zeros((levels, LANES), F32)
+        for j in range(rows):
+            out = jnp.where(group == j, roll(strided(ref, j), 4 * j + 2), out)
+        return out
 
     def mirrored(x):
         index = (LANES - iota(x.shape, 1)) % LANES
@@ -374,18 +363,11 @@
         )
         lon.append(group)
 
-    slot = iota((8, LANES), 0)
-    last = LANES // 4 - 1
-    own_lanes = [last - iota((8, LANES), 1) // 4 == slot + 8 * block for block in range(rows // 8)]
-    reverse = 4 * (last - lane // 4) + place
+    edge_lanes = (lane >= LANES - 2) | (lane < 2)
     for q, (p_ref, new_ref) in enumerate(((pt_ref, t_new), (ps_ref, s_new))):
-        sides = jnp.take_along_axis(lon[q], reverse, axis=1)
-        for k in range(levels):
-            line = jnp.broadcast_to(sides[k : k + 1], (8, LANES))
-            for block, mine in enumerate(own_lanes):
-                moved = pltpu.roll(jnp.where(mine, line, 0.0), 32 * block + 2, 1, stride=4, stride_axis=0)
-                at = slice(8 * block, 8 * block + 8)
-                new_ref[k, at, :] = p_ref[k, at, :] + moved
+        for j in range(rows):
+            moved = jnp.where(edge_lanes, roll(lon[q], LANES - 2 - 4 * j), 0.0)
+            put(new_ref, j, strided(p_ref, j) + moved)
 
 
 def latitude_kernel(

time: 12.8 us -> 12.8 us (level)
  waiting for transfers between devices: 0.02 us -> 0.45 us
  starting transfers between devices: 7.21 us -> 6.81 us
    pallas_call x1, Pallas kernels: 0.82 us -> 0.41 us  [body(): pl.pallas_call(f(interior_kernel, levels, rows, middle, rows), out_shape=...]
    ppermute x3, starting transfers between devices: 5.18 us -> 4.78 us  [exchange(): return lax.ppermute(array, ('lon', 'lat'), pairs)]
    pallas_call x1, Pallas kernels: 0.83 us -> 1.23 us  [body(): pl.pallas_call(f(south_kernel, levels, rows, middle, True), out_shape=sou...]
    ppermute x1, waiting for transfers between devices: 0.01 us -> 0.22 us  [body(): lax.ppermute(lat, 'lat', [(i, (i + 1) % nlat) for i in rung])]
    ppermute x1, waiting for transfers between devices: 0.01 us -> 0.17 us  [body(): core_in = lax.ppermute(core, 'lon', [(i, i ^ 1) for i in ring])]
  transfers between devices with their start and end apart: 6 -> 6, of which waited for: 0 -> 3; matrix products, arithmetic and copies ran while one was open for 0% -> 0% of each run, Pallas kernels for 12% -> 8%
where the time goes in v7:
time: 12.8 us; the launch traced here: 12.6 us
  starting transfers between devices  6.81 us (53%)
  Pallas kernels  4.68 us (37%)
  between operations  0.68 us (5%)
  waiting for transfers between devices  0.45 us (4%)
    ppermute x3, starting transfers between devices, exchange(): return lax.ppermute(array, ('lon', 'lat'), pairs)  4.78 us
    pallas_call x1, Pallas kernels, body(): pl.pallas_call(f(pack_kernel, levels, rows, nlat), out_shape=tuple(shapes...  1.55 us
    ppermute x1, starting transfers between devices, body(): lax.ppermute(lat, 'lat', [(i, (i + 1) % nlat) for i in rung])  1.52 us
    pallas_call x1, Pallas kernels, body(): pl.pallas_call(f(south_kernel, levels, rows, middle, True), out_shape=sou...  1.23 us
    pallas_call x1, Pallas kernels, body(): pl.pallas_call(f(latitude_kernel, levels, rows, nlat, nlon), out_shape=(o...  0.87 us
    pallas_call x1, Pallas kernels, body(): pl.pallas_call(f(longitude_kernel, levels, rows, nlat, nlon), out_shape=(...  0.54 us
    pallas_call x1, Pallas kernels, body(): pl.pallas_call(f(interior_kernel, levels, rows, middle, rows), out_shape=...  0.41 us
    ppermute x1, starting transfers between devices, body(): core_in = lax.ppermute(core, 'lon', [(i, i ^ 1) for i in ring])  0.4 us
  transfers between devices with their start and end apart: 6, of which 3 were waited for; matrix products, arithmetic and copies ran while one was open for 0% of the time, Pallas kernels for 8%

profile of v7, /device:TPU:0, one launch (start us, length us, event | category | flops | bytes accessed | tf_op | source)
XLA Modules:
  0.0 12.6 jit_solution(4682266198747722287)
XLA Ops:
  0.6 1.6 %pack.1 = (f32[16,40,128]{2,1,0:T(8,128)S(1)}, f32[16,40,128]{2,1,0:T(8,128)S(1)}, f32[16,40,128]{2,1,0:T(8,128)S(1)}, f32[16,40,128]{2,1,0:T(8,128)S(1)}, s32[3...) custom-call(f32[16,32,128]{2,1,0:T(8,128)} %t_hbm.1, ...), custom_call_target="tpu_custom_call" | custom-call | tf_op jit(solution)/shard_map/pack/pallas_call | solution.py:454
  2.2 1.2 %south_at_origin.1 = (f32[16,40,128]{2,1,0:T(8,128)S(1)}, f32[16,40,128]{2,1,0:T(8,128)S(1)}, f32[19,16,128]{2,1,0:T(8,128)S(1)}, f32[104,128]{1,0:T(8,128)S(1)}) custom-call(f32[16,40,128]{2,1,0:T(8,128)S(1)} %get-tuple-element.25.t_ref, f32[16,40,128]{2,1,0:T(8,128)S(1)} %get-tuple-element.26.s_ref, ...), custom_call_target="tpu_custom_call", output_to_operand_aliasing={{3}: (5, {})} | custom-call | flops 20000000 | bytes 1000000 | tf_op jit(solution)/shard_map/south_at_origin/pallas_call | solution.py:492
  3.4 4.3 %collective-permute-start = (f32[104,128]{1,0:T(8,128)S(1)}, f32[104,128]{1,0:T(8,128)S(1)}, u32[]{:S(2)}, u32[]{:S(2)}) collective-permute-start(f32[104,128]{1,0:T(8,128)S(1)} %get-tuple-element.36), channel_id=1, source_target_pairs={{0,30},{1,31},{2,4},{3,29},{4,2},{5,27},{6,8},{7,25},{8,6},{9,23},... | collective-permute-start | bytes 159752 | tf_op jit(solution)/shard_map/ppermute | solution.py:477
  7.7 1.5 %collective-permute-start.3 = (f32[88,128]{1,0:T(8,128)S(1)}, f32[88,128]{1,0:T(8,128)S(1)}, u32[]{:S(2)}, u32[]{:S(2)}) collective-permute-start(f32[88,128]{1,0:T(8,128)S(1)} %get-tuple-element.46), channel_id=1, source_target_pairs={{0,1},{1,0},{2,3},{3,2},{4,5},{5,4},{6,7},{7,6},{8,9},{9,8},{10,11... | collective-permute-start | bytes 135176 | tf_op jit(solution)/shard_map/ppermute | solution.py:505
  9.2 0.4 %collective-permute-start.4 = (f32[40,128]{1,0:T(8,128)S(1)}, f32[40,128]{1,0:T(8,128)S(1)}, u32[]{:S(2)}, u32[]{:S(2)}) collective-permute-start(f32[40,128]{1,0:T(8,128)S(1)} %get-tuple-element.47.own_column), channel_id=1, source_target_pairs={{0,2},{1,3},{2,0},{3,1},{4,6},{5,29},{6,4},{7,11},{8,10},{9,25},{1... | collective-permute-start | bytes 61448 | tf_op jit(solution)/shard_map/ppermute | solution.py:477
  9.6 0.1 collective-permute-start.1
  9.7 0.4 %collective-permute-start.2 = (f32[32,128]{1,0:T(8,128)S(1)}, f32[32,128]{1,0:T(8,128)S(1)}, u32[]{:S(2)}, u32[]{:S(2)}) collective-permute-start(f32[32,128]{1,0:T(8,128)S(1)} %get-tuple-element.42), channel_id=1, source_target_pairs={{0,2},{2,0},{4,6},{6,4},{8,10},{10,8},{12,14},{14,12},{16,18},{18,... | collective-permute-start | bytes 49160 | tf_op jit(solution)/shard_map/ppermute | solution.py:514
  10.1 0.0 collective-permute-done.far_ref.far_in
  10.1 0.1 relay.1.more_2_
  10.2 0.1 collective-permute-start.5
  10.3 0.4 %interior_north.1 = (f32[16,40,128]{2,1,0:T(8,128)S(1)}, f32[16,40,128]{2,1,0:T(8,128)S(1)}) custom-call(f32[16,40,128]{2,1,0:T(8,128)S(1)} %get-tuple-element.25.t_ref, f32[16,40,128]{2,1,0:T(8,128)S(1)} %get-tuple-element.26.s_ref, f32[16,40,128]{2,1,0:T(8,128)S(1)} %get-tuple-element.27.c_ref, ...), custom_call_target="tpu_custom_call", output_to_operand_aliasing={{0}: (5, {}), {1}: (6, {})} | custom-call | flops 20000000 | bytes 1000000 | tf_op jit(solution)/shard_map/interior_north/pallas_call | solution.py:537
  10.7 0.1 collective-permute-done.1.near_in
  10.8 0.2 %collective-permute-done.2.core_in = f32[32,128]{1,0:T(8,128)S(1)} collective-permute-done((f32[32,128]{1,0:T(8,128)S(1)}, f32[32,128]{1,0:T(8,128)S(1)}, u32[]{:S(2)}, u32[]{:S(2)}) %collective-permute-start.2) | collective-permute-done | bytes 16416 | tf_op jit(solution)/shard_map/ppermute | solution.py:514
  11.0 0.5 %longitude_edges.1 = (f32[16,40,128]{2,1,0:T(8,128)S(1)}, f32[16,40,128]{2,1,0:T(8,128)S(1)}) custom-call(f32[16,40,128]{2,1,0:T(8,128)S(1)} %get-tuple-element.38.pt_ref, f32[16,40,128]{2,1,0:T(8,128)S(1)} %get-tuple-element.39.ps_ref, f32[56,128]{1,0:T(8,128)S(1)} %get-tuple-element.40.side_ref, ...), custom_call_target="tpu_custom_call", output_to_operand_aliasing={{0}: (0, {}), {1}: (1, {})} | custom-call | flops 5000000 | bytes 1000000 | tf_op jit(solution)/shard_map/longitude_edges/pallas_call | solution.py:548
  11.5 0.0 collective-permute-done.4.column_in
  11.5 0.2 %collective-permute-done.3.below_in.above_in = f32[88,128]{1,0:T(8,128)S(1)} collective-permute-done((f32[88,128]{1,0:T(8,128)S(1)}, f32[88,128]{1,0:T(8,128)S(1)}, u32[]{:S(2)}, u32[]{:S(2)}) %collective-permute-start.3) | collective-permute-done | bytes 45088 | tf_op jit(solution)/shard_map/ppermute | solution.py:505
  11.7 0.0 collective-permute-done.5.relay_in
  11.8 0.9 %latitude_edges.1 = (f32[16,32,128]{2,1,0:T(8,128)}, f32[16,32,128]{2,1,0:T(8,128)}) custom-call(f32[16,40,128]{2,1,0:T(8,128)S(1)} %get-tuple-element.43.t_new, f32[16,40,128]{2,1,0:T(8,128)S(1)} %get-tuple-element.44.s_new, f32[16,40,128]{2,1,0:T(8,128)S(1)} %get-tuple-element.25.t_ref, f32[16,40,128]{2,1,0:T(8,128)S(1)} %get-tuple-element.26.s_ref, ...), custom_call_target="tpu_custom_call" | custom-call | tf_op jit(solution)/shard_map/latitude_edges/pallas_call | solution.py:559
  (1 shorter events, 0.0 us)
Async XLA Ops:
  3.4 6.7 %collective-permute-start = (f32[104,128]{1,0:T(8,128)S(1)}, f32[104,128]{1,0:T(8,128)S(1)}, u32[]{:S(2)}, u32[]{:S(2)}) collective-permute-start(f32[104,128]{1,0:T(8,128)S(1)} %get-tuple-element.36), channel_id=1, source_target_pairs={{0,30},{1,31},{2,4},{3,29},{4,2},{5,27},{6,8},{7,25},{8,6},{9,23},... | collective-permute-start | bytes 159752 | tf_op jit(solution)/shard_map/ppermute | solution.py:477
  7.7 4.0 %collective-permute-start.3 = (f32[88,128]{1,0:T(8,128)S(1)}, f32[88,128]{1,0:T(8,128)S(1)}, u32[]{:S(2)}, u32[]{:S(2)}) collective-permute-start(f32[88,128]{1,0:T(8,128)S(1)} %get-tuple-element.46), channel_id=1, source_target_pairs={{0,1},{1,0},{2,3},{3,2},{4,5},{5,4},{6,7},{7,6},{8,9},{9,8},{10,11... | collective-permute-start | bytes 135176 | tf_op jit(solution)/shard_map/ppermute | solution.py:505
  9.2 2.3 %collective-permute-start.4 = (f32[40,128]{1,0:T(8,128)S(1)}, f32[40,128]{1,0:T(8,128)S(1)}, u32[]{:S(2)}, u32[]{:S(2)}) collective-permute-start(f32[40,128]{1,0:T(8,128)S(1)} %get-tuple-element.47.own_column), channel_id=1, source_target_pairs={{0,2},{1,3},{2,0},{3,1},{4,6},{5,29},{6,4},{7,11},{8,10},{9,25},{1... | collective-permute-start | bytes 61448 | tf_op jit(solution)/shard_map/ppermute | solution.py:477
  9.6 1.2 %collective-permute-start.1 = (f32[32,128]{1,0:T(8,128)S(1)}, f32[32,128]{1,0:T(8,128)S(1)}, u32[]{:S(2)}, u32[]{:S(2)}) collective-permute-start(f32[32,128]{1,0:T(8,128)S(1)} %get-tuple-element.41), channel_id=1, source_target_pairs={{0,2},{1,8},{2,0},{3,5},{4,6},{5,3},{6,4},{7,9},{8,10},{9,7},{10,1... | collective-permute-start | bytes 49160 | tf_op jit(solution)/shard_map/ppermute | solution.py:477
  9.7 1.2 %collective-permute-start.2 = (f32[32,128]{1,0:T(8,128)S(1)}, f32[32,128]{1,0:T(8,128)S(1)}, u32[]{:S(2)}, u32[]{:S(2)}) collective-permute-start(f32[32,128]{1,0:T(8,128)S(1)} %get-tuple-element.42), channel_id=1, source_target_pairs={{0,2},{2,0},{4,6},{6,4},{8,10},{10,8},{12,14},{14,12},{16,18},{18,... | collective-permute-start | bytes 49160 | tf_op jit(solution)/shard_map/ppermute | solution.py:514
  10.2 1.5 %collective-permute-start.5 = (f32[24,128]{1,0:T(8,128)S(1)}, f32[24,128]{1,0:T(8,128)S(1)}, u32[]{:S(2)}, u32[]{:S(2)}) collective-permute-start(f32[24,128]{1,0:T(8,128)S(1)} %relay.1.more_2_), channel_id=1, source_target_pairs={{0,2},{2,0},{4,6},{6,4},{8,10},{10,8},{12,14},{14,12},{16,18},{18,... | collective-permute-start | bytes 36872 | tf_op jit(solution)/shard_map/ppermute | solution.py:535

commit v8 on v7

--- a/solution.py
+++ b/solution.py
@@ -315,7 +315,7 @@
 
 
 def longitude_kernel(
-    levels, rows, lat_size, lon_size, pt_ref, ps_ref, side_ref, near_in, core_in, far_in, t_new, s_new
+    levels, rows, lat_size, lon_size, pt_ref, ps_ref, side_ref, near_in, core_in, far_in, t_new, s_new, ends_ref
 ):
     shape = (levels, LANES)
     lane = iota(shape, 1)
@@ -367,11 +367,17 @@
     for q, (p_ref, new_ref) in enumerate(((pt_ref, t_new), (ps_ref, s_new))):
         for j in range(rows):
             moved = jnp.where(edge_lanes, roll(lon[q], LANES - 2 - 4 * j), 0.0)
-            put(new_ref, j, strided(p_ref, j) + moved)
+            value = strided(p_ref, j) + moved
+            if j < 8:
+                put(ends_ref.at[q], j, value)
+            elif j >= rows - 8:
+                put(ends_ref.at[q], j - rows + 16, value)
+            else:
+                put(new_ref, j, value)
 
 
 def latitude_kernel(
-    levels, rows, lat_size, lon_size, t_new, s_new, t_ref, s_ref, n_ref, own_ref,
+    levels, rows, lat_size, lon_size, t_new, s_new, _, t_ref, s_ref, n_ref, own_ref,
     far_in, below_in, above_in, column_in, relay_in, own_column, t_out, s_out, ends_ref, sems,
 ):
     shape = (levels, LANES)
@@ -415,10 +421,8 @@
     cells = [own_row(rows - 2), own_row(rows - 1), sent_row(above, 0, 4 * K), sent_row(above, 1, 4 * K)]
     north_first, north_flux, _ = edge_faces(cells, [own_ref[K : 2 * K], own_ref[2 * K :], None])
 
-    for q, (new_ref, out_ref) in enumerate(((t_new, t_out), (s_new, s_out))):
+    for q, out_ref in enumerate((t_out, s_out)):
         ends = ends_ref.at[q]
-        ends[:, :8, :] = new_ref[:, :8, :]
-        ends[:, 8:16, :] = new_ref[:, rows - 8 : rows, :]
         extra = {
             0: south_flux[q] - south_last[q],
             1: south_last[q],
@@ -545,26 +549,29 @@
         name="interior_north",
     )(*fields, pt, ps, relay, state)
 
-    t_new, s_new = pl.pallas_call(
+    ends = out(2, K, 24, LANES)
+    t_new, s_new, ends_new = pl.pallas_call(
         f(longitude_kernel, levels, rows, nlat, nlon),
-        out_shape=(room, room),
+        out_shape=(room, room, ends),
         in_specs=[vmem] * 6,
-        out_specs=(vmem,) * 2,
+        out_specs=(vmem,) * 3,
         input_output_aliases={0: 0, 1: 1},
         cost_estimate=pl.CostEstimate(flops=5_000_000, bytes_accessed=1_000_000, transcendentals=0),
         compiler_params=params,
         name="longitude_edges",
     )(pt, ps, side, near_in, core_in, far_in)
 
-    return pl.pallas_call(
+    t_next, s_next, _ = pl.pallas_call(
         f(latitude_kernel, levels, rows, nlat, nlon),
-        out_shape=(out(*t.shape),) * 2,
-        in_specs=[vmem] * 12,
-        out_specs=(hbm,) * 2,
-        scratch_shapes=[pltpu.VMEM((2, K, 24, LANES), F32), pltpu.SemaphoreType.DMA((6,))],
+        out_shape=(out(*t.shape), out(*t.shape), ends),
+        in_specs=[vmem] * 13,
+        out_specs=(hbm, hbm, vmem),
+        input_output_aliases={2: 2},
+        scratch_shapes=[pltpu.SemaphoreType.DMA((6,))],
         compiler_params=params,
         name="latitude_edges",
-    )(t_new, s_new, t_v, s_v, n_v, own, far_in, below_in, above_in, column_in, relay_in, column)
+    )(t_new, s_new, ends_new, t_v, s_v, n_v, own, far_in, below_in, above_in, column_in, relay_in, column)
+    return t_next, s_next
 
 
 def solution(mesh):

time: 12.8 us -> 12.8 us (level)
  no operation moved by 1% of the time
where the time goes in v8:
time: 12.8 us; the launch traced here: 12.6 us
  starting transfers between devices  6.81 us (53%)
  Pallas kernels  4.65 us (36%)
  between operations  0.68 us (5%)
  waiting for transfers between devices  0.47 us (4%)
    ppermute x3, starting transfers between devices, exchange(): return lax.ppermute(array, ('lon', 'lat'), pairs)  4.78 us
    pallas_call x1, Pallas kernels, body(): pl.pallas_call(f(pack_kernel, levels, rows, nlat), out_shape=tuple(shapes...  1.55 us
    ppermute x1, starting transfers between devices, body(): lax.ppermute(lat, 'lat', [(i, (i + 1) % nlat) for i in rung])  1.52 us
    pallas_call x1, Pallas kernels, body(): pl.pallas_call(f(south_kernel, levels, rows, middle, True), out_shape=sou...  1.23 us
    pallas_call x1, Pallas kernels, body(): pl.pallas_call(f(latitude_kernel, levels, rows, nlat, nlon), out_shape=(o...  0.86 us
    pallas_call x1, Pallas kernels, body(): pl.pallas_call(f(longitude_kernel, levels, rows, nlat, nlon), out_shape=(...  0.52 us
    pallas_call x1, Pallas kernels, body(): pl.pallas_call(f(interior_kernel, levels, rows, middle, rows), out_shape=...  0.41 us
    ppermute x1, starting transfers between devices, body(): core_in = lax.ppermute(core, 'lon', [(i, i ^ 1) for i in ring])  0.4 us
  transfers between devices with their start and end apart: 6, of which 3 were waited for; matrix products, arithmetic and copies ran while one was open for 0% of the time, Pallas kernels for 8%

profile of v8, /device:TPU:0, one launch (start us, length us, event | category | flops | bytes accessed | tf_op | source)
XLA Modules:
  0.0 12.6 jit_solution(5859921909604125873)
XLA Ops:
  0.6 1.6 %pack.1 = (f32[16,40,128]{2,1,0:T(8,128)S(1)}, f32[16,40,128]{2,1,0:T(8,128)S(1)}, f32[16,40,128]{2,1,0:T(8,128)S(1)}, f32[16,40,128]{2,1,0:T(8,128)S(1)}, s32[3...) custom-call(f32[16,32,128]{2,1,0:T(8,128)} %t_hbm.1, ...), custom_call_target="tpu_custom_call" | custom-call | tf_op jit(solution)/shard_map/pack/pallas_call | solution.py:458
  2.2 1.2 %south_at_origin.1 = (f32[16,40,128]{2,1,0:T(8,128)S(1)}, f32[16,40,128]{2,1,0:T(8,128)S(1)}, f32[19,16,128]{2,1,0:T(8,128)S(1)}, f32[104,128]{1,0:T(8,128)S(1)}) custom-call(f32[16,40,128]{2,1,0:T(8,128)S(1)} %get-tuple-element.28.t_ref, f32[16,40,128]{2,1,0:T(8,128)S(1)} %get-tuple-element.29.s_ref, ...), custom_call_target="tpu_custom_call", output_to_operand_aliasing={{3}: (5, {})} | custom-call | flops 20000000 | bytes 1000000 | tf_op jit(solution)/shard_map/south_at_origin/pallas_call | solution.py:496
  3.4 4.3 %collective-permute-start = (f32[104,128]{1,0:T(8,128)S(1)}, f32[104,128]{1,0:T(8,128)S(1)}, u32[]{:S(2)}, u32[]{:S(2)}) collective-permute-start(f32[104,128]{1,0:T(8,128)S(1)} %get-tuple-element.39), channel_id=1, source_target_pairs={{0,30},{1,31},{2,4},{3,29},{4,2},{5,27},{6,8},{7,25},{8,6},{9,23},... | collective-permute-start | bytes 159752 | tf_op jit(solution)/shard_map/ppermute | solution.py:481
  7.7 1.5 %collective-permute-start.3 = (f32[88,128]{1,0:T(8,128)S(1)}, f32[88,128]{1,0:T(8,128)S(1)}, u32[]{:S(2)}, u32[]{:S(2)}) collective-permute-start(f32[88,128]{1,0:T(8,128)S(1)} %get-tuple-element.50), channel_id=1, source_target_pairs={{0,1},{1,0},{2,3},{3,2},{4,5},{5,4},{6,7},{7,6},{8,9},{9,8},{10,11... | collective-permute-start | bytes 135176 | tf_op jit(solution)/shard_map/ppermute | solution.py:509
  9.2 0.4 %collective-permute-start.4 = (f32[40,128]{1,0:T(8,128)S(1)}, f32[40,128]{1,0:T(8,128)S(1)}, u32[]{:S(2)}, u32[]{:S(2)}) collective-permute-start(f32[40,128]{1,0:T(8,128)S(1)} %get-tuple-element.51.own_column), channel_id=1, source_target_pairs={{0,2},{1,3},{2,0},{3,1},{4,6},{5,29},{6,4},{7,11},{8,10},{9,25},{1... | collective-permute-start | bytes 61448 | tf_op jit(solution)/shard_map/ppermute | solution.py:481
  9.6 0.1 collective-permute-start.1
  9.7 0.4 %collective-permute-start.2 = (f32[32,128]{1,0:T(8,128)S(1)}, f32[32,128]{1,0:T(8,128)S(1)}, u32[]{:S(2)}, u32[]{:S(2)}) collective-permute-start(f32[32,128]{1,0:T(8,128)S(1)} %get-tuple-element.45), channel_id=1, source_target_pairs={{0,2},{2,0},{4,6},{6,4},{8,10},{10,8},{12,14},{14,12},{16,18},{18,... | collective-permute-start | bytes 49160 | tf_op jit(solution)/shard_map/ppermute | solution.py:518
  10.1 0.0 collective-permute-done.far_ref.far_in
  10.1 0.1 relay.1.more_2_
  10.2 0.1 collective-permute-start.5
  10.3 0.4 %interior_north.1 = (f32[16,40,128]{2,1,0:T(8,128)S(1)}, f32[16,40,128]{2,1,0:T(8,128)S(1)}) custom-call(f32[16,40,128]{2,1,0:T(8,128)S(1)} %get-tuple-element.28.t_ref, f32[16,40,128]{2,1,0:T(8,128)S(1)} %get-tuple-element.29.s_ref, f32[16,40,128]{2,1,0:T(8,128)S(1)} %get-tuple-element.30.c_ref, ...), custom_call_target="tpu_custom_call", output_to_operand_aliasing={{0}: (5, {}), {1}: (6, {})} | custom-call | flops 20000000 | bytes 1000000 | tf_op jit(solution)/shard_map/interior_north/pallas_call | solution.py:541
  10.7 0.1 collective-permute-done.1.near_in
  10.8 0.2 %collective-permute-done.2.core_in = f32[32,128]{1,0:T(8,128)S(1)} collective-permute-done((f32[32,128]{1,0:T(8,128)S(1)}, f32[32,128]{1,0:T(8,128)S(1)}, u32[]{:S(2)}, u32[]{:S(2)}) %collective-permute-start.2) | collective-permute-done | bytes 16416 | tf_op jit(solution)/shard_map/ppermute | solution.py:518
  11.0 0.5 %longitude_edges.1 = (f32[16,40,128]{2,1,0:T(8,128)S(1)}, f32[16,40,128]{2,1,0:T(8,128)S(1)}, f32[2,16,24,128]{3,2,1,0:T(8,128)S(1)}) custom-call(f32[16,40,128]{2,1,0:T(8,128)S(1)} %get-tuple-element.41.pt_ref, f32[16,40,128]{2,1,0:T(8,128)S(1)} %get-tuple-element.42.ps_ref, ...), custom_call_target="tpu_custom_call", output_to_operand_aliasing={{0}: (0, {}), {1}: (1, {})} | custom-call | flops 5000000 | bytes 1000000 | tf_op jit(solution)/shard_map/longitude_edges/pallas_call | solution.py:553
  11.5 0.0 collective-permute-done.4.column_in
  11.5 0.2 %collective-permute-done.3.below_in.above_in = f32[88,128]{1,0:T(8,128)S(1)} collective-permute-done((f32[88,128]{1,0:T(8,128)S(1)}, f32[88,128]{1,0:T(8,128)S(1)}, u32[]{:S(2)}, u32[]{:S(2)}) %collective-permute-start.3) | collective-permute-done | bytes 45088 | tf_op jit(solution)/shard_map/ppermute | solution.py:509
  11.7 0.0 collective-permute-done.5.relay_in
  11.8 0.9 %latitude_edges.1 = (f32[16,32,128]{2,1,0:T(8,128)}, f32[16,32,128]{2,1,0:T(8,128)}, f32[2,16,24,128]{3,2,1,0:T(8,128)S(1)}) custom-call(f32[16,40,128]{2,1,0:T(8,128)S(1)} %get-tuple-element.46.t_new, f32[16,40,128]{2,1,0:T(8,128)S(1)} %get-tuple-element.47.s_new, f32[2,16,24,128]{3,2,1,0:T(8,128)S(1)} %get-tuple-element.48._, ...), custom_call_target="tpu_custom_call", output_to_operand_aliasing={{2}: (2, {})} | custom-call | tf_op jit(solution)/shard_map/latitude_edges/pallas_call | solution.py:564
  (1 shorter events, 0.0 us)
Async XLA Ops:
  3.4 6.7 %collective-permute-start = (f32[104,128]{1,0:T(8,128)S(1)}, f32[104,128]{1,0:T(8,128)S(1)}, u32[]{:S(2)}, u32[]{:S(2)}) collective-permute-start(f32[104,128]{1,0:T(8,128)S(1)} %get-tuple-element.39), channel_id=1, source_target_pairs={{0,30},{1,31},{2,4},{3,29},{4,2},{5,27},{6,8},{7,25},{8,6},{9,23},... | collective-permute-start | bytes 159752 | tf_op jit(solution)/shard_map/ppermute | solution.py:481
  7.7 4.0 %collective-permute-start.3 = (f32[88,128]{1,0:T(8,128)S(1)}, f32[88,128]{1,0:T(8,128)S(1)}, u32[]{:S(2)}, u32[]{:S(2)}) collective-permute-start(f32[88,128]{1,0:T(8,128)S(1)} %get-tuple-element.50), channel_id=1, source_target_pairs={{0,1},{1,0},{2,3},{3,2},{4,5},{5,4},{6,7},{7,6},{8,9},{9,8},{10,11... | collective-permute-start | bytes 135176 | tf_op jit(solution)/shard_map/ppermute | solution.py:509
  9.2 2.3 %collective-permute-start.4 = (f32[40,128]{1,0:T(8,128)S(1)}, f32[40,128]{1,0:T(8,128)S(1)}, u32[]{:S(2)}, u32[]{:S(2)}) collective-permute-start(f32[40,128]{1,0:T(8,128)S(1)} %get-tuple-element.51.own_column), channel_id=1, source_target_pairs={{0,2},{1,3},{2,0},{3,1},{4,6},{5,29},{6,4},{7,11},{8,10},{9,25},{1... | collective-permute-start | bytes 61448 | tf_op jit(solution)/shard_map/ppermute | solution.py:481
  9.6 1.2 %collective-permute-start.1 = (f32[32,128]{1,0:T(8,128)S(1)}, f32[32,128]{1,0:T(8,128)S(1)}, u32[]{:S(2)}, u32[]{:S(2)}) collective-permute-start(f32[32,128]{1,0:T(8,128)S(1)} %get-tuple-element.44), channel_id=1, source_target_pairs={{0,2},{1,8},{2,0},{3,5},{4,6},{5,3},{6,4},{7,9},{8,10},{9,7},{10,1... | collective-permute-start | bytes 49160 | tf_op jit(solution)/shard_map/ppermute | solution.py:481
  9.7 1.2 %collective-permute-start.2 = (f32[32,128]{1,0:T(8,128)S(1)}, f32[32,128]{1,0:T(8,128)S(1)}, u32[]{:S(2)}, u32[]{:S(2)}) collective-permute-start(f32[32,128]{1,0:T(8,128)S(1)} %get-tuple-element.45), channel_id=1, source_target_pairs={{0,2},{2,0},{4,6},{6,4},{8,10},{10,8},{12,14},{14,12},{16,18},{18,... | collective-permute-start | bytes 49160 | tf_op jit(solution)/shard_map/ppermute | solution.py:518
  10.2 1.5 %collective-permute-start.5 = (f32[24,128]{1,0:T(8,128)S(1)}, f32[24,128]{1,0:T(8,128)S(1)}, u32[]{:S(2)}, u32[]{:S(2)}) collective-permute-start(f32[24,128]{1,0:T(8,128)S(1)} %relay.1.more_2_), channel_id=1, source_target_pairs={{0,2},{2,0},{4,6},{6,4},{8,10},{10,8},{12,14},{14,12},{16,18},{18,... | collective-permute-start | bytes 36872 | tf_op jit(solution)/shard_map/ppermute | solution.py:539

commit v9 on v7

--- a/solution.py
+++ b/solution.py
@@ -162,10 +162,12 @@
     sides.append(gather(c_ref))
     copies[3].wait()
     counts = n_ref[...].astype(F32)
-    moved = jnp.concatenate([roll(counts[j : j + 1], 4 * j + 2) for j in range(rows)], axis=0)
-    line = jnp.sum(
-        jnp.where(iota((rows, LANES), 1) // 4 == iota((rows, LANES), 0), moved, 0.0), axis=0, keepdims=True
-    )
+    line = jnp.zeros((8, LANES), F32)
+    for at in range(0, rows, 8):
+        moved = pltpu.roll(counts[at : at + 8], 4 * at + 2, 1, stride=4, stride_axis=0)
+        mine = iota((8, LANES), 1) // 4 == iota((8, LANES), 0) + at
+        line = jnp.where(mine, moved, line)
+    line = jnp.sum(line, axis=0, keepdims=True)
     heat, salt, speed = sides
     line = jnp.broadcast_to(line, (levels, LANES))
     for i, value in enumerate((heat, salt, speed)):

time: 12.8 us -> 12.7 us (level)
  no operation moved by 1% of the time
where the time goes in v9:
time: 12.7 us; the launch traced here: 12.6 us
  starting transfers between devices  6.81 us (54%)
  Pallas kernels  4.65 us (37%)
  between operations  0.68 us (5%)
  waiting for transfers between devices  0.45 us (4%)
    ppermute x3, starting transfers between devices, exchange(): return lax.ppermute(array, ('lon', 'lat'), pairs)  4.78 us
    pallas_call x1, Pallas kernels, body(): pl.pallas_call(f(pack_kernel, levels, rows, nlat), out_shape=tuple(shapes...  1.53 us
    ppermute x1, starting transfers between devices, body(): lax.ppermute(lat, 'lat', [(i, (i + 1) % nlat) for i in rung])  1.52 us
    pallas_call x1, Pallas kernels, body(): pl.pallas_call(f(south_kernel, levels, rows, middle, True), out_shape=sou...  1.23 us
    pallas_call x1, Pallas kernels, body(): pl.pallas_call(f(latitude_kernel, levels, rows, nlat, nlon), out_shape=(o...  0.87 us
    pallas_call x1, Pallas kernels, body(): pl.pallas_call(f(longitude_kernel, levels, rows, nlat, nlon), out_shape=(...  0.54 us
    pallas_call x1, Pallas kernels, body(): pl.pallas_call(f(interior_kernel, levels, rows, middle, rows), out_shape=...  0.41 us
    ppermute x1, starting transfers between devices, body(): core_in = lax.ppermute(core, 'lon', [(i, i ^ 1) for i in ring])  0.4 us
  transfers between devices with their start and end apart: 6, of which 3 were waited for; matrix products, arithmetic and copies ran while one was open for 0% of the time, Pallas kernels for 8%

profile of v9, /device:TPU:0, one launch (start us, length us, event | category | flops | bytes accessed | tf_op | source)
XLA Modules:
  0.0 12.6 jit_solution(16067811138957918437)
XLA Ops:
  0.6 1.5 %pack.1 = (f32[16,40,128]{2,1,0:T(8,128)S(1)}, f32[16,40,128]{2,1,0:T(8,128)S(1)}, f32[16,40,128]{2,1,0:T(8,128)S(1)}, f32[16,40,128]{2,1,0:T(8,128)S(1)}, s32[3...) custom-call(f32[16,32,128]{2,1,0:T(8,128)} %t_hbm.1, ...), custom_call_target="tpu_custom_call" | custom-call | tf_op jit(solution)/shard_map/pack/pallas_call | solution.py:456
  2.2 1.2 %south_at_origin.1 = (f32[16,40,128]{2,1,0:T(8,128)S(1)}, f32[16,40,128]{2,1,0:T(8,128)S(1)}, f32[19,16,128]{2,1,0:T(8,128)S(1)}, f32[104,128]{1,0:T(8,128)S(1)}) custom-call(f32[16,40,128]{2,1,0:T(8,128)S(1)} %get-tuple-element.25.t_ref, f32[16,40,128]{2,1,0:T(8,128)S(1)} %get-tuple-element.26.s_ref, ...), custom_call_target="tpu_custom_call", output_to_operand_aliasing={{3}: (5, {})} | custom-call | flops 20000000 | bytes 1000000 | tf_op jit(solution)/shard_map/south_at_origin/pallas_call | solution.py:494
  3.4 4.3 %collective-permute-start = (f32[104,128]{1,0:T(8,128)S(1)}, f32[104,128]{1,0:T(8,128)S(1)}, u32[]{:S(2)}, u32[]{:S(2)}) collective-permute-start(f32[104,128]{1,0:T(8,128)S(1)} %get-tuple-element.36), channel_id=1, source_target_pairs={{0,30},{1,31},{2,4},{3,29},{4,2},{5,27},{6,8},{7,25},{8,6},{9,23},... | collective-permute-start | bytes 159752 | tf_op jit(solution)/shard_map/ppermute | solution.py:479
  7.7 1.5 %collective-permute-start.3 = (f32[88,128]{1,0:T(8,128)S(1)}, f32[88,128]{1,0:T(8,128)S(1)}, u32[]{:S(2)}, u32[]{:S(2)}) collective-permute-start(f32[88,128]{1,0:T(8,128)S(1)} %get-tuple-element.46), channel_id=1, source_target_pairs={{0,1},{1,0},{2,3},{3,2},{4,5},{5,4},{6,7},{7,6},{8,9},{9,8},{10,11... | collective-permute-start | bytes 135176 | tf_op jit(solution)/shard_map/ppermute | solution.py:507
  9.2 0.4 %collective-permute-start.4 = (f32[40,128]{1,0:T(8,128)S(1)}, f32[40,128]{1,0:T(8,128)S(1)}, u32[]{:S(2)}, u32[]{:S(2)}) collective-permute-start(f32[40,128]{1,0:T(8,128)S(1)} %get-tuple-element.47.own_column), channel_id=1, source_target_pairs={{0,2},{1,3},{2,0},{3,1},{4,6},{5,29},{6,4},{7,11},{8,10},{9,25},{1... | collective-permute-start | bytes 61448 | tf_op jit(solution)/shard_map/ppermute | solution.py:479
  9.6 0.1 collective-permute-start.1
  9.7 0.4 %collective-permute-start.2 = (f32[32,128]{1,0:T(8,128)S(1)}, f32[32,128]{1,0:T(8,128)S(1)}, u32[]{:S(2)}, u32[]{:S(2)}) collective-permute-start(f32[32,128]{1,0:T(8,128)S(1)} %get-tuple-element.42), channel_id=1, source_target_pairs={{0,2},{2,0},{4,6},{6,4},{8,10},{10,8},{12,14},{14,12},{16,18},{18,... | collective-permute-start | bytes 49160 | tf_op jit(solution)/shard_map/ppermute | solution.py:516
  10.1 0.0 collective-permute-done.far_ref.far_in
  10.1 0.1 relay.1.more_2_
  10.2 0.1 collective-permute-start.5
  10.3 0.4 %interior_north.1 = (f32[16,40,128]{2,1,0:T(8,128)S(1)}, f32[16,40,128]{2,1,0:T(8,128)S(1)}) custom-call(f32[16,40,128]{2,1,0:T(8,128)S(1)} %get-tuple-element.25.t_ref, f32[16,40,128]{2,1,0:T(8,128)S(1)} %get-tuple-element.26.s_ref, f32[16,40,128]{2,1,0:T(8,128)S(1)} %get-tuple-element.27.c_ref, ...), custom_call_target="tpu_custom_call", output_to_operand_aliasing={{0}: (5, {}), {1}: (6, {})} | custom-call | flops 20000000 | bytes 1000000 | tf_op jit(solution)/shard_map/interior_north/pallas_call | solution.py:539
  10.7 0.1 collective-permute-done.1.near_in
  10.8 0.2 %collective-permute-done.2.core_in = f32[32,128]{1,0:T(8,128)S(1)} collective-permute-done((f32[32,128]{1,0:T(8,128)S(1)}, f32[32,128]{1,0:T(8,128)S(1)}, u32[]{:S(2)}, u32[]{:S(2)}) %collective-permute-start.2) | collective-permute-done | bytes 16416 | tf_op jit(solution)/shard_map/ppermute | solution.py:516
  10.9 0.5 %longitude_edges.1 = (f32[16,40,128]{2,1,0:T(8,128)S(1)}, f32[16,40,128]{2,1,0:T(8,128)S(1)}) custom-call(f32[16,40,128]{2,1,0:T(8,128)S(1)} %get-tuple-element.38.pt_ref, f32[16,40,128]{2,1,0:T(8,128)S(1)} %get-tuple-element.39.ps_ref, f32[56,128]{1,0:T(8,128)S(1)} %get-tuple-element.40.side_ref, ...), custom_call_target="tpu_custom_call", output_to_operand_aliasing={{0}: (0, {}), {1}: (1, {})} | custom-call | flops 5000000 | bytes 1000000 | tf_op jit(solution)/shard_map/longitude_edges/pallas_call | solution.py:550
  11.5 0.0 collective-permute-done.4.column_in
  11.5 0.2 %collective-permute-done.3.below_in.above_in = f32[88,128]{1,0:T(8,128)S(1)} collective-permute-done((f32[88,128]{1,0:T(8,128)S(1)}, f32[88,128]{1,0:T(8,128)S(1)}, u32[]{:S(2)}, u32[]{:S(2)}) %collective-permute-start.3) | collective-permute-done | bytes 45088 | tf_op jit(solution)/shard_map/ppermute | solution.py:507
  11.7 0.0 collective-permute-done.5.relay_in
  11.7 0.9 %latitude_edges.1 = (f32[16,32,128]{2,1,0:T(8,128)}, f32[16,32,128]{2,1,0:T(8,128)}) custom-call(f32[16,40,128]{2,1,0:T(8,128)S(1)} %get-tuple-element.43.t_new, f32[16,40,128]{2,1,0:T(8,128)S(1)} %get-tuple-element.44.s_new, f32[16,40,128]{2,1,0:T(8,128)S(1)} %get-tuple-element.25.t_ref, f32[16,40,128]{2,1,0:T(8,128)S(1)} %get-tuple-element.26.s_ref, ...), custom_call_target="tpu_custom_call" | custom-call | tf_op jit(solution)/shard_map/latitude_edges/pallas_call | solution.py:561
  (1 shorter events, 0.0 us)
Async XLA Ops:
  3.4 6.7 %collective-permute-start = (f32[104,128]{1,0:T(8,128)S(1)}, f32[104,128]{1,0:T(8,128)S(1)}, u32[]{:S(2)}, u32[]{:S(2)}) collective-permute-start(f32[104,128]{1,0:T(8,128)S(1)} %get-tuple-element.36), channel_id=1, source_target_pairs={{0,30},{1,31},{2,4},{3,29},{4,2},{5,27},{6,8},{7,25},{8,6},{9,23},... | collective-permute-start | bytes 159752 | tf_op jit(solution)/shard_map/ppermute | solution.py:479
  7.7 4.0 %collective-permute-start.3 = (f32[88,128]{1,0:T(8,128)S(1)}, f32[88,128]{1,0:T(8,128)S(1)}, u32[]{:S(2)}, u32[]{:S(2)}) collective-permute-start(f32[88,128]{1,0:T(8,128)S(1)} %get-tuple-element.46), channel_id=1, source_target_pairs={{0,1},{1,0},{2,3},{3,2},{4,5},{5,4},{6,7},{7,6},{8,9},{9,8},{10,11... | collective-permute-start | bytes 135176 | tf_op jit(solution)/shard_map/ppermute | solution.py:507
  9.2 2.3 %collective-permute-start.4 = (f32[40,128]{1,0:T(8,128)S(1)}, f32[40,128]{1,0:T(8,128)S(1)}, u32[]{:S(2)}, u32[]{:S(2)}) collective-permute-start(f32[40,128]{1,0:T(8,128)S(1)} %get-tuple-element.47.own_column), channel_id=1, source_target_pairs={{0,2},{1,3},{2,0},{3,1},{4,6},{5,29},{6,4},{7,11},{8,10},{9,25},{1... | collective-permute-start | bytes 61448 | tf_op jit(solution)/shard_map/ppermute | solution.py:479
  9.6 1.2 %collective-permute-start.1 = (f32[32,128]{1,0:T(8,128)S(1)}, f32[32,128]{1,0:T(8,128)S(1)}, u32[]{:S(2)}, u32[]{:S(2)}) collective-permute-start(f32[32,128]{1,0:T(8,128)S(1)} %get-tuple-element.41), channel_id=1, source_target_pairs={{0,2},{1,8},{2,0},{3,5},{4,6},{5,3},{6,4},{7,9},{8,10},{9,7},{10,1... | collective-permute-start | bytes 49160 | tf_op jit(solution)/shard_map/ppermute | solution.py:479
  9.7 1.2 %collective-permute-start.2 = (f32[32,128]{1,0:T(8,128)S(1)}, f32[32,128]{1,0:T(8,128)S(1)}, u32[]{:S(2)}, u32[]{:S(2)}) collective-permute-start(f32[32,128]{1,0:T(8,128)S(1)} %get-tuple-element.42), channel_id=1, source_target_pairs={{0,2},{2,0},{4,6},{6,4},{8,10},{10,8},{12,14},{14,12},{16,18},{18,... | collective-permute-start | bytes 49160 | tf_op jit(solution)/shard_map/ppermute | solution.py:516
  10.2 1.5 %collective-permute-start.5 = (f32[24,128]{1,0:T(8,128)S(1)}, f32[24,128]{1,0:T(8,128)S(1)}, u32[]{:S(2)}, u32[]{:S(2)}) collective-permute-start(f32[24,128]{1,0:T(8,128)S(1)} %relay.1.more_2_), channel_id=1, source_target_pairs={{0,2},{2,0},{4,6},{6,4},{8,10},{10,8},{12,14},{14,12},{16,18},{18,... | collective-permute-start | bytes 36872 | tf_op jit(solution)/shard_map/ppermute | solution.py:537

commit v10 on v9

--- a/solution.py
+++ b/solution.py
@@ -116,7 +116,7 @@
 ):
     *more, sems = more
     K = levels
-    pairs = ((t_hbm, t_ref), (s_hbm, s_ref), (c_hbm, c_ref), (n_hbm, n_ref), (m_hbm, m_ref))
+    pairs = ((t_hbm, t_ref), (s_hbm, s_ref), (n_hbm, n_ref), (c_hbm, c_ref), (m_hbm, m_ref))
     pairs = [(src, dst if dst is n_ref else dst.at[:, :rows]) for src, dst in pairs]
     copies = [pltpu.make_async_copy(src, dst, sems.at[i]) for i, (src, dst) in enumerate(pairs)]
     for copy in copies:
@@ -158,9 +158,9 @@
                 at = (2 * tracer + i) * K
                 lat_ref[at : at + K, :] = jnp.where(is_top, strided(ref, south[i]), strided(ref, north[i]))
 
+    copies[3].wait()
+    sides.append(gather(c_ref))
     copies[2].wait()
-    sides.append(gather(c_ref))
-    copies[3].wait()
     counts = n_ref[...].astype(F32)
     line = jnp.zeros((8, LANES), F32)
     for at in range(0, rows, 8):

time: 12.7 us -> 12.7 us (level)
  no operation moved by 1% of the time
where the time goes in v10:
time: 12.7 us; the launch traced here: 12.6 us
  starting transfers between devices  6.81 us (54%)
  Pallas kernels  4.65 us (37%)
  between operations  0.68 us (5%)
  waiting for transfers between devices  0.45 us (4%)
    ppermute x3, starting transfers between devices, exchange(): return lax.ppermute(array, ('lon', 'lat'), pairs)  4.78 us
    pallas_call x1, Pallas kernels, body(): pl.pallas_call(f(pack_kernel, levels, rows, nlat), out_shape=tuple(shapes...  1.53 us
    ppermute x1, starting transfers between devices, body(): lax.ppermute(lat, 'lat', [(i, (i + 1) % nlat) for i in rung])  1.52 us
    pallas_call x1, Pallas kernels, body(): pl.pallas_call(f(south_kernel, levels, rows, middle, True), out_shape=sou...  1.23 us
    pallas_call x1, Pallas kernels, body(): pl.pallas_call(f(latitude_kernel, levels, rows, nlat, nlon), out_shape=(o...  0.87 us
    pallas_call x1, Pallas kernels, body(): pl.pallas_call(f(longitude_kernel, levels, rows, nlat, nlon), out_shape=(...  0.54 us
    pallas_call x1, Pallas kernels, body(): pl.pallas_call(f(interior_kernel, levels, rows, middle, rows), out_shape=...  0.41 us
    ppermute x1, starting transfers between devices, body(): core_in = lax.ppermute(core, 'lon', [(i, i ^ 1) for i in ring])  0.4 us
  transfers between devices with their start and end apart: 6, of which 3 were waited for; matrix products, arithmetic and copies ran while one was open for 0% of the time, Pallas kernels for 8%

profile of v10, /device:TPU:0, one launch (start us, length us, event | category | flops | bytes accessed | tf_op | source)
XLA Modules:
  0.0 12.6 jit_solution(5420610174154496914)
XLA Ops:
  0.6 1.5 %pack.1 = (f32[16,40,128]{2,1,0:T(8,128)S(1)}, f32[16,40,128]{2,1,0:T(8,128)S(1)}, f32[16,40,128]{2,1,0:T(8,128)S(1)}, f32[16,40,128]{2,1,0:T(8,128)S(1)}, s32[3...) custom-call(f32[16,32,128]{2,1,0:T(8,128)} %t_hbm.1, ...), custom_call_target="tpu_custom_call" | custom-call | tf_op jit(solution)/shard_map/pack/pallas_call | solution.py:456
  2.2 1.2 %south_at_origin.1 = (f32[16,40,128]{2,1,0:T(8,128)S(1)}, f32[16,40,128]{2,1,0:T(8,128)S(1)}, f32[19,16,128]{2,1,0:T(8,128)S(1)}, f32[104,128]{1,0:T(8,128)S(1)}) custom-call(f32[16,40,128]{2,1,0:T(8,128)S(1)} %get-tuple-element.25.t_ref, f32[16,40,128]{2,1,0:T(8,128)S(1)} %get-tuple-element.26.s_ref, ...), custom_call_target="tpu_custom_call", output_to_operand_aliasing={{3}: (5, {})} | custom-call | flops 20000000 | bytes 1000000 | tf_op jit(solution)/shard_map/south_at_origin/pallas_call | solution.py:494
  3.4 4.3 %collective-permute-start = (f32[104,128]{1,0:T(8,128)S(1)}, f32[104,128]{1,0:T(8,128)S(1)}, u32[]{:S(2)}, u32[]{:S(2)}) collective-permute-start(f32[104,128]{1,0:T(8,128)S(1)} %get-tuple-element.36), channel_id=1, source_target_pairs={{0,30},{1,31},{2,4},{3,29},{4,2},{5,27},{6,8},{7,25},{8,6},{9,23},... | collective-permute-start | bytes 159752 | tf_op jit(solution)/shard_map/ppermute | solution.py:479
  7.7 1.5 %collective-permute-start.3 = (f32[88,128]{1,0:T(8,128)S(1)}, f32[88,128]{1,0:T(8,128)S(1)}, u32[]{:S(2)}, u32[]{:S(2)}) collective-permute-start(f32[88,128]{1,0:T(8,128)S(1)} %get-tuple-element.46), channel_id=1, source_target_pairs={{0,1},{1,0},{2,3},{3,2},{4,5},{5,4},{6,7},{7,6},{8,9},{9,8},{10,11... | collective-permute-start | bytes 135176 | tf_op jit(solution)/shard_map/ppermute | solution.py:507
  9.2 0.4 %collective-permute-start.4 = (f32[40,128]{1,0:T(8,128)S(1)}, f32[40,128]{1,0:T(8,128)S(1)}, u32[]{:S(2)}, u32[]{:S(2)}) collective-permute-start(f32[40,128]{1,0:T(8,128)S(1)} %get-tuple-element.47.own_column), channel_id=1, source_target_pairs={{0,2},{1,3},{2,0},{3,1},{4,6},{5,29},{6,4},{7,11},{8,10},{9,25},{1... | collective-permute-start | bytes 61448 | tf_op jit(solution)/shard_map/ppermute | solution.py:479
  9.6 0.1 collective-permute-start.1
  9.7 0.4 %collective-permute-start.2 = (f32[32,128]{1,0:T(8,128)S(1)}, f32[32,128]{1,0:T(8,128)S(1)}, u32[]{:S(2)}, u32[]{:S(2)}) collective-permute-start(f32[32,128]{1,0:T(8,128)S(1)} %get-tuple-element.42), channel_id=1, source_target_pairs={{0,2},{2,0},{4,6},{6,4},{8,10},{10,8},{12,14},{14,12},{16,18},{18,... | collective-permute-start | bytes 49160 | tf_op jit(solution)/shard_map/ppermute | solution.py:516
  10.1 0.0 collective-permute-done.far_ref.far_in
  10.1 0.1 relay.1.more_2_
  10.2 0.1 collective-permute-start.5
  10.3 0.4 %interior_north.1 = (f32[16,40,128]{2,1,0:T(8,128)S(1)}, f32[16,40,128]{2,1,0:T(8,128)S(1)}) custom-call(f32[16,40,128]{2,1,0:T(8,128)S(1)} %get-tuple-element.25.t_ref, f32[16,40,128]{2,1,0:T(8,128)S(1)} %get-tuple-element.26.s_ref, f32[16,40,128]{2,1,0:T(8,128)S(1)} %get-tuple-element.27.c_ref, ...), custom_call_target="tpu_custom_call", output_to_operand_aliasing={{0}: (5, {}), {1}: (6, {})} | custom-call | flops 20000000 | bytes 1000000 | tf_op jit(solution)/shard_map/interior_north/pallas_call | solution.py:539
  10.7 0.1 collective-permute-done.1.near_in
  10.8 0.2 %collective-permute-done.2.core_in = f32[32,128]{1,0:T(8,128)S(1)} collective-permute-done((f32[32,128]{1,0:T(8,128)S(1)}, f32[32,128]{1,0:T(8,128)S(1)}, u32[]{:S(2)}, u32[]{:S(2)}) %collective-permute-start.2) | collective-permute-done | bytes 16416 | tf_op jit(solution)/shard_map/ppermute | solution.py:516
  10.9 0.5 %longitude_edges.1 = (f32[16,40,128]{2,1,0:T(8,128)S(1)}, f32[16,40,128]{2,1,0:T(8,128)S(1)}) custom-call(f32[16,40,128]{2,1,0:T(8,128)S(1)} %get-tuple-element.38.pt_ref, f32[16,40,128]{2,1,0:T(8,128)S(1)} %get-tuple-element.39.ps_ref, f32[56,128]{1,0:T(8,128)S(1)} %get-tuple-element.40.side_ref, ...), custom_call_target="tpu_custom_call", output_to_operand_aliasing={{0}: (0, {}), {1}: (1, {})} | custom-call | flops 5000000 | bytes 1000000 | tf_op jit(solution)/shard_map/longitude_edges/pallas_call | solution.py:550
  11.5 0.0 collective-permute-done.4.column_in
  11.5 0.2 %collective-permute-done.3.below_in.above_in = f32[88,128]{1,0:T(8,128)S(1)} collective-permute-done((f32[88,128]{1,0:T(8,128)S(1)}, f32[88,128]{1,0:T(8,128)S(1)}, u32[]{:S(2)}, u32[]{:S(2)}) %collective-permute-start.3) | collective-permute-done | bytes 45088 | tf_op jit(solution)/shard_map/ppermute | solution.py:507
  11.7 0.0 collective-permute-done.5.relay_in
  11.7 0.9 %latitude_edges.1 = (f32[16,32,128]{2,1,0:T(8,128)}, f32[16,32,128]{2,1,0:T(8,128)}) custom-call(f32[16,40,128]{2,1,0:T(8,128)S(1)} %get-tuple-element.43.t_new, f32[16,40,128]{2,1,0:T(8,128)S(1)} %get-tuple-element.44.s_new, f32[16,40,128]{2,1,0:T(8,128)S(1)} %get-tuple-element.25.t_ref, f32[16,40,128]{2,1,0:T(8,128)S(1)} %get-tuple-element.26.s_ref, ...), custom_call_target="tpu_custom_call" | custom-call | tf_op jit(solution)/shard_map/latitude_edges/pallas_call | solution.py:561
  (1 shorter events, 0.0 us)
Async XLA Ops:
  3.4 6.7 %collective-permute-start = (f32[104,128]{1,0:T(8,128)S(1)}, f32[104,128]{1,0:T(8,128)S(1)}, u32[]{:S(2)}, u32[]{:S(2)}) collective-permute-start(f32[104,128]{1,0:T(8,128)S(1)} %get-tuple-element.36), channel_id=1, source_target_pairs={{0,30},{1,31},{2,4},{3,29},{4,2},{5,27},{6,8},{7,25},{8,6},{9,23},... | collective-permute-start | bytes 159752 | tf_op jit(solution)/shard_map/ppermute | solution.py:479
  7.7 4.0 %collective-permute-start.3 = (f32[88,128]{1,0:T(8,128)S(1)}, f32[88,128]{1,0:T(8,128)S(1)}, u32[]{:S(2)}, u32[]{:S(2)}) collective-permute-start(f32[88,128]{1,0:T(8,128)S(1)} %get-tuple-element.46), channel_id=1, source_target_pairs={{0,1},{1,0},{2,3},{3,2},{4,5},{5,4},{6,7},{7,6},{8,9},{9,8},{10,11... | collective-permute-start | bytes 135176 | tf_op jit(solution)/shard_map/ppermute | solution.py:507
  9.2 2.3 %collective-permute-start.4 = (f32[40,128]{1,0:T(8,128)S(1)}, f32[40,128]{1,0:T(8,128)S(1)}, u32[]{:S(2)}, u32[]{:S(2)}) collective-permute-start(f32[40,128]{1,0:T(8,128)S(1)} %get-tuple-element.47.own_column), channel_id=1, source_target_pairs={{0,2},{1,3},{2,0},{3,1},{4,6},{5,29},{6,4},{7,11},{8,10},{9,25},{1... | collective-permute-start | bytes 61448 | tf_op jit(solution)/shard_map/ppermute | solution.py:479
  9.6 1.2 %collective-permute-start.1 = (f32[32,128]{1,0:T(8,128)S(1)}, f32[32,128]{1,0:T(8,128)S(1)}, u32[]{:S(2)}, u32[]{:S(2)}) collective-permute-start(f32[32,128]{1,0:T(8,128)S(1)} %get-tuple-element.41), channel_id=1, source_target_pairs={{0,2},{1,8},{2,0},{3,5},{4,6},{5,3},{6,4},{7,9},{8,10},{9,7},{10,1... | collective-permute-start | bytes 49160 | tf_op jit(solution)/shard_map/ppermute | solution.py:479
  9.7 1.2 %collective-permute-start.2 = (f32[32,128]{1,0:T(8,128)S(1)}, f32[32,128]{1,0:T(8,128)S(1)}, u32[]{:S(2)}, u32[]{:S(2)}) collective-permute-start(f32[32,128]{1,0:T(8,128)S(1)} %get-tuple-element.42), channel_id=1, source_target_pairs={{0,2},{2,0},{4,6},{6,4},{8,10},{10,8},{12,14},{14,12},{16,18},{18,... | collective-permute-start | bytes 49160 | tf_op jit(solution)/shard_map/ppermute | solution.py:516
  10.2 1.5 %collective-permute-start.5 = (f32[24,128]{1,0:T(8,128)S(1)}, f32[24,128]{1,0:T(8,128)S(1)}, u32[]{:S(2)}, u32[]{:S(2)}) collective-permute-start(f32[24,128]{1,0:T(8,128)S(1)} %relay.1.more_2_), channel_id=1, source_target_pairs={{0,2},{2,0},{4,6},{6,4},{8,10},{10,8},{12,14},{14,12},{16,18},{18,... | collective-permute-start | bytes 36872 | tf_op jit(solution)/shard_map/ppermute | solution.py:537

commit v11 on v10

--- a/solution.py
+++ b/solution.py
@@ -21,7 +21,7 @@
 LANES = 128
 VMEM = 8 * 1024 * 1024
 UNROLL = 8
-HEAD = 24
+HEAD = 16
 SPARE = 8
 F32 = jnp.float32
 

time: 12.7 us -> 12.8 us (level)
  waiting for transfers between devices: 0.45 us -> 0.02 us
  starting transfers between devices: 6.81 us -> 7.21 us
    pallas_call x1, Pallas kernels: 0.41 us -> 0.82 us  [body(): pl.pallas_call(f(interior_kernel, levels, rows, middle, rows), out_shape=...]
    ppermute x3, starting transfers between devices: 4.78 us -> 5.18 us  [exchange(): return lax.ppermute(array, ('lon', 'lat'), pairs)]
    pallas_call x1, Pallas kernels: 1.23 us -> 0.83 us  [body(): pl.pallas_call(f(south_kernel, levels, rows, middle, True), out_shape=sou...]
    ppermute x1, waiting for transfers between devices: 0.22 us -> 0.01 us  [body(): lax.ppermute(lat, 'lat', [(i, (i + 1) % nlat) for i in rung])]
    ppermute x1, waiting for transfers between devices: 0.17 us -> 0.01 us  [body(): core_in = lax.ppermute(core, 'lon', [(i, i ^ 1) for i in ring])]
  transfers between devices with their start and end apart: 6 -> 6, of which waited for: 3 -> 0; matrix products, arithmetic and copies ran while one was open for 0% -> 0% of each run, Pallas kernels for 8% -> 11%
where the time goes in v11:
time: 12.8 us; the launch traced here: 12.6 us
  starting transfers between devices  7.21 us (56%)
  Pallas kernels  4.68 us (37%)
  between operations  0.71 us (6%)
    ppermute x3, starting transfers between devices, exchange(): return lax.ppermute(array, ('lon', 'lat'), pairs)  5.18 us
    pallas_call x1, Pallas kernels, body(): pl.pallas_call(f(pack_kernel, levels, rows, nlat), out_shape=tuple(shapes...  1.53 us
    ppermute x1, starting transfers between devices, body(): lax.ppermute(lat, 'lat', [(i, (i + 1) % nlat) for i in rung])  1.52 us
    pallas_call x1, Pallas kernels, body(): pl.pallas_call(f(latitude_kernel, levels, rows, nlat, nlon), out_shape=(o...  0.88 us
    pallas_call x1, Pallas kernels, body(): pl.pallas_call(f(south_kernel, levels, rows, middle, True), out_shape=sou...  0.83 us
    pallas_call x1, Pallas kernels, body(): pl.pallas_call(f(interior_kernel, levels, rows, middle, rows), out_shape=...  0.82 us
    pallas_call x1, Pallas kernels, body(): pl.pallas_call(f(longitude_kernel, levels, rows, nlat, nlon), out_shape=(...  0.55 us
    ppermute x1, starting transfers between devices, body(): core_in = lax.ppermute(core, 'lon', [(i, i ^ 1) for i in ring])  0.4 us
  transfers between devices with their start and end apart: 6, of which 0 were waited for; matrix products, arithmetic and copies ran while one was open for 0% of the time, Pallas kernels for 11%

profile of v11, /device:TPU:0, one launch (start us, length us, event | category | flops | bytes accessed | tf_op | source)
XLA Modules:
  0.0 12.6 jit_solution(6029482089558349055)
XLA Ops:
  0.6 1.5 %pack.1 = (f32[16,40,128]{2,1,0:T(8,128)S(1)}, f32[16,40,128]{2,1,0:T(8,128)S(1)}, f32[16,40,128]{2,1,0:T(8,128)S(1)}, f32[16,40,128]{2,1,0:T(8,128)S(1)}, s32[3...) custom-call(f32[16,32,128]{2,1,0:T(8,128)} %t_hbm.1, ...), custom_call_target="tpu_custom_call" | custom-call | tf_op jit(solution)/shard_map/pack/pallas_call | solution.py:456
  2.2 0.8 %south_at_origin.1 = (f32[16,40,128]{2,1,0:T(8,128)S(1)}, f32[16,40,128]{2,1,0:T(8,128)S(1)}, f32[19,16,128]{2,1,0:T(8,128)S(1)}, f32[104,128]{1,0:T(8,128)S(1)}) custom-call(f32[16,40,128]{2,1,0:T(8,128)S(1)} %get-tuple-element.25.t_ref, f32[16,40,128]{2,1,0:T(8,128)S(1)} %get-tuple-element.26.s_ref, ...), custom_call_target="tpu_custom_call", output_to_operand_aliasing={{3}: (5, {})} | custom-call | flops 20000000 | bytes 1000000 | tf_op jit(solution)/shard_map/south_at_origin/pallas_call | solution.py:494
  3.0 4.7 %collective-permute-start = (f32[104,128]{1,0:T(8,128)S(1)}, f32[104,128]{1,0:T(8,128)S(1)}, u32[]{:S(2)}, u32[]{:S(2)}) collective-permute-start(f32[104,128]{1,0:T(8,128)S(1)} %get-tuple-element.36), channel_id=1, source_target_pairs={{0,30},{1,31},{2,4},{3,29},{4,2},{5,27},{6,8},{7,25},{8,6},{9,23},... | collective-permute-start | bytes 159752 | tf_op jit(solution)/shard_map/ppermute | solution.py:479
  7.7 1.5 %collective-permute-start.3 = (f32[88,128]{1,0:T(8,128)S(1)}, f32[88,128]{1,0:T(8,128)S(1)}, u32[]{:S(2)}, u32[]{:S(2)}) collective-permute-start(f32[88,128]{1,0:T(8,128)S(1)} %get-tuple-element.46), channel_id=1, source_target_pairs={{0,1},{1,0},{2,3},{3,2},{4,5},{5,4},{6,7},{7,6},{8,9},{9,8},{10,11... | collective-permute-start | bytes 135176 | tf_op jit(solution)/shard_map/ppermute | solution.py:507
  9.2 0.4 %collective-permute-start.4 = (f32[40,128]{1,0:T(8,128)S(1)}, f32[40,128]{1,0:T(8,128)S(1)}, u32[]{:S(2)}, u32[]{:S(2)}) collective-permute-start(f32[40,128]{1,0:T(8,128)S(1)} %get-tuple-element.47.own_column), channel_id=1, source_target_pairs={{0,2},{1,3},{2,0},{3,1},{4,6},{5,29},{6,4},{7,11},{8,10},{9,25},{1... | collective-permute-start | bytes 61448 | tf_op jit(solution)/shard_map/ppermute | solution.py:479
  9.6 0.1 collective-permute-start.1
  9.7 0.4 %collective-permute-start.2 = (f32[32,128]{1,0:T(8,128)S(1)}, f32[32,128]{1,0:T(8,128)S(1)}, u32[]{:S(2)}, u32[]{:S(2)}) collective-permute-start(f32[32,128]{1,0:T(8,128)S(1)} %get-tuple-element.42), channel_id=1, source_target_pairs={{0,2},{2,0},{4,6},{6,4},{8,10},{10,8},{12,14},{14,12},{16,18},{18,... | collective-permute-start | bytes 49160 | tf_op jit(solution)/shard_map/ppermute | solution.py:516
  10.1 0.0 collective-permute-done.far_ref.far_in
  10.1 0.1 relay.1.more_2_
  10.2 0.1 collective-permute-start.5
  10.3 0.8 %interior_north.1 = (f32[16,40,128]{2,1,0:T(8,128)S(1)}, f32[16,40,128]{2,1,0:T(8,128)S(1)}) custom-call(f32[16,40,128]{2,1,0:T(8,128)S(1)} %get-tuple-element.25.t_ref, f32[16,40,128]{2,1,0:T(8,128)S(1)} %get-tuple-element.26.s_ref, f32[16,40,128]{2,1,0:T(8,128)S(1)} %get-tuple-element.27.c_ref, ...), custom_call_target="tpu_custom_call", output_to_operand_aliasing={{0}: (5, {}), {1}: (6, {})} | custom-call | flops 20000000 | bytes 1000000 | tf_op jit(solution)/shard_map/interior_north/pallas_call | solution.py:539
  11.1 0.0 collective-permute-done.1.near_in
  11.1 0.0 collective-permute-done.2.core_in
  11.1 0.6 %longitude_edges.1 = (f32[16,40,128]{2,1,0:T(8,128)S(1)}, f32[16,40,128]{2,1,0:T(8,128)S(1)}) custom-call(f32[16,40,128]{2,1,0:T(8,128)S(1)} %get-tuple-element.38.pt_ref, f32[16,40,128]{2,1,0:T(8,128)S(1)} %get-tuple-element.39.ps_ref, f32[56,128]{1,0:T(8,128)S(1)} %get-tuple-element.40.side_ref, ...), custom_call_target="tpu_custom_call", output_to_operand_aliasing={{0}: (0, {}), {1}: (1, {})} | custom-call | flops 5000000 | bytes 1000000 | tf_op jit(solution)/shard_map/longitude_edges/pallas_call | solution.py:550
  11.7 0.0 collective-permute-done.4.column_in
  11.7 0.0 collective-permute-done.3.below_in.above_in
  11.7 0.0 collective-permute-done.5.relay_in
  11.7 0.9 %latitude_edges.1 = (f32[16,32,128]{2,1,0:T(8,128)}, f32[16,32,128]{2,1,0:T(8,128)}) custom-call(f32[16,40,128]{2,1,0:T(8,128)S(1)} %get-tuple-element.43.t_new, f32[16,40,128]{2,1,0:T(8,128)S(1)} %get-tuple-element.44.s_new, f32[16,40,128]{2,1,0:T(8,128)S(1)} %get-tuple-element.25.t_ref, f32[16,40,128]{2,1,0:T(8,128)S(1)} %get-tuple-element.26.s_ref, ...), custom_call_target="tpu_custom_call" | custom-call | tf_op jit(solution)/shard_map/latitude_edges/pallas_call | solution.py:561
  (1 shorter events, 0.0 us)
Async XLA Ops:
  3.0 7.1 %collective-permute-start = (f32[104,128]{1,0:T(8,128)S(1)}, f32[104,128]{1,0:T(8,128)S(1)}, u32[]{:S(2)}, u32[]{:S(2)}) collective-permute-start(f32[104,128]{1,0:T(8,128)S(1)} %get-tuple-element.36), channel_id=1, source_target_pairs={{0,30},{1,31},{2,4},{3,29},{4,2},{5,27},{6,8},{7,25},{8,6},{9,23},... | collective-permute-start | bytes 159752 | tf_op jit(solution)/shard_map/ppermute | solution.py:479
  7.7 4.0 %collective-permute-start.3 = (f32[88,128]{1,0:T(8,128)S(1)}, f32[88,128]{1,0:T(8,128)S(1)}, u32[]{:S(2)}, u32[]{:S(2)}) collective-permute-start(f32[88,128]{1,0:T(8,128)S(1)} %get-tuple-element.46), channel_id=1, source_target_pairs={{0,1},{1,0},{2,3},{3,2},{4,5},{5,4},{6,7},{7,6},{8,9},{9,8},{10,11... | collective-permute-start | bytes 135176 | tf_op jit(solution)/shard_map/ppermute | solution.py:507
  9.2 2.5 %collective-permute-start.4 = (f32[40,128]{1,0:T(8,128)S(1)}, f32[40,128]{1,0:T(8,128)S(1)}, u32[]{:S(2)}, u32[]{:S(2)}) collective-permute-start(f32[40,128]{1,0:T(8,128)S(1)} %get-tuple-element.47.own_column), channel_id=1, source_target_pairs={{0,2},{1,3},{2,0},{3,1},{4,6},{5,29},{6,4},{7,11},{8,10},{9,25},{1... | collective-permute-start | bytes 61448 | tf_op jit(solution)/shard_map/ppermute | solution.py:479
  9.6 1.5 %collective-permute-start.1 = (f32[32,128]{1,0:T(8,128)S(1)}, f32[32,128]{1,0:T(8,128)S(1)}, u32[]{:S(2)}, u32[]{:S(2)}) collective-permute-start(f32[32,128]{1,0:T(8,128)S(1)} %get-tuple-element.41), channel_id=1, source_target_pairs={{0,2},{1,8},{2,0},{3,5},{4,6},{5,3},{6,4},{7,9},{8,10},{9,7},{10,1... | collective-permute-start | bytes 49160 | tf_op jit(solution)/shard_map/ppermute | solution.py:479
  9.7 1.4 %collective-permute-start.2 = (f32[32,128]{1,0:T(8,128)S(1)}, f32[32,128]{1,0:T(8,128)S(1)}, u32[]{:S(2)}, u32[]{:S(2)}) collective-permute-start(f32[32,128]{1,0:T(8,128)S(1)} %get-tuple-element.42), channel_id=1, source_target_pairs={{0,2},{2,0},{4,6},{6,4},{8,10},{10,8},{12,14},{14,12},{16,18},{18,... | collective-permute-start | bytes 49160 | tf_op jit(solution)/shard_map/ppermute | solution.py:516
  10.2 1.6 %collective-permute-start.5 = (f32[24,128]{1,0:T(8,128)S(1)}, f32[24,128]{1,0:T(8,128)S(1)}, u32[]{:S(2)}, u32[]{:S(2)}) collective-permute-start(f32[24,128]{1,0:T(8,128)S(1)} %relay.1.more_2_), channel_id=1, source_target_pairs={{0,2},{2,0},{4,6},{6,4},{8,10},{10,8},{12,14},{14,12},{16,18},{18,... | collective-permute-start | bytes 36872 | tf_op jit(solution)/shard_map/ppermute | solution.py:537

commit v12 on v10

--- a/solution.py
+++ b/solution.py
@@ -218,9 +218,10 @@
 STATE = 19
 
 
-def south_kernel(levels, rows, last, early, t_ref, s_ref, c_ref, m_ref, n_ref, *more):
+def south_kernel(levels, rows, last, early, lon_size, t_ref, s_ref, c_ref, m_ref, n_ref, *more):
     *more, pt_ref, ps_ref, state_out = more[:-1] if early else more
-    at_origin = (lax.axis_index("lat") == 0) & (lax.axis_index("lon") < 2)
+    lon_at = lax.axis_index("lon")
+    at_origin = (lax.axis_index("lat") == 0) & ((lon_at < 2) | (lon_at == lon_size // 4 + 1))
 
     @pl.when(at_origin if early else jnp.logical_not(at_origin))
     def _():
@@ -492,7 +493,7 @@
     south_out = (room, room, out(STATE, K, LANES))
     cost = pl.CostEstimate(flops=20_000_000, bytes_accessed=1_000_000, transcendentals=0)
     pt, ps, state, far = pl.pallas_call(
-        f(south_kernel, levels, rows, middle, True),
+        f(south_kernel, levels, rows, middle, True, nlon),
         out_shape=south_out + (out(*far.shape),),
         in_specs=[vmem] * 6,
         out_specs=(vmem,) * 4,
@@ -517,7 +518,7 @@
     column_in = exchange(column, columns.get, lambda i: i ^ 1)
 
     pt, ps, state = pl.pallas_call(
-        f(south_kernel, levels, rows, middle, False),
+        f(south_kernel, levels, rows, middle, False, nlon),
         out_shape=south_out,
         in_specs=[vmem] * 8,
         out_specs=(vmem,) * 3,

time: 12.7 us -> 12.7 us (level)
  no operation moved by 1% of the time
where the time goes in v12:
time: 12.7 us; the launch traced here: 12.6 us
  starting transfers between devices  6.81 us (54%)
  Pallas kernels  4.66 us (37%)
  between operations  0.68 us (5%)
  waiting for transfers between devices  0.45 us (4%)
    ppermute x3, starting transfers between devices, exchange(): return lax.ppermute(array, ('lon', 'lat'), pairs)  4.78 us
    pallas_call x1, Pallas kernels, body(): pl.pallas_call(f(pack_kernel, levels, rows, nlat), out_shape=tuple(shapes...  1.53 us
    ppermute x1, starting transfers between devices, body(): lax.ppermute(lat, 'lat', [(i, (i + 1) % nlat) for i in rung])  1.52 us
    pallas_call x1, Pallas kernels, body(): pl.pallas_call(f(south_kernel, levels, rows, middle, True, nlon), out_sha...  1.23 us
    pallas_call x1, Pallas kernels, body(): pl.pallas_call(f(latitude_kernel, levels, rows, nlat, nlon), out_shape=(o...  0.87 us
    pallas_call x1, Pallas kernels, body(): pl.pallas_call(f(longitude_kernel, levels, rows, nlat, nlon), out_shape=(...  0.54 us
    pallas_call x1, Pallas kernels, body(): pl.pallas_call(f(interior_kernel, levels, rows, middle, rows), out_shape=...  0.41 us
    ppermute x1, starting transfers between devices, body(): core_in = lax.ppermute(core, 'lon', [(i, i ^ 1) for i in ring])  0.4 us
  transfers between devices with their start and end apart: 6, of which 3 were waited for; matrix products, arithmetic and copies ran while one was open for 0% of the time, Pallas kernels for 8%

profile of v12, /device:TPU:0, one launch (start us, length us, event | category | flops | bytes accessed | tf_op | source)
XLA Modules:
  0.0 12.6 jit_solution(913136654292118613)
XLA Ops:
  0.6 1.5 %pack.1 = (f32[16,40,128]{2,1,0:T(8,128)S(1)}, f32[16,40,128]{2,1,0:T(8,128)S(1)}, f32[16,40,128]{2,1,0:T(8,128)S(1)}, f32[16,40,128]{2,1,0:T(8,128)S(1)}, s32[3...) custom-call(f32[16,32,128]{2,1,0:T(8,128)} %t_hbm.1, ...), custom_call_target="tpu_custom_call" | custom-call | tf_op jit(solution)/shard_map/pack/pallas_call | solution.py:457
  2.2 1.2 %south_at_origin.1 = (f32[16,40,128]{2,1,0:T(8,128)S(1)}, f32[16,40,128]{2,1,0:T(8,128)S(1)}, f32[19,16,128]{2,1,0:T(8,128)S(1)}, f32[104,128]{1,0:T(8,128)S(1)}) custom-call(f32[16,40,128]{2,1,0:T(8,128)S(1)} %get-tuple-element.25.t_ref, f32[16,40,128]{2,1,0:T(8,128)S(1)} %get-tuple-element.26.s_ref, ...), custom_call_target="tpu_custom_call", output_to_operand_aliasing={{3}: (5, {})} | custom-call | flops 20000000 | bytes 1000000 | tf_op jit(solution)/shard_map/south_at_origin/pallas_call | solution.py:495
  3.4 4.3 %collective-permute-start = (f32[104,128]{1,0:T(8,128)S(1)}, f32[104,128]{1,0:T(8,128)S(1)}, u32[]{:S(2)}, u32[]{:S(2)}) collective-permute-start(f32[104,128]{1,0:T(8,128)S(1)} %get-tuple-element.36), channel_id=1, source_target_pairs={{0,30},{1,31},{2,4},{3,29},{4,2},{5,27},{6,8},{7,25},{8,6},{9,23},... | collective-permute-start | bytes 159752 | tf_op jit(solution)/shard_map/ppermute | solution.py:480
  7.7 1.5 %collective-permute-start.3 = (f32[88,128]{1,0:T(8,128)S(1)}, f32[88,128]{1,0:T(8,128)S(1)}, u32[]{:S(2)}, u32[]{:S(2)}) collective-permute-start(f32[88,128]{1,0:T(8,128)S(1)} %get-tuple-element.46), channel_id=1, source_target_pairs={{0,1},{1,0},{2,3},{3,2},{4,5},{5,4},{6,7},{7,6},{8,9},{9,8},{10,11... | collective-permute-start | bytes 135176 | tf_op jit(solution)/shard_map/ppermute | solution.py:508
  9.2 0.4 %collective-permute-start.4 = (f32[40,128]{1,0:T(8,128)S(1)}, f32[40,128]{1,0:T(8,128)S(1)}, u32[]{:S(2)}, u32[]{:S(2)}) collective-permute-start(f32[40,128]{1,0:T(8,128)S(1)} %get-tuple-element.47.own_column), channel_id=1, source_target_pairs={{0,2},{1,3},{2,0},{3,1},{4,6},{5,29},{6,4},{7,11},{8,10},{9,25},{1... | collective-permute-start | bytes 61448 | tf_op jit(solution)/shard_map/ppermute | solution.py:480
  9.6 0.1 collective-permute-start.1
  9.7 0.4 %collective-permute-start.2 = (f32[32,128]{1,0:T(8,128)S(1)}, f32[32,128]{1,0:T(8,128)S(1)}, u32[]{:S(2)}, u32[]{:S(2)}) collective-permute-start(f32[32,128]{1,0:T(8,128)S(1)} %get-tuple-element.42), channel_id=1, source_target_pairs={{0,2},{2,0},{4,6},{6,4},{8,10},{10,8},{12,14},{14,12},{16,18},{18,... | collective-permute-start | bytes 49160 | tf_op jit(solution)/shard_map/ppermute | solution.py:517
  10.1 0.0 collective-permute-done.far_ref.far_in
  10.1 0.1 relay.1.more_2_
  10.2 0.1 collective-permute-start.5
  10.3 0.4 %interior_north.1 = (f32[16,40,128]{2,1,0:T(8,128)S(1)}, f32[16,40,128]{2,1,0:T(8,128)S(1)}) custom-call(f32[16,40,128]{2,1,0:T(8,128)S(1)} %get-tuple-element.25.t_ref, f32[16,40,128]{2,1,0:T(8,128)S(1)} %get-tuple-element.26.s_ref, f32[16,40,128]{2,1,0:T(8,128)S(1)} %get-tuple-element.27.c_ref, ...), custom_call_target="tpu_custom_call", output_to_operand_aliasing={{0}: (5, {}), {1}: (6, {})} | custom-call | flops 20000000 | bytes 1000000 | tf_op jit(solution)/shard_map/interior_north/pallas_call | solution.py:540
  10.7 0.1 collective-permute-done.1.near_in
  10.8 0.2 %collective-permute-done.2.core_in = f32[32,128]{1,0:T(8,128)S(1)} collective-permute-done((f32[32,128]{1,0:T(8,128)S(1)}, f32[32,128]{1,0:T(8,128)S(1)}, u32[]{:S(2)}, u32[]{:S(2)}) %collective-permute-start.2) | collective-permute-done | bytes 16416 | tf_op jit(solution)/shard_map/ppermute | solution.py:517
  10.9 0.5 %longitude_edges.1 = (f32[16,40,128]{2,1,0:T(8,128)S(1)}, f32[16,40,128]{2,1,0:T(8,128)S(1)}) custom-call(f32[16,40,128]{2,1,0:T(8,128)S(1)} %get-tuple-element.38.pt_ref, f32[16,40,128]{2,1,0:T(8,128)S(1)} %get-tuple-element.39.ps_ref, f32[56,128]{1,0:T(8,128)S(1)} %get-tuple-element.40.side_ref, ...), custom_call_target="tpu_custom_call", output_to_operand_aliasing={{0}: (0, {}), {1}: (1, {})} | custom-call | flops 5000000 | bytes 1000000 | tf_op jit(solution)/shard_map/longitude_edges/pallas_call | solution.py:551
  11.5 0.0 collective-permute-done.4.column_in
  11.5 0.2 %collective-permute-done.3.below_in.above_in = f32[88,128]{1,0:T(8,128)S(1)} collective-permute-done((f32[88,128]{1,0:T(8,128)S(1)}, f32[88,128]{1,0:T(8,128)S(1)}, u32[]{:S(2)}, u32[]{:S(2)}) %collective-permute-start.3) | collective-permute-done | bytes 45088 | tf_op jit(solution)/shard_map/ppermute | solution.py:508
  11.7 0.0 collective-permute-done.5.relay_in
  11.7 0.9 %latitude_edges.1 = (f32[16,32,128]{2,1,0:T(8,128)}, f32[16,32,128]{2,1,0:T(8,128)}) custom-call(f32[16,40,128]{2,1,0:T(8,128)S(1)} %get-tuple-element.43.t_new, f32[16,40,128]{2,1,0:T(8,128)S(1)} %get-tuple-element.44.s_new, f32[16,40,128]{2,1,0:T(8,128)S(1)} %get-tuple-element.25.t_ref, f32[16,40,128]{2,1,0:T(8,128)S(1)} %get-tuple-element.26.s_ref, ...), custom_call_target="tpu_custom_call" | custom-call | tf_op jit(solution)/shard_map/latitude_edges/pallas_call | solution.py:562
  (1 shorter events, 0.0 us)
Async XLA Ops:
  3.4 6.7 %collective-permute-start = (f32[104,128]{1,0:T(8,128)S(1)}, f32[104,128]{1,0:T(8,128)S(1)}, u32[]{:S(2)}, u32[]{:S(2)}) collective-permute-start(f32[104,128]{1,0:T(8,128)S(1)} %get-tuple-element.36), channel_id=1, source_target_pairs={{0,30},{1,31},{2,4},{3,29},{4,2},{5,27},{6,8},{7,25},{8,6},{9,23},... | collective-permute-start | bytes 159752 | tf_op jit(solution)/shard_map/ppermute | solution.py:480
  7.7 4.0 %collective-permute-start.3 = (f32[88,128]{1,0:T(8,128)S(1)}, f32[88,128]{1,0:T(8,128)S(1)}, u32[]{:S(2)}, u32[]{:S(2)}) collective-permute-start(f32[88,128]{1,0:T(8,128)S(1)} %get-tuple-element.46), channel_id=1, source_target_pairs={{0,1},{1,0},{2,3},{3,2},{4,5},{5,4},{6,7},{7,6},{8,9},{9,8},{10,11... | collective-permute-start | bytes 135176 | tf_op jit(solution)/shard_map/ppermute | solution.py:508
  9.2 2.3 %collective-permute-start.4 = (f32[40,128]{1,0:T(8,128)S(1)}, f32[40,128]{1,0:T(8,128)S(1)}, u32[]{:S(2)}, u32[]{:S(2)}) collective-permute-start(f32[40,128]{1,0:T(8,128)S(1)} %get-tuple-element.47.own_column), channel_id=1, source_target_pairs={{0,2},{1,3},{2,0},{3,1},{4,6},{5,29},{6,4},{7,11},{8,10},{9,25},{1... | collective-permute-start | bytes 61448 | tf_op jit(solution)/shard_map/ppermute | solution.py:480
  9.6 1.2 %collective-permute-start.1 = (f32[32,128]{1,0:T(8,128)S(1)}, f32[32,128]{1,0:T(8,128)S(1)}, u32[]{:S(2)}, u32[]{:S(2)}) collective-permute-start(f32[32,128]{1,0:T(8,128)S(1)} %get-tuple-element.41), channel_id=1, source_target_pairs={{0,2},{1,8},{2,0},{3,5},{4,6},{5,3},{6,4},{7,9},{8,10},{9,7},{10,1... | collective-permute-start | bytes 49160 | tf_op jit(solution)/shard_map/ppermute | solution.py:480
  9.7 1.2 %collective-permute-start.2 = (f32[32,128]{1,0:T(8,128)S(1)}, f32[32,128]{1,0:T(8,128)S(1)}, u32[]{:S(2)}, u32[]{:S(2)}) collective-permute-start(f32[32,128]{1,0:T(8,128)S(1)} %get-tuple-element.42), channel_id=1, source_target_pairs={{0,2},{2,0},{4,6},{6,4},{8,10},{10,8},{12,14},{14,12},{16,18},{18,... | collective-permute-start | bytes 49160 | tf_op jit(solution)/shard_map/ppermute | solution.py:517
  10.2 1.5 %collective-permute-start.5 = (f32[24,128]{1,0:T(8,128)S(1)}, f32[24,128]{1,0:T(8,128)S(1)}, u32[]{:S(2)}, u32[]{:S(2)}) collective-permute-start(f32[24,128]{1,0:T(8,128)S(1)} %relay.1.more_2_), channel_id=1, source_target_pairs={{0,2},{2,0},{4,6},{6,4},{8,10},{10,8},{12,14},{14,12},{16,18},{18,... | collective-permute-start | bytes 36872 | tf_op jit(solution)/shard_map/ppermute | solution.py:538
